TPU v7x, 32 devices: a whole 2x2x4 slice. The times are simulated.
32 devices in a mesh: dp: 8 (over z, x), grp: 4 (over y, core).
Axes of the slice: x: 2, y: 2, z: 4, core: 2. Of those that a mesh axis runs over, the one named last changes fastest.
Arguments:
- images: bfloat16 [16384, 128, 128], P(('dp', 'grp')), may hold values from -6 to 6
- shifts: int32 [16384, 2], P(('dp', 'grp')), may hold values from -16 to 16
- class_ids: int32 [16384], P(('dp', 'grp')), may hold values from 0 to 255
- next_block: bfloat16 [1024, 2, 4096], P('grp'), may hold values from -6 to 6
Outputs:
- averages: float32 [256, 2, 4096], P(('dp', 'grp'))
- scores: float32 [256, 1024], P('dp', 'grp')
All inputs are finite; a program needn't handle non-finite values.
Results may differ from a plain program's by a relative error of at most 0.014.
Values may be sent and summed in bfloat16 or wider, within the bound.
No kernel may reach another device: no remote copies, remote signals or barrier semaphores. Data moves between devices by JAX's collectives and lax.ppermute only.
A program may use at most 128 MiB of HBM per device.

v0:
```python
import math

import jax
import jax.numpy as jnp
from jax import lax
from jax.sharding import PartitionSpec as P

PIX = 128
BAND = 64
CLASSES = 256


ridge = 4.0


def dft_tables():
    positions = jnp.arange(PIX, dtype=jnp.int32)
    signed_freq = jnp.arange(BAND, dtype=jnp.int32) - BAND // 2
    residue = positions[:, None] * signed_freq[None, :] % PIX
    phase_angle = residue.astype(jnp.float32) * (2.0 * math.pi / PIX)
    scaling = 1.0 / math.sqrt(PIX)
    cosine = (jnp.cos(phase_angle) * scaling).astype(jnp.bfloat16)
    sine = (jnp.sin(phase_angle) * scaling).astype(jnp.bfloat16)
    return (jnp.concatenate([cosine, sine], axis=1), signed_freq)


def band_filter(signed_freq):
    squared = signed_freq.astype(jnp.float32) ** 2
    radius = squared[:, None] + squared[None, :]
    return jnp.exp(-radius / (BAND * BAND / 2.0)).reshape(BAND * BAND)


def shifted_transform(block_imgs, block_shifts, tables, signed_freq):
    num_img = block_imgs.shape[0]
    column_section = jnp.einsum(
        "iyx,xm->iym", block_imgs, tables, preferred_element_type=jnp.float32
    ).astype(jnp.bfloat16)
    row_section = jnp.einsum(
        "yt,iym->itm", tables, column_section, preferred_element_type=jnp.float32
    )
    cos_cos = row_section[:, :BAND, :BAND]
    cos_sin = row_section[:, :BAND, BAND:]
    sin_cos = row_section[:, BAND:, :BAND]
    sin_sin = row_section[:, BAND:, BAND:]
    four_real = cos_cos - sin_sin
    four_imag = -(sin_cos + cos_sin)
    shift_x = block_shifts[:, 0][:, None, None]
    shift_y = block_shifts[:, 1][:, None, None]
    residue = (signed_freq[None, :, None] * shift_y + signed_freq[None, None, :] * shift_x) % PIX
    phase_angle = residue.astype(jnp.float32) * (2.0 * math.pi / PIX)
    ramp_cos = jnp.cos(phase_angle)
    ramp_sin = jnp.sin(phase_angle)
    moved_real = four_real * ramp_cos + four_imag * ramp_sin
    moved_imag = four_imag * ramp_cos - four_real * ramp_sin
    return (
        jnp.stack([moved_real, moved_imag], axis=1)
        .reshape(num_img, 2 * BAND * BAND)
        .astype(jnp.bfloat16)
    )


def body(images, shifts, class_ids, next_block):
    tables, signed_freq = dft_tables()
    moved = shifted_transform(images, shifts, tables, signed_freq)
    num_img = moved.shape[0]
    tally_block = (jnp.arange(128, dtype=jnp.int32)[None, :] == 0).astype(jnp.bfloat16) * jnp.ones(
        (num_img, 1), jnp.bfloat16
    )
    extended = jnp.concatenate([moved, tally_block], axis=1)
    dp_count = lax.axis_size("dp")
    grp_count = lax.axis_size("grp")
    owned = CLASSES // (dp_count * grp_count)
    onehot = (
        jnp.arange(lax.axis_size("dp") * (owned * grp_count), dtype=jnp.int32)[:, None]
        == class_ids[None, :]
    ).astype(jnp.bfloat16)
    partial_value = lax.psum_scatter(
        jnp.dot(onehot, extended, preferred_element_type=jnp.float32).astype(jnp.bfloat16),
        "dp",
        scatter_dimension=0,
        tiled=True,
    )
    summed = lax.psum_scatter(partial_value, "grp", scatter_dimension=0, tiled=True).astype(
        jnp.float32
    )
    class_sum = summed[:, : 2 * BAND * BAND]
    members = summed[:, 2 * BAND * BAND]
    averages = (
        class_sum.reshape(owned, 2, BAND * BAND)
        * band_filter(signed_freq)[None, None, :]
        / (members + ridge)[:, None, None]
    )
    references = averages.astype(jnp.bfloat16)
    next_flat = next_block.reshape(next_block.shape[0], 2 * BAND * BAND)
    ref_piece = lax.all_gather(references, "grp", axis=0, tiled=True)
    energy = jnp.sum(jnp.square(ref_piece.astype(jnp.float32)), axis=(1, 2))
    flat_piece = ref_piece.reshape(ref_piece.shape[0], 2 * BAND * BAND)
    inner_prod = lax.dot_general(
        flat_piece, next_flat, (((1,), (1,)), ((), ())), preferred_element_type=jnp.float32
    )
    scores = (inner_prod - 0.5 * energy[:, None]) / BAND
    return (averages, scores)


def solution(mesh):
    placed = (
        P(("dp", "grp"), None, None),
        P(("dp", "grp"), None),
        P(("dp", "grp")),
        P("grp", None, None),
    )
    return jax.shard_map(
        body,
        mesh=mesh,
        in_specs=placed,
        out_specs=(P(("dp", "grp"), None, None), P("dp", "grp")),
        check_vma=False,
    )
```

profile of v0, /device:TPU:0, one launch (start us, length us, event | category | flops | bytes accessed | tf_op | source)
XLA Modules:
  0.0 296.4 jit_solution(536559923440776832)
XLA Ops:
  7.2 0.0 reduce-scatter.2.cloned.1.call-start
  7.2 0.2 multiply_convert_fusion.1
  7.5 0.8 fusion.46
  8.2 0.2 broadcast_multiply_fusion.1
  8.4 19.5 %fusion.9 = f32[512,128,128]{1,2,0:T(8,128)} fusion(bf16[512,128,128]{2,1,0:T(8,128)(2,1)} %param.4, bf16[128,64]{0,1:T(8,128)(2,1)S(1)} %get-tuple-element.15, bf16[128,64]{0,1:T(8,128)(2,1)S(1)} %get-tuple-element.14), kind=kOutput, calls=%fused_computation.18 | convolution fusion | flops 4303486976 | bytes 50364416 | tf_op jit(solution)/shard_map/yt,iym->itm/dot_general | solution.py:38
  27.9 81.0 %fusion.14 = (bf16[512,1,64,64]{2,3,0,1:T(8,128)(2,1)S(1)}, bf16[512,1,64,64]{2,3,0,1:T(8,128)(2,1)S(1)}) fusion(s32[512,64]{1,0:T(8,128)S(1)} %get-tuple-element.17, s32[512,64]{1,0:T(8,128)S(1)} %get-tuple-element.16, f32[512,128,128]{1,2,0:T(8,128)} %fusion.9), kind=kLoop, calls=%fused_computation.22 | loop fusion | flops 52428800 | bytes 42205184 | tf_op jit(solution)/shard_map/stack | solution.py:56
  108.9 7.9 %pad_maximum_fusion = bf16[512,2,64,64]{2,3,0,1:T(8,128)(2,1)} fusion(bf16[512,1,64,64]{2,3,0,1:T(8,128)(2,1)S(1)} %get-tuple-element.11, bf16[512,1,64,64]{2,3,0,1:T(8,128)(2,1)S(1)} %get-tuple-element.10), kind=kLoop, calls=%fused_computation.11 | loop fusion | flops 4194304 | bytes 16777216 | tf_op jit(solution)/shard_map/stack | solution.py:56
  116.8 22.3 %copy.12 = bf16[512,2,64,64]{0,3,2,1:T(8,128)(2,1)} copy(bf16[512,2,64,64]{2,3,0,1:T(8,128)(2,1)} %pad_maximum_fusion) | data formatting | bytes 16777216 | tf_op jit(solution)/shard_map/stack | solution.py:56
  139.2 8.7 %convolution_convert_fusion = bf16[256,8320]{1,0:T(8,128)(2,1)} fusion(bf16[512,8192]{0,1:T(8,128)(2,1)} %bitcast.29, bf16[8320]{0:T(1024)(128)(2,1)S(1)} %pad.1.clone, s32[512]{0:T(512)S(1)} %copy-done), kind=kOutput, calls=%fused_computation.19 | convolution fusion | flops 2200338432 | bytes 12667136 | tf_op jit(solution)/shard_map/dot_general | solution.py:78
  147.8 0.0 reduce-scatter.2.cloned.1.call-update
  147.9 0.0 all-reduce.3.cloned.1.call-start
  147.9 92.2 %reduce-scatter.2.cloned.1.call-done = bf16[32,8320]{1,0:T(8,128)(2,1)} async-done(((bf16[256,8320]{1,0:T(8,128)(2,1)}), bf16[32,8320]{1,0:T(8,128)(2,1)}) %reduce-scatter.2.cloned.1.call-update) | async-done | bytes 532496 | tf_op jit(solution)/shard_map/reduce_scatter | solution.py:77
  240.1 0.0 all-reduce.3.cloned.1.call-update
  240.2 0.1 multiply_exponential_fusion
  240.2 0.1 exp.11
  240.3 0.6 dynamic-slice
  241.6 33.8 %all-reduce.3.cloned.1.call-done = bf16[32,8320]{1,0:T(8,128)(2,1)} async-done(((bf16[32,8320]{1,0:T(8,128)(2,1)}), bf16[32,8320]{1,0:T(8,128)(2,1)}) %all-reduce.3.cloned.1.call-update) | async-done | bytes 532496
  275.4 0.9 dynamic-slice_convert_fusion
  276.3 0.1 fusion.41
  276.4 0.1 fusion.45
  276.5 6.7 %all_gather.3 = bf16[32,2,4096]{2,0,1:T(8,128)(2,1)S(1)} all-gather(bf16[8,2,4096]{2,0,1:T(8,128)(2,1)S(1)} %get-tuple-element.8), channel_id=1, replica_groups=mesh['dp'=8,'grp'=4] {'grp'}, dimensions={0}, use_global_device_ids=true | all-gather | bytes 655360 | tf_op jit(solution)/shard_map/all_gather | solution.py:95
  283.2 0.2 multiply_reduce_fusion
  283.5 0.9 copy.14
  284.4 5.2 %fusion.27 = f32[32,256]{1,0:T(8,128)} fusion(bf16[32,2,4096]{2,0,1:T(8,128)(2,1)S(1)} %all_gather.3, bf16[256,2,4096]{2,1,0:T(2,128)(2,1)} %param.7, f32[32]{0:T(128)S(1)} %broadcast_multiply_fusion.2), kind=kOutput, calls=%fused_computation.31 | convolution fusion | flops 134234112 | bytes 4751488 | tf_op jit(solution)/shard_map/dot_general | solution.py:98
  (10 shorter events, 0.1 us)
Async XLA Ops:
  7.2 232.9 %reduce-scatter.2.cloned.1.call-start = ((), (), s32[]{:S(2)}) async-start(), calls=%async_computation.1 | async-start | bytes 4792320 | tf_op jit(solution)/shard_map/reduce_scatter | solution.py:77
  116.8 22.3 %copy-start = (s32[512]{0:T(512)S(1)}, s32[512]{0:T(512)}, u32[]{:S(2)}) copy-start(s32[512]{0:T(512)} %param.6) | copy-start | bytes 6148
  139.1 101.2 %copy-start.1 = (u32[32]{0:T(128)S(1)}, u32[32]{0:T(128)}, u32[]{:S(2)}) copy-start(u32[32]{0:T(128)} %constant.46) | copy-start | bytes 388
  147.9 127.5 %all-reduce.3.cloned.1.call-start = ((), (), s32[]{:S(2)}) async-start(), calls=%async_computation.2 | async-start | bytes 1064960
Sparse Core Ops, SparseCore 0:
  148.0 92.0 reduce-scatter.1
  242.6 32.7 all-reduce.2
where the time goes:
time: 297 us; the launch traced here: 296 us
  waiting for transfers between devices  126 us (42%)
  other arithmetic  90.7 us (31%)
  matrix products  33.4 us (11%)
  local copies, waits for them, and re-layouts  24.7 us (8%)
  between operations  14.8 us (5%)
  blocking collectives  6.69 us (2%)
    reduce_scatter x1, waiting for transfers between devices, body(): lax.psum_scatter(jnp.dot(onehot, extended, preferred_element_type=jnp.flo...  92.2 us
    another operation x2, other arithmetic, shifted_transform(): jnp.stack([moved_real, moved_imag], axis=1)  88.9 us
    unnamed x3, waiting for transfers between devices  33.8 us
    another operation x1, local copies, waits for them, and re-layouts, shifted_transform(): jnp.stack([moved_real, moved_imag], axis=1)  22.3 us
    dot_general x1, matrix products, shifted_transform(): jnp.einsum('yt,iym->itm', tables, column_section, preferred_element_type=...  19.5 us
    dot_general x1, matrix products, body(): jnp.dot(onehot, extended, preferred_element_type=jnp.float32)  8.67 us
    all_gather x1, blocking collectives, body(): ref_piece = lax.all_gather(references, 'grp', axis=0, tiled=True)  6.69 us
  transfers between devices with their start and end apart: 2, of which 2 were waited for; matrix products, arithmetic and copies ran while one was open for 0% of the time, Pallas kernels for 0%

commit v1 on v0

v1 whole, which is shorter than its diff:
```python
import functools
import math

import jax
import jax.numpy as jnp
import ml_dtypes
import numpy as np
from jax import lax
from jax.experimental import pallas as pl
from jax.experimental.pallas import tpu as pltpu
from jax.sharding import PartitionSpec as P

PIX = 128
BAND = 64
CLASSES = 256
HALF = BAND // 2
RIDGE = 4.0
REACH = 16
SLAB = PIX + 2 * REACH
TILE = 8
PACK = 16
DIGITS = 4
CHUNK = 32
UNROLL = 8
MIB = 1 << 20


def basis():
    position = np.arange(PIX)
    freq = np.concatenate([np.arange(HALF + 1), np.arange(1, HALF + 1)])
    angle = (position[:, None] * freq[None, :] % PIX) * (2.0 * math.pi / PIX)
    is_cos = np.arange(BAND + 1) <= HALF
    table = np.where(is_cos[None, :], np.cos(angle), np.sin(angle)) / math.sqrt(PIX)
    return table.astype(np.float32).astype(ml_dtypes.bfloat16)


def column_table(pairs):
    table = basis()
    out = np.zeros((2 * PIX, 2 * PIX), ml_dtypes.bfloat16)
    for side in range(2):
        rows = slice(side * PIX, (side + 1) * PIX)
        out[rows, side * BAND : (side + 1) * BAND] = table[:, :BAND]
        out[rows, PIX + side * pairs] = table[:, BAND]
    return out


def row_table():
    out = np.zeros((5 * PACK, PIX), ml_dtypes.bfloat16)
    out[: BAND + 1] = basis().T
    return out


def expand_table():
    out = np.zeros((PIX, 2 * PIX), np.float32)
    for at in range(BAND):
        k = at - HALF
        for copy in range(2):
            out[abs(k), copy * BAND + at] = 1.0
            if k:
                row = BAND if abs(k) == HALF else HALF + abs(k)
                out[row, PIX + copy * BAND + at] = math.copysign(1.0, k)
    return out


def filter_table():
    squared = (np.arange(BAND, dtype=np.float32) - HALF) ** 2
    radius = squared[:, None] + squared[None, :]
    return np.exp(-radius / (BAND * BAND / 2.0)).reshape(BAND // 2, 2 * BAND).astype(np.float32)


def owner_of(me, near, far, other, groups):
    dp, grp = me[0], me[1]
    there_dp = dp ^ ((far << 1) | (near & 1))
    there_grp = grp ^ (((near >> 1) << 1) | other)
    return there_dp * groups + there_grp


def sums_kernel(
    me, ids, shifts, ids_rows, images, col, row, send, keep, held, acc, sems, *, groups, own
):
    count = images.shape[0]
    chunks = count // CHUNK
    pairs = own // 2
    nears, fars = send.shape[0], send.shape[1]

    def fetch(k):
        span = pl.ds(pl.multiple_of(k * CHUNK, CHUNK), CHUNK)
        return pltpu.make_async_copy(images.at[span], held.at[span], sems.at[k])

    for k in range(chunks):
        fetch(k).start()
    acc[...] = jnp.zeros_like(acc)

    def add_chunk(k, _):
        fetch(k).wait()

        def add_some(s, _):
            for u in range(UNROLL):
                i = k * CHUNK + s * UNROLL + u
                dx = shifts[0, i]
                at = ids[i] * SLAB + REACH + shifts[1, i]
                turned = pltpu.roll(
                    held[i].astype(jnp.float32), jnp.where(dx < 0, dx + PIX, dx), 1
                )
                acc[pl.ds(at, PIX), :] = acc[pl.ds(at, PIX), :] + turned
            return 0

        return lax.fori_loop(0, CHUNK // UNROLL, add_some, 0)

    lax.fori_loop(0, chunks, add_chunk, 0)

    lane = lax.broadcasted_iota(jnp.int32, (TILE, PIX), 1)
    sub = lax.broadcasted_iota(jnp.int32, (TILE, PIX), 0)

    def folded(c):
        at = pl.multiple_of(c * SLAB, TILE)
        head = acc[pl.ds(at + REACH, REACH), :] + acc[pl.ds(at + PIX + REACH, REACH), :]
        mid = acc[pl.ds(at + 2 * REACH, PIX - 2 * REACH), :]
        tail = acc[pl.ds(at + PIX, REACH), :] + acc[pl.ds(at, REACH), :]
        return jnp.concatenate([head, mid, tail], axis=0).astype(jnp.bfloat16)

    def transform(owner, out):
        stacked = jnp.concatenate(
            [
                jnp.concatenate([folded(owner * own + j), folded(owner * own + j + pairs)], axis=1)
                for j in range(pairs)
            ],
            axis=0,
        )
        section = jnp.dot(stacked, col[...], preferred_element_type=jnp.float32).astype(
            jnp.bfloat16
        )
        extra = None
        edge = []
        for j in range(pairs):
            both = jnp.dot(
                row[...], section[j * PIX : (j + 1) * PIX], preferred_element_type=jnp.float32
            )
            out[j * BAND : (j + 1) * BAND, :] = both[:BAND, :PIX].astype(jnp.bfloat16)
            edge.append(both[BAND : BAND + 1, :PIX])
            last = both[:, PIX:]
            last = pltpu.roll(last, j, 1) if j else last
            extra = last if extra is None else extra + last
        extra = jnp.concatenate(
            [extra, jnp.zeros((PIX - extra.shape[0], PIX), jnp.float32)], axis=0
        ).T[:TILE]
        hits = jnp.zeros((TILE, PIX), jnp.float32)
        for r in range(ids_rows.shape[0]):
            hits += (ids_rows[r : r + 1, :] == owner * own + sub).astype(jnp.float32)
        rest = jnp.sum(hits, axis=1, keepdims=True)
        for d in range(DIGITS):
            upper = jnp.floor(rest * 0.125) if d < DIGITS - 1 else jnp.zeros_like(rest)
            extra = jnp.where(lane == BAND + 1 + d, rest - 8.0 * upper, extra)
            rest = upper
        edge.append(jnp.zeros((TILE - pairs, PIX), jnp.float32))
        out[pairs * BAND :, :] = jnp.concatenate([*edge, extra], axis=0).astype(jnp.bfloat16)

    def one(n, _):
        near, far = n // fars, n % fars
        transform(owner_of(me, near, far, 1, groups), send.at[near, far])
        transform(owner_of(me, near, far, 0, groups), keep.at[near, far])
        return 0

    lax.fori_loop(0, nears * fars, one, 0)


def averages_kernel(*refs, own, parts):
    pieces, (expand, taper, real, imag, rounded, wide, rows) = refs[:parts], refs[parts:]
    pairs = own // 2
    total = pieces[0][...].astype(jnp.float32)
    for piece in pieces[1:]:
        total += piece[...].astype(jnp.float32)
    main, ends = total[: pairs * BAND], total[pairs * BAND :]
    if own < TILE:
        wide[...] = jnp.zeros_like(wide)
    wide[: pairs * BAND, :] = main
    wide[pairs * BAND : 2 * pairs * BAND, :] = pltpu.roll(main, BAND, 1)
    extra = ends[TILE:]
    lane = lax.broadcasted_iota(jnp.int32, (TILE, PIX), 1)
    for t in range(BAND + 1):
        if t < BAND:
            line = wide[pl.ds(t, TILE, stride=BAND), :]
        else:
            edge = ends[:pairs]
            line = jnp.concatenate([edge, pltpu.roll(ends[:TILE], BAND, 1)[:pairs]], axis=0)
            if own < TILE:
                line = jnp.concatenate([line, jnp.zeros((TILE - own, PIX), jnp.float32)], axis=0)
        line = jnp.where(
            lane < BAND, line, jnp.where(lane == BAND, extra[:, t : t + 1], 0.0)
        )
        rows[t * TILE : (t + 1) * TILE, :] = line
    spread = jnp.dot(
        rows[...], expand[...], preferred_element_type=jnp.float32, precision=lax.Precision.HIGHEST
    )

    def cos_part(t):
        return spread[t * TILE : (t + 1) * TILE, :PIX]

    def sin_part(t):
        return spread[t * TILE : (t + 1) * TILE, PIX:]

    members = jnp.zeros((TILE, 1), jnp.float32)
    for d in range(DIGITS):
        members += extra[:, BAND + 1 + d : BAND + 2 + d] * float(8**d)
    weight = members + RIDGE

    def at_frequency(k):
        c = abs(k)
        if k == 0:
            return cos_part(0), -sin_part(0)
        s = BAND if c == HALF else HALF + c
        if k > 0:
            return cos_part(c) - sin_part(s), -(cos_part(s) + sin_part(c))
        return cos_part(c) + sin_part(s), cos_part(s) - sin_part(c)

    for u in range(BAND // 2):
        even, odd = at_frequency(2 * u - HALF), at_frequency(2 * u + 1 - HALF)
        span = slice(u * PIX, (u + 1) * PIX)
        for part, out in ((0, real), (1, imag)):
            value = jnp.where(lane < BAND, even[part], odd[part]) * taper[u : u + 1, :] / weight
            out[:, span] = value
            at = part * BAND * BAND + u * PIX
            rounded[:, at : at + PIX] = value.astype(jnp.bfloat16)


def scores_kernel(me, *refs, own, groups):
    pieces, (block, out) = refs[:groups], refs[groups:]
    held = jnp.concatenate([piece[:own] for piece in pieces], axis=0)
    inner = lax.dot_general(
        held, block[...], (((1,), (1,)), ((), ())), preferred_element_type=jnp.float32
    )
    energy = jnp.sum(jnp.square(held.astype(jnp.float32)), axis=1, keepdims=True)
    result = (inner - 0.5 * energy) / BAND
    for k in range(groups):
        at = (me[1] ^ k) * own
        if own % TILE == 0:
            out[pl.ds(pl.multiple_of(at, TILE), own), :] = result[k * own : (k + 1) * own]
        else:
            for j in range(own):
                out[pl.ds(at + j, 1), :] = result[k * own + j : k * own + j + 1]


def swap(array, axis, flip):
    size = lax.axis_size(axis)
    return lax.ppermute(array, axis, [(i, i ^ flip) for i in range(size)])


def hop(array, near, groups):
    both = lax.axis_size("dp") * groups
    return lax.ppermute(
        array,
        ("dp", "grp"),
        [(i, i ^ ((near & 1) * groups | (near >> 1) * 2)) for i in range(both)],
    )


def body(images, shifts, class_ids, next_block):
    dp_count, groups = lax.axis_size("dp"), lax.axis_size("grp")
    own = CLASSES // (dp_count * groups)
    pairs = own // 2
    count = images.shape[0]
    nears, fars = groups, dp_count // 2
    block_rows = pairs * BAND + PACK
    me = jnp.stack([lax.axis_index("dp"), lax.axis_index("grp")]).astype(jnp.int32)
    smem = pl.BlockSpec(memory_space=pltpu.SMEM)
    vmem = pl.BlockSpec(memory_space=pltpu.VMEM)
    hbm = pl.BlockSpec(memory_space=pl.ANY)
    partial = jax.ShapeDtypeStruct((nears, fars, block_rows, PIX), jnp.bfloat16)
    send, keep = pl.pallas_call(
        functools.partial(sums_kernel, groups=groups, own=own),
        out_shape=(partial, partial),
        in_specs=[smem, smem, smem, vmem, hbm, vmem, vmem],
        out_specs=(vmem, vmem),
        scratch_shapes=[
            pltpu.VMEM((count, PIX, PIX), jnp.bfloat16),
            pltpu.VMEM((CLASSES * SLAB, PIX), jnp.float32),
            pltpu.SemaphoreType.DMA((count // CHUNK,)),
        ],
        compiler_params=pltpu.CompilerParams(vmem_limit_bytes=52 * MIB),
    )(
        me,
        class_ids,
        shifts.T,
        class_ids.reshape(count // PIX, PIX),
        images,
        jnp.asarray(column_table(pairs)),
        jnp.asarray(row_table()),
    )
    got = swap(send, "grp", 1)
    part = [(keep[q].astype(jnp.float32) + got[q].astype(jnp.float32)).astype(jnp.bfloat16) for q in range(nears)]
    met = [part[0]] + [hop(part[q], q, groups) for q in range(1, nears)]
    chip_sum = sum(m.astype(jnp.float32) for m in met).astype(jnp.bfloat16)
    pieces = [chip_sum[0]] + [swap(chip_sum[r], "dp", r << 1) for r in range(1, fars)]
    flat = BAND * BAND
    real, imag, rounded = pl.pallas_call(
        functools.partial(averages_kernel, own=own, parts=fars),
        out_shape=(
            jax.ShapeDtypeStruct((TILE, flat), jnp.float32),
            jax.ShapeDtypeStruct((TILE, flat), jnp.float32),
            jax.ShapeDtypeStruct((TILE, 2 * flat), jnp.bfloat16),
        ),
        in_specs=[vmem] * (fars + 2),
        out_specs=(vmem, vmem, vmem),
        scratch_shapes=[
            pltpu.VMEM((TILE * BAND, PIX), jnp.float32),
            pltpu.VMEM(((BAND + 1) * TILE, PIX), jnp.float32),
        ],
    )(*pieces, jnp.asarray(expand_table()), jnp.asarray(filter_table()))
    averages = jnp.stack([real[:own], imag[:own]], axis=1)
    held = [rounded] + [swap(rounded, "grp", k) for k in range(1, groups)]
    fresh = next_block.reshape(next_block.shape[0], 2 * flat)
    scores = pl.pallas_call(
        functools.partial(scores_kernel, own=own, groups=groups),
        out_shape=jax.ShapeDtypeStruct((own * groups, fresh.shape[0]), jnp.float32),
        in_specs=[smem] + [vmem] * (groups + 1),
        out_specs=vmem,
    )(me, *held, fresh)
    return averages, scores


def solution(mesh):
    placed = (
        P(("dp", "grp"), None, None),
        P(("dp", "grp"), None),
        P(("dp", "grp")),
        P("grp", None, None),
    )
    return jax.shard_map(
        body,
        mesh=mesh,
        in_specs=placed,
        out_specs=(P(("dp", "grp"), None, None), P("dp", "grp")),
        check_vma=False,
    )
```

time: 297 us -> 80.6 us (0.27)
  waiting for transfers between devices: 126 us -> 19.5 us
  other arithmetic: 90.7 us -> 3.7 us
  matrix products: 33.4 us -> 0 us
  Pallas kernels: 0 us -> 32.5 us
  between operations: 14.8 us -> 0.71 us
  local copies, waits for them, and re-layouts: 24.7 us -> 12.4 us
  starting transfers between devices: 0.08 us -> 11.2 us
  blocking collectives: 6.69 us -> 0 us
    reduce_scatter x1 -> x0, waiting for transfers between devices: 92.2 us -> none  [body(): lax.psum_scatter(jnp.dot(onehot, extended, preferred_element_type=jnp.flo...]
    another operation x2, other arithmetic: 88.9 us -> 1.06 us  [the longest x1 0.99 us: body(): averages = jnp.stack([real[:own], imag[:own]], axis=1)]
    unnamed x3 -> x0, waiting for transfers between devices: 33.8 us -> none
    dot_general x3 -> x0, matrix products: 33.4 us -> none  [the longest x1 19.5 us: shifted_transform(): jnp.einsum('yt,iym->itm', tables, column_section, preferred_element_type=...]
    pallas_call x0 -> x3, Pallas kernels: none -> 32.5 us  [the longest x1 25.6 us: body(): pl.pallas_call(functools.partial(sums_kernel, groups=groups, own=own), ou...]
    another operation x1 -> x0, local copies, waits for them, and re-layouts: 22.3 us -> none  [shifted_transform(): jnp.stack([moved_real, moved_imag], axis=1)]
    ppermute x0 -> x10, waiting for transfers between devices: none -> 19.5 us  [the longest x3 14.1 us: hop(): lax.ppermute(array, ('dp', 'grp'), [(i, i ^ ((near & 1) * groups | (near...]
    ppermute x0 -> x10, starting transfers between devices: none -> 11.2 us  [the longest x7 6.77 us: swap(): return lax.ppermute(array, axis, [(i, i ^ flip) for i in range(size)])]
  transfers between devices with their start and end apart: 2 -> 10, of which waited for: 2 -> 6; matrix products, arithmetic and copies ran while one was open for 0% -> 10% of each run, Pallas kernels for 0% -> 0%
where the time goes in v1:
time: 80.6 us; the launch traced here: 80 us
  Pallas kernels  32.5 us (40%)
  waiting for transfers between devices  19.5 us (24%)
  local copies, waits for them, and re-layouts  12.4 us (15%)
  starting transfers between devices  11.2 us (14%)
  other arithmetic  3.7 us (5%)
    pallas_call x1, Pallas kernels, body(): pl.pallas_call(functools.partial(sums_kernel, groups=groups, own=own), ou...  25.6 us
    ppermute x3, waiting for transfers between devices, hop(): lax.ppermute(array, ('dp', 'grp'), [(i, i ^ ((near & 1) * groups | (near...  14.1 us
    unnamed x26, local copies, waits for them, and re-layouts  11.7 us
    ppermute x7, starting transfers between devices, swap(): return lax.ppermute(array, axis, [(i, i ^ flip) for i in range(size)])  6.77 us
    ppermute x7, waiting for transfers between devices, swap(): return lax.ppermute(array, axis, [(i, i ^ flip) for i in range(size)])  5.41 us
    ppermute x3, starting transfers between devices, hop(): lax.ppermute(array, ('dp', 'grp'), [(i, i ^ ((near & 1) * groups | (near...  4.47 us
    pallas_call x1, Pallas kernels, body(): pl.pallas_call(functools.partial(scores_kernel, own=own, groups=groups),...  4.44 us
    pallas_call x1, Pallas kernels, body(): pl.pallas_call(functools.partial(averages_kernel, own=own, parts=fars), o...  2.47 us
  transfers between devices with their start and end apart: 10, of which 6 were waited for; matrix products, arithmetic and copies ran while one was open for 10% of the time, Pallas kernels for 0%

profile of v1, /device:TPU:0, one launch (start us, length us, event | category | flops | bytes accessed | tf_op | source)
XLA Modules:
  0.0 80.0 jit_solution(1330728384758357912)
XLA Ops:
  0.7 0.9 %copy-done = bf16[256,256]{1,0:T(8,128)(2,1)S(1)} copy-done((bf16[256,256]{1,0:T(8,128)(2,1)S(1)}, bf16[256,256]{1,0:T(8,128)(2,1)}, u32[]{:S(2)}) %copy-start) | copy-done | bytes 131096
  1.6 0.7 copy-done.1
  2.3 0.7 copy-done.2
  3.0 0.7 copy-done.3
  3.7 25.6 %shard_map.95 = (bf16[4,4,272,128]{3,2,1,0:T(8,128)(2,1)S(1)}, bf16[4,4,272,128]{3,2,1,0:T(8,128)(2,1)}) custom-call(s32[2]{0:T(128)S(1)} %pad_add_fusion.me, s32[512]{0:T(512)S(1)} %copy-done.2, s32[2,512]{1,0:T(2,128)S(1)} %bitcast.28, s32[4,128]{1,0:T(4,128)S(1)} %bitcast.27, bf16[512,128,128]{2,1,0:T(8,128)(2,1)} %images.1, ...), custom_call_target="tpu_custom_call" | custom-call | tf_op jit(solution)/shard_map/pallas_call | solution.py:269
  29.8 2.4 %collective-permute-done = bf16[4,4,272,128]{3,2,1,0:T(8,128)(2,1)S(1)} collective-permute-done((bf16[4,4,272,128]{3,2,1,0:T(8,128)(2,1)S(1)}, bf16[4,4,272,128]{3,2,1,0:T(8,128)(2,1)S(1)}, u32[]{:S(2)}, u32[]{:S(2)}) %collective-permute-start) | collective-permute-done | bytes 1114144 | tf_op jit(solution)/shard_map/ppermute | solution.py:245
  32.2 1.5 %fusion.4 = (bf16[4,272,128]{2,1,0:T(8,128)(2,1)S(1)}, bf16[4,272,128]{2,1,0:T(8,128)(2,1)S(1)}, bf16[4,272,128]{2,1,0:T(8,128)(2,1)S(1)}) fusion(bf16[4,4,272,128]{3,2,1,0:T(8,128)(2,1)S(1)} %collective-permute-done, bf16[4,4,272,128]{3,2,1,0:T(8,128)(2,1)} %get-tuple-element.7), kind=kLoop, calls=%fused_computation.9 | loop fusion | flops 1671168 | bytes 2506752 | tf_op jit(solution)/shard_map/convert_element_type | solution.py:290
  33.7 2.9 %collective-permute-start.1 = (bf16[4,272,128]{2,1,0:T(8,128)(2,1)S(1)}, bf16[4,272,128]{2,1,0:T(8,128)(2,1)S(1)}, u32[]{:S(2)}, u32[]{:S(2)}) collective-permute-start(bf16[4,272,128]{2,1,0:T(8,128)(2,1)S(1)} %get-tuple-element.14), channel_id=1, source_target_pairs={{0,4},{1,5},{2,6},{3,7},{4,0},{5,1},{6,2},{7,3},{8,12},{9,13},{10,... | collective-permute-start | bytes 835592 | tf_op jit(solution)/shard_map/ppermute | solution.py:250
  36.6 1.5 %collective-permute-start.3 = (bf16[4,272,128]{2,1,0:T(8,128)(2,1)S(1)}, bf16[4,272,128]{2,1,0:T(8,128)(2,1)S(1)}, u32[]{:S(2)}, u32[]{:S(2)}) collective-permute-start(bf16[4,272,128]{2,1,0:T(8,128)(2,1)S(1)} %get-tuple-element.15), channel_id=1, source_target_pairs={{0,6},{1,7},{2,4},{3,5},{4,2},{5,3},{6,0},{7,1},{8,14},{9,15},{10,... | collective-permute-start | bytes 835592 | tf_op jit(solution)/shard_map/ppermute | solution.py:250
  38.2 5.9 %collective-permute-done.1 = bf16[4,272,128]{2,1,0:T(8,128)(2,1)S(1)} collective-permute-done((bf16[4,272,128]{2,1,0:T(8,128)(2,1)S(1)}, bf16[4,272,128]{2,1,0:T(8,128)(2,1)S(1)}, u32[]{:S(2)}, u32[]{:S(2)}) %collective-permute-start.1) | collective-permute-done | bytes 278560 | tf_op jit(solution)/shard_map/ppermute | solution.py:250
  44.1 6.8 %collective-permute-done.3 = bf16[4,272,128]{2,1,0:T(8,128)(2,1)S(1)} collective-permute-done((bf16[4,272,128]{2,1,0:T(8,128)(2,1)S(1)}, bf16[4,272,128]{2,1,0:T(8,128)(2,1)S(1)}, u32[]{:S(2)}, u32[]{:S(2)}) %collective-permute-start.3) | collective-permute-done | bytes 278560 | tf_op jit(solution)/shard_map/ppermute | solution.py:250
  50.9 1.4 %collective-permute-done.2 = bf16[4,272,128]{2,1,0:T(8,128)(2,1)S(1)} collective-permute-done((bf16[4,272,128]{2,1,0:T(8,128)(2,1)S(1)}, bf16[4,272,128]{2,1,0:T(8,128)(2,1)S(1)}, u32[]{:S(2)}, u32[]{:S(2)}) %collective-permute-start.2) | collective-permute-done | bytes 278560 | tf_op jit(solution)/shard_map/ppermute | solution.py:250
  52.2 1.1 %fusion.2 = bf16[4,272,128]{2,1,0:T(8,128)(2,1)S(1)} fusion(bf16[4,272,128]{2,1,0:T(8,128)(2,1)S(1)} %collective-permute-done.3, bf16[4,272,128]{2,1,0:T(8,128)(2,1)S(1)} %collective-permute-done.2, bf16[4,272,128]{2,1,0:T(8,128)(2,1)S(1)} %collective-permute-done.1, bf16[4,4,272,128]{3,2,1,0:T(8,128)(2,1)S(1)} %collective-permute-done, ...), kind=kLoop, calls=%fused_computation.3 | loop fusion | flops 1671168 | bytes 1671168 | tf_op jit(solution)/shard_map/convert_element_type | solution.py:292
  54.0 3.6 %collective-permute-start.6 = (bf16[272,128]{1,0:T(8,128)(2,1)S(1)}, bf16[272,128]{1,0:T(8,128)(2,1)S(1)}, u32[]{:S(2)}, u32[]{:S(2)}) collective-permute-start(bf16[272,128]{1,0:T(8,128)(2,1)S(1)} %get-tuple-element.17), channel_id=1, source_target_pairs={{0,24},{4,28},{8,16},{12,20},{16,8},{20,12},{24,0},{28,4},{1,25},{... | collective-permute-start | bytes 208904 | tf_op jit(solution)/shard_map/ppermute | solution.py:245
  57.6 0.8 collective-permute-start.4
  58.4 6.4 %copy.11 = bf16[32,8,2,4096]{3,1,2,0:T(8,128)(2,1)} copy(bf16[32,8,2,4096]{3,2,1,0:T(2,128)(2,1)S(1)} %bitcast.30) | data formatting | bytes 8388608
  65.6 2.5 %shard_map.96 = (f32[8,4096]{1,0:T(8,128)}, f32[8,4096]{1,0:T(8,128)}, bf16[8,8192]{1,0:T(8,128)(2,1)}) custom-call(bf16[272,128]{1,0:T(8,128)(2,1)} %get-tuple-element.20.refs_0_, bf16[272,128]{1,0:T(8,128)(2,1)} %copy-done.11, bf16[272,128]{1,0:T(8,128)(2,1)} %copy-done.10, bf16[272,128]{1,0:T(8,128)(2,1)} %copy-done.9, ...), custom_call_target="tpu_custom_call" | custom-call | tf_op jit(solution)/shard_map/pallas_call | solution.py:295
  68.4 1.5 %collective-permute-start.7 = (bf16[8,8192]{1,0:T(8,128)(2,1)}, bf16[8,8192]{1,0:T(8,128)(2,1)S(1)}, u32[]{:S(2)}, u32[]{:S(2)}) collective-permute-start(bf16[8,8192]{1,0:T(8,128)(2,1)} %get-tuple-element.11.refs_0_), channel_id=1, source_target_pairs={{0,1},{1,0},{2,3},{3,2},{4,5},{5,4},{6,7},{7,6},{8,9},{9,8},{10,11... | collective-permute-start | bytes 393224 | tf_op jit(solution)/shard_map/ppermute | solution.py:245
  69.9 1.0 %pad_maximum_fusion = f32[8,2,4096]{2,0,1:T(8,128)S(1)} fusion(f32[8,1,4096]{2,0,1:T(8,128)} %bitcast.32, f32[8,1,4096]{2,0,1:T(8,128)} %bitcast.31), kind=kLoop, calls=%fused_computation.12 | loop fusion | flops 65536 | bytes 524288 | tf_op jit(solution)/shard_map/stack | solution.py:309
  70.9 0.9 %copy.10 = f32[8,2,4096]{2,1,0:T(2,128)} copy(f32[8,2,4096]{2,0,1:T(8,128)S(1)} %pad_maximum_fusion) | data formatting | bytes 524288
  71.8 2.2 %collective-permute-done.9.refs_3_ = bf16[8,8192]{1,0:T(8,128)(2,1)S(1)} collective-permute-done((bf16[8,8192]{1,0:T(8,128)(2,1)}, bf16[8,8192]{1,0:T(8,128)(2,1)S(1)}, u32[]{:S(2)}, u32[]{:S(2)}) %collective-permute-start.9) | collective-permute-done | bytes 131104 | tf_op jit(solution)/shard_map/ppermute | solution.py:245
  74.0 0.8 collective-permute-done.8.refs_2_
  74.8 0.6 copy-done.7
  75.5 4.4 %shard_map.97 = f32[32,256]{1,0:T(8,128)} custom-call(s32[2]{0:T(128)} %copy-done.4, bf16[8,8192]{1,0:T(8,128)(2,1)} %get-tuple-element.11.refs_0_, bf16[8,8192]{1,0:T(8,128)(2,1)} %copy-done.8, bf16[8,8192]{1,0:T(8,128)(2,1)} %copy-done.7, bf16[8,8192]{1,0:T(8,128)(2,1)} %copy-done.6, bf16[256,8192]{1,0:T(8,128)(2,1)} %bitcast.29), custom_call_target="tpu_custom_call" | custom-call | tf_op jit(solution)/shard_map/pallas_call | solution.py:312
  (30 shorter events, 2.4 us)
Async XLA Ops:
  0.7 28.6 %copy-start.4 = (s32[2]{0:T(128)}, s32[2]{0:T(128)S(1)}, u32[]{:S(2)}) copy-start(s32[2]{0:T(128)S(1)} %pad_add_fusion.me) | copy-start | bytes 28
  0.7 0.9 %copy-start = (bf16[256,256]{1,0:T(8,128)(2,1)S(1)}, bf16[256,256]{1,0:T(8,128)(2,1)}, u32[]{:S(2)}) copy-start(bf16[256,256]{1,0:T(8,128)(2,1)} %constant.17.clone.col) | copy-start | bytes 393220
  1.6 0.7 copy-start.1
  2.3 0.7 copy-start.2
  3.0 0.7 copy-start.3
  29.3 2.9 %collective-permute-start = (bf16[4,4,272,128]{3,2,1,0:T(8,128)(2,1)S(1)}, bf16[4,4,272,128]{3,2,1,0:T(8,128)(2,1)S(1)}, u32[]{:S(2)}, u32[]{:S(2)}) collective-permute-start(bf16[4,4,272,128]{3,2,1,0:T(8,128)(2,1)S(1)} %get-tuple-element.8), channel_id=1, source_target_pairs={{0,1},{1,0},{2,3},{3,2},{4,5},{5,4},{6,7},{7,6},{8,9},{9,8},{10,11... | collective-permute-start | bytes 3342344 | tf_op jit(solution)/shard_map/ppermute | solution.py:245
  32.2 26.2 %copy-start.5 = (bf16[256,2,4096]{2,1,0:T(2,128)(2,1)S(1)}, bf16[256,2,4096]{2,1,0:T(2,128)(2,1)}, u32[]{:S(2)}) copy-start(bf16[256,2,4096]{2,1,0:T(2,128)(2,1)} %param.11) | copy-start | bytes 12582916
  33.7 10.4 %collective-permute-start.1 = (bf16[4,272,128]{2,1,0:T(8,128)(2,1)S(1)}, bf16[4,272,128]{2,1,0:T(8,128)(2,1)S(1)}, u32[]{:S(2)}, u32[]{:S(2)}) collective-permute-start(bf16[4,272,128]{2,1,0:T(8,128)(2,1)S(1)} %get-tuple-element.14), channel_id=1, source_target_pairs={{0,4},{1,5},{2,6},{3,7},{4,0},{5,1},{6,2},{7,3},{8,12},{9,13},{10,... | collective-permute-start | bytes 835592 | tf_op jit(solution)/shard_map/ppermute | solution.py:250
  36.6 14.2 %collective-permute-start.3 = (bf16[4,272,128]{2,1,0:T(8,128)(2,1)S(1)}, bf16[4,272,128]{2,1,0:T(8,128)(2,1)S(1)}, u32[]{:S(2)}, u32[]{:S(2)}) collective-permute-start(bf16[4,272,128]{2,1,0:T(8,128)(2,1)S(1)} %get-tuple-element.15), channel_id=1, source_target_pairs={{0,6},{1,7},{2,4},{3,5},{4,2},{5,3},{6,0},{7,1},{8,14},{9,15},{10,... | collective-permute-start | bytes 835592 | tf_op jit(solution)/shard_map/ppermute | solution.py:250
  38.1 14.1 %collective-permute-start.2 = (bf16[4,272,128]{2,1,0:T(8,128)(2,1)S(1)}, bf16[4,272,128]{2,1,0:T(8,128)(2,1)S(1)}, u32[]{:S(2)}, u32[]{:S(2)}) collective-permute-start(bf16[4,272,128]{2,1,0:T(8,128)(2,1)S(1)} %get-tuple-element.16), channel_id=1, source_target_pairs={{0,2},{1,3},{2,0},{3,1},{4,6},{5,7},{6,4},{7,5},{8,10},{9,11},{10,... | collective-permute-start | bytes 835592 | tf_op jit(solution)/shard_map/ppermute | solution.py:250
  54.0 10.8 %collective-permute-start.6 = (bf16[272,128]{1,0:T(8,128)(2,1)S(1)}, bf16[272,128]{1,0:T(8,128)(2,1)S(1)}, u32[]{:S(2)}, u32[]{:S(2)}) collective-permute-start(bf16[272,128]{1,0:T(8,128)(2,1)S(1)} %get-tuple-element.17), channel_id=1, source_target_pairs={{0,24},{4,28},{8,16},{12,20},{16,8},{20,12},{24,0},{28,4},{1,25},{... | collective-permute-start | bytes 208904 | tf_op jit(solution)/shard_map/ppermute | solution.py:245
  57.6 7.2 %collective-permute-start.5 = (bf16[272,128]{1,0:T(8,128)(2,1)S(1)}, bf16[272,128]{1,0:T(8,128)(2,1)S(1)}, u32[]{:S(2)}, u32[]{:S(2)}) collective-permute-start(bf16[272,128]{1,0:T(8,128)(2,1)S(1)} %get-tuple-element.18), channel_id=1, source_target_pairs={{0,16},{4,20},{8,24},{12,28},{16,0},{20,4},{24,8},{28,12},{1,17},{... | collective-permute-start | bytes 208904 | tf_op jit(solution)/shard_map/ppermute | solution.py:245
  57.6 7.3 %collective-permute-start.4 = (bf16[272,128]{1,0:T(8,128)(2,1)S(1)}, bf16[272,128]{1,0:T(8,128)(2,1)S(1)}, u32[]{:S(2)}, u32[]{:S(2)}) collective-permute-start(bf16[272,128]{1,0:T(8,128)(2,1)S(1)} %get-tuple-element.19), channel_id=1, source_target_pairs={{0,8},{4,12},{8,0},{12,4},{16,24},{20,28},{24,16},{28,20},{1,9},{5... | collective-permute-start | bytes 208904 | tf_op jit(solution)/shard_map/ppermute | solution.py:245
  64.9 0.6 copy-start.9
  64.9 0.7 copy-start.10
  64.9 0.7 copy-start.11
  68.0 6.0 %collective-permute-start.9 = (bf16[8,8192]{1,0:T(8,128)(2,1)}, bf16[8,8192]{1,0:T(8,128)(2,1)S(1)}, u32[]{:S(2)}, u32[]{:S(2)}) collective-permute-start(bf16[8,8192]{1,0:T(8,128)(2,1)} %get-tuple-element.11.refs_0_), channel_id=1, source_target_pairs={{0,3},{1,2},{2,1},{3,0},{4,7},{5,6},{6,5},{7,4},{8,11},{9,10},{10,... | collective-permute-start | bytes 393224 | tf_op jit(solution)/shard_map/ppermute | solution.py:245
  68.0 6.8 %collective-permute-start.8 = (bf16[8,8192]{1,0:T(8,128)(2,1)}, bf16[8,8192]{1,0:T(8,128)(2,1)S(1)}, u32[]{:S(2)}, u32[]{:S(2)}) collective-permute-start(bf16[8,8192]{1,0:T(8,128)(2,1)} %get-tuple-element.11.refs_0_), channel_id=1, source_target_pairs={{0,2},{1,3},{2,0},{3,1},{4,6},{5,7},{6,4},{7,5},{8,10},{9,11},{10,... | collective-permute-start | bytes 393224 | tf_op jit(solution)/shard_map/ppermute | solution.py:245
  68.4 6.4 %collective-permute-start.7 = (bf16[8,8192]{1,0:T(8,128)(2,1)}, bf16[8,8192]{1,0:T(8,128)(2,1)S(1)}, u32[]{:S(2)}, u32[]{:S(2)}) collective-permute-start(bf16[8,8192]{1,0:T(8,128)(2,1)} %get-tuple-element.11.refs_0_), channel_id=1, source_target_pairs={{0,1},{1,0},{2,3},{3,2},{4,5},{5,4},{6,7},{7,6},{8,9},{9,8},{10,11... | collective-permute-start | bytes 393224 | tf_op jit(solution)/shard_map/ppermute | solution.py:245
  74.0 0.8 %copy-start.6 = (bf16[8,8192]{1,0:T(8,128)(2,1)}, bf16[8,8192]{1,0:T(8,128)(2,1)S(1)}, u32[]{:S(2)}) copy-start(bf16[8,8192]{1,0:T(8,128)(2,1)S(1)} %collective-permute-done.9.refs_3_) | copy-start | bytes 393220
  74.8 0.7 copy-start.7
  74.8 0.7 copy-start.8

commit v2 on v1

--- a/solution.py
+++ b/solution.py
@@ -19,9 +19,11 @@
 SLAB = PIX + 2 * REACH
 TILE = 8
 PACK = 16
+ROWS = BAND + PACK
 DIGITS = 4
 CHUNK = 32
-UNROLL = 8
+RING = 6
+UNROLL = 32
 MIB = 1 << 20
 
 
@@ -34,18 +36,25 @@
     return table.astype(np.float32).astype(ml_dtypes.bfloat16)
 
 
-def column_table(pairs):
+def column_table():
     table = basis()
-    out = np.zeros((2 * PIX, 2 * PIX), ml_dtypes.bfloat16)
+    out = np.zeros((2 * PIX, PIX), ml_dtypes.bfloat16)
     for side in range(2):
-        rows = slice(side * PIX, (side + 1) * PIX)
-        out[rows, side * BAND : (side + 1) * BAND] = table[:, :BAND]
-        out[rows, PIX + side * pairs] = table[:, BAND]
+        out[side * PIX : (side + 1) * PIX, side * BAND : (side + 1) * BAND] = table[:, :BAND]
     return out
 
 
+def last_table(pairs):
+    table = basis()
+    out = np.zeros((pairs, PACK, 2 * PIX), ml_dtypes.bfloat16)
+    for j in range(pairs):
+        for side in range(2):
+            out[j, j + side * pairs, side * PIX : (side + 1) * PIX] = table[:, BAND]
+    return out
+
+
 def row_table():
-    out = np.zeros((5 * PACK, PIX), ml_dtypes.bfloat16)
+    out = np.zeros((ROWS, PIX), ml_dtypes.bfloat16)
     out[: BAND + 1] = basis().T
     return out
 
@@ -68,31 +77,38 @@
     return np.exp(-radius / (BAND * BAND / 2.0)).reshape(BAND // 2, 2 * BAND).astype(np.float32)
 
 
-def owner_of(me, near, far, other, groups):
-    dp, grp = me[0], me[1]
+def owner_of(near, far, other, groups):
+    dp, grp = lax.axis_index("dp"), lax.axis_index("grp")
     there_dp = dp ^ ((far << 1) | (near & 1))
     there_grp = grp ^ (((near >> 1) << 1) | other)
     return there_dp * groups + there_grp
 
 
 def sums_kernel(
-    me, ids, shifts, ids_rows, images, col, row, send, keep, held, acc, sems, *, groups, own
+    class_ids, pixel_shifts, images, acc, held, ids, shifts, sems, small_sem
 ):
-    count = images.shape[0]
-    chunks = count // CHUNK
-    pairs = own // 2
-    nears, fars = send.shape[0], send.shape[1]
+    chunks = images.shape[0] // CHUNK
 
     def fetch(k):
         span = pl.ds(pl.multiple_of(k * CHUNK, CHUNK), CHUNK)
-        return pltpu.make_async_copy(images.at[span], held.at[span], sems.at[k])
-
-    for k in range(chunks):
+        slot = lax.rem(k, RING)
+        return pltpu.make_async_copy(images.at[span], held.at[slot], sems.at[slot])
+
+    small = [
+        pltpu.make_async_copy(class_ids, ids, small_sem.at[0]),
+        pltpu.make_async_copy(pixel_shifts, shifts, small_sem.at[1]),
+    ]
+    for copy in small:
+        copy.start()
+    for k in range(min(RING, chunks)):
         fetch(k).start()
     acc[...] = jnp.zeros_like(acc)
+    for copy in small:
+        copy.wait()
 
     def add_chunk(k, _):
         fetch(k).wait()
+        slot = lax.rem(k, RING)
 
         def add_some(s, _):
             for u in range(UNROLL):
@@ -100,17 +116,39 @@
                 dx = shifts[0, i]
                 at = ids[i] * SLAB + REACH + shifts[1, i]
                 turned = pltpu.roll(
-                    held[i].astype(jnp.float32), jnp.where(dx < 0, dx + PIX, dx), 1
+                    held[slot, s * UNROLL + u].astype(jnp.float32), jnp.where(dx < 0, dx + PIX, dx), 1
                 )
                 acc[pl.ds(at, PIX), :] = acc[pl.ds(at, PIX), :] + turned
             return 0
 
-        return lax.fori_loop(0, CHUNK // UNROLL, add_some, 0)
+        lax.fori_loop(0, CHUNK // UNROLL, add_some, 0)
+
+        @pl.when(k + RING < chunks)
+        def _():
+            fetch(k + RING).start()
+
+        return 0
 
     lax.fori_loop(0, chunks, add_chunk, 0)
 
-    lane = lax.broadcasted_iota(jnp.int32, (TILE, PIX), 1)
+
+def transform_kernel(
+    _, acc, ids_rows, col, row, last, block, out, fresh, edges, sems, *, near, other, groups, own
+):
+    pairs = own // 2
+    fars = out.shape[0]
+    together = 2 if fars % 2 == 0 else 1
+    lane = lax.broadcasted_iota(jnp.int32, (TILE, ROWS), 1)
     sub = lax.broadcasted_iota(jnp.int32, (TILE, PIX), 0)
+    edges[...] = jnp.zeros_like(edges)
+    spans = fresh.shape[0]
+
+    def regroup(f):
+        at = ((2 * near + other) * spans + f) * PIX
+        return pltpu.make_async_copy(block.at[:, :, pl.ds(at, PIX)], fresh.at[f], sems.at[f])
+
+    for f in range(spans):
+        regroup(f).start()
 
     def folded(c):
         at = pl.multiple_of(c * SLAB, TILE)
@@ -119,49 +157,46 @@
         tail = acc[pl.ds(at + PIX, REACH), :] + acc[pl.ds(at, REACH), :]
         return jnp.concatenate([head, mid, tail], axis=0).astype(jnp.bfloat16)
 
-    def transform(owner, out):
-        stacked = jnp.concatenate(
-            [
-                jnp.concatenate([folded(owner * own + j), folded(owner * own + j + pairs)], axis=1)
-                for j in range(pairs)
-            ],
-            axis=0,
+    def transform(far, edge):
+        owner = owner_of(near, far, other, groups)
+        section = []
+        ends = jnp.zeros((PACK, ROWS), jnp.float32)
+        for j in range(pairs):
+            both = jnp.concatenate(
+                [folded(owner * own + j), folded(owner * own + j + pairs)], axis=1
+            )
+            part = jnp.dot(row[...], both, preferred_element_type=jnp.float32).astype(jnp.bfloat16)
+            ends += lax.dot_general(
+                last[j], part, (((1,), (1,)), ((), ())), preferred_element_type=jnp.float32
+            )
+            section.append(part)
+        full = jnp.dot(
+            jnp.concatenate(section, axis=0), col[...], preferred_element_type=jnp.float32
         )
-        section = jnp.dot(stacked, col[...], preferred_element_type=jnp.float32).astype(
-            jnp.bfloat16
-        )
-        extra = None
-        edge = []
         for j in range(pairs):
-            both = jnp.dot(
-                row[...], section[j * PIX : (j + 1) * PIX], preferred_element_type=jnp.float32
-            )
-            out[j * BAND : (j + 1) * BAND, :] = both[:BAND, :PIX].astype(jnp.bfloat16)
-            edge.append(both[BAND : BAND + 1, :PIX])
-            last = both[:, PIX:]
-            last = pltpu.roll(last, j, 1) if j else last
-            extra = last if extra is None else extra + last
-        extra = jnp.concatenate(
-            [extra, jnp.zeros((PIX - extra.shape[0], PIX), jnp.float32)], axis=0
-        ).T[:TILE]
+            at = j * ROWS
+            out[far, j * BAND : (j + 1) * BAND, :] = full[at : at + BAND].astype(jnp.bfloat16)
+            edge[j : j + 1, :] = full[at + BAND : at + BAND + 1]
         hits = jnp.zeros((TILE, PIX), jnp.float32)
         for r in range(ids_rows.shape[0]):
             hits += (ids_rows[r : r + 1, :] == owner * own + sub).astype(jnp.float32)
         rest = jnp.sum(hits, axis=1, keepdims=True)
+        ends = ends[:TILE]
         for d in range(DIGITS):
             upper = jnp.floor(rest * 0.125) if d < DIGITS - 1 else jnp.zeros_like(rest)
-            extra = jnp.where(lane == BAND + 1 + d, rest - 8.0 * upper, extra)
+            ends = jnp.where(lane == BAND + 1 + d, rest - 8.0 * upper, ends)
             rest = upper
-        edge.append(jnp.zeros((TILE - pairs, PIX), jnp.float32))
-        out[pairs * BAND :, :] = jnp.concatenate([*edge, extra], axis=0).astype(jnp.bfloat16)
-
-    def one(n, _):
-        near, far = n // fars, n % fars
-        transform(owner_of(me, near, far, 1, groups), send.at[near, far])
-        transform(owner_of(me, near, far, 0, groups), keep.at[near, far])
+        edge[TILE:, :ROWS] = ends
+        out[far, pairs * BAND :, :] = edge[...].astype(jnp.bfloat16)
+
+    def some(n, _):
+        for k in range(together):
+            transform(n * together + k, edges.at[k])
         return 0
 
-    lax.fori_loop(0, nears * fars, one, 0)
+    lax.fori_loop(0, fars // together, some, 0)
+    for f in range(spans):
+        regroup(f).wait()
 
 
 def averages_kernel(*refs, own, parts):
@@ -223,16 +258,32 @@
             rounded[:, at : at + PIX] = value.astype(jnp.bfloat16)
 
 
-def scores_kernel(me, *refs, own, groups):
-    pieces, (block, out) = refs[:groups], refs[groups:]
+def scores_kernel(*refs, own, groups):
+    pieces, fresh, (out, sums) = refs[:groups], refs[groups:-2], refs[-2:]
+    each = fresh[0].shape[0]
+    spans = len(fresh) * each
+    classes = own * groups
     held = jnp.concatenate([piece[:own] for piece in pieces], axis=0)
-    inner = lax.dot_general(
-        held, block[...], (((1,), (1,)), ((), ())), preferred_element_type=jnp.float32
+    both = jnp.concatenate([held[:, : spans * PIX], held[:, spans * PIX :]], axis=0)
+    total = None
+    for f in range(0, spans, 2):
+        here = jnp.concatenate([fresh[g // each][g % each] for g in (f, f + 1)], axis=1)
+        term = lax.dot_general(
+            here,
+            both[:, f * PIX : (f + 2) * PIX],
+            (((1,), (1,)), ((), ())),
+            preferred_element_type=jnp.float32,
+        )
+        total = term if total is None else total + term
+    sums[:, : 2 * classes] = total
+    count = out.shape[1]
+    inner = sums[pl.ds(0, count, stride=2), :] + pltpu.roll(
+        sums[pl.ds(1, count, stride=2), :], PIX - classes, 1
     )
     energy = jnp.sum(jnp.square(held.astype(jnp.float32)), axis=1, keepdims=True)
-    result = (inner - 0.5 * energy) / BAND
+    result = (inner.T[:classes] - 0.5 * energy) / BAND
     for k in range(groups):
-        at = (me[1] ^ k) * own
+        at = (lax.axis_index("grp") ^ k) * own
         if own % TILE == 0:
             out[pl.ds(pl.multiple_of(at, TILE), own), :] = result[k * own : (k + 1) * own]
         else:
@@ -261,37 +312,63 @@
     count = images.shape[0]
     nears, fars = groups, dp_count // 2
     block_rows = pairs * BAND + PACK
-    me = jnp.stack([lax.axis_index("dp"), lax.axis_index("grp")]).astype(jnp.int32)
-    smem = pl.BlockSpec(memory_space=pltpu.SMEM)
     vmem = pl.BlockSpec(memory_space=pltpu.VMEM)
-    hbm = pl.BlockSpec(memory_space=pl.ANY)
-    partial = jax.ShapeDtypeStruct((nears, fars, block_rows, PIX), jnp.bfloat16)
-    send, keep = pl.pallas_call(
-        functools.partial(sums_kernel, groups=groups, own=own),
-        out_shape=(partial, partial),
-        in_specs=[smem, smem, smem, vmem, hbm, vmem, vmem],
-        out_specs=(vmem, vmem),
+    hbm = pl.BlockSpec(memory_space=pltpu.HBM)
+    anywhere = pl.BlockSpec(memory_space=pl.ANY)
+    flat = BAND * BAND
+    spans = flat // PIX // (2 * nears)
+    fresh_count = next_block.shape[0]
+
+    def put(space, *arrays):
+        return [pltpu.with_memory_space_constraint(a, space) for a in arrays]
+
+    acc = pl.pallas_call(
+        sums_kernel,
+        out_shape=pltpu.VMEM((CLASSES * SLAB, PIX), jnp.float32),
+        in_specs=[hbm] * 3,
+        out_specs=vmem,
         scratch_shapes=[
-            pltpu.VMEM((count, PIX, PIX), jnp.bfloat16),
-            pltpu.VMEM((CLASSES * SLAB, PIX), jnp.float32),
-            pltpu.SemaphoreType.DMA((count // CHUNK,)),
+            pltpu.VMEM((RING, CHUNK, PIX, PIX), jnp.bfloat16),
+            pltpu.SMEM((count,), jnp.int32),
+            pltpu.SMEM((2, count), jnp.int32),
+            pltpu.SemaphoreType.DMA((RING,)),
+            pltpu.SemaphoreType.DMA((2,)),
         ],
-        compiler_params=pltpu.CompilerParams(vmem_limit_bytes=52 * MIB),
-    )(
-        me,
-        class_ids,
-        shifts.T,
-        class_ids.reshape(count // PIX, PIX),
-        images,
-        jnp.asarray(column_table(pairs)),
-        jnp.asarray(row_table()),
-    )
-    got = swap(send, "grp", 1)
-    part = [(keep[q].astype(jnp.float32) + got[q].astype(jnp.float32)).astype(jnp.bfloat16) for q in range(nears)]
-    met = [part[0]] + [hop(part[q], q, groups) for q in range(1, nears)]
+        compiler_params=pltpu.CompilerParams(vmem_limit_bytes=10 * MIB),
+    )(*put(pltpu.HBM, class_ids, shifts.T, images))
+    piece = jax.ShapeDtypeStruct((fars, block_rows, PIX), jnp.bfloat16)
+    ids_rows = class_ids.reshape(count // PIX, PIX)
+    tables = [jnp.asarray(t) for t in (column_table(), row_table(), last_table(pairs))]
+
+    (block,) = put(pltpu.HBM, next_block)
+    (held_acc,) = put(pltpu.VMEM, acc)
+
+    def transform(after, near, other):
+        return pl.pallas_call(
+            functools.partial(transform_kernel, near=near, other=other, groups=groups, own=own),
+            out_shape=(piece, pltpu.VMEM((spans, fresh_count, 2, PIX), jnp.bfloat16)),
+            in_specs=[anywhere] + [vmem] * 5 + [hbm],
+            out_specs=(vmem, vmem),
+            scratch_shapes=[
+                pltpu.VMEM((2, PACK, PIX), jnp.float32),
+                pltpu.SemaphoreType.DMA((spans,)),
+            ],
+            compiler_params=pltpu.CompilerParams(vmem_limit_bytes=8 * MIB),
+            cost_estimate=pl.CostEstimate(flops=10**10, bytes_accessed=MIB, transcendentals=0),
+        )(after, held_acc, ids_rows, *tables, block)
+
+    met = [None] * nears
+    done = ids_rows
+    fresh = [None] * (2 * nears)
+    for near in reversed(range(nears)):
+        send, fresh[2 * near + 1] = transform(done, near, 1)
+        got = swap(send, "grp", 1)
+        keep, fresh[2 * near] = transform(send, near, 0)
+        part = (keep.astype(jnp.float32) + got.astype(jnp.float32)).astype(jnp.bfloat16)
+        met[near] = hop(part, near, groups) if near else part
+        done = part
     chip_sum = sum(m.astype(jnp.float32) for m in met).astype(jnp.bfloat16)
     pieces = [chip_sum[0]] + [swap(chip_sum[r], "dp", r << 1) for r in range(1, fars)]
-    flat = BAND * BAND
     real, imag, rounded = pl.pallas_call(
         functools.partial(averages_kernel, own=own, parts=fars),
         out_shape=(
@@ -305,16 +382,19 @@
             pltpu.VMEM((TILE * BAND, PIX), jnp.float32),
             pltpu.VMEM(((BAND + 1) * TILE, PIX), jnp.float32),
         ],
-    )(*pieces, jnp.asarray(expand_table()), jnp.asarray(filter_table()))
+        compiler_params=pltpu.CompilerParams(vmem_limit_bytes=8 * MIB),
+    )(*put(pltpu.VMEM, *pieces), jnp.asarray(expand_table()), jnp.asarray(filter_table()))
     averages = jnp.stack([real[:own], imag[:own]], axis=1)
     held = [rounded] + [swap(rounded, "grp", k) for k in range(1, groups)]
-    fresh = next_block.reshape(next_block.shape[0], 2 * flat)
+    fresh = [f.reshape(spans, 2 * fresh_count, PIX) for f in fresh]
     scores = pl.pallas_call(
         functools.partial(scores_kernel, own=own, groups=groups),
-        out_shape=jax.ShapeDtypeStruct((own * groups, fresh.shape[0]), jnp.float32),
-        in_specs=[smem] + [vmem] * (groups + 1),
+        out_shape=jax.ShapeDtypeStruct((own * groups, fresh_count), jnp.float32),
+        in_specs=[vmem] * (groups + len(fresh)),
         out_specs=vmem,
-    )(me, *held, fresh)
+        scratch_shapes=[pltpu.VMEM((2 * fresh_count, PIX), jnp.float32)],
+        compiler_params=pltpu.CompilerParams(vmem_limit_bytes=16 * MIB),
+    )(*put(pltpu.VMEM, *held, *fresh))
     return averages, scores
 
 

time: 80.6 us -> 52 us (0.65)
  Pallas kernels: 32.5 us -> 21 us
  local copies, waits for them, and re-layouts: 12.4 us -> 0.97 us
  other arithmetic: 3.7 us -> 0.44 us
  waiting for transfers between devices: 19.5 us -> 16.6 us
    unnamed x26 -> x13, local copies, waits for them, and re-layouts: 11.7 us -> 0.94 us
    ppermute x3, waiting for transfers between devices: 14.1 us -> 5.65 us  [hop(): lax.ppermute(array, ('dp', 'grp'), [(i, i ^ ((near & 1) * groups | (near...]
    pallas_call x1 -> x9, Pallas kernels: 25.6 us -> 18.3 us  [the longest x8 11.1 us: transform(): pl.pallas_call(functools.partial(transform_kernel, near=near, other=other...]
    ppermute x7 -> x10, waiting for transfers between devices: 5.41 us -> 11 us  [swap(): return lax.ppermute(array, axis, [(i, i ^ flip) for i in range(size)])]
    pallas_call x1, Pallas kernels: 4.44 us -> 2.01 us  [body(): pl.pallas_call(functools.partial(scores_kernel, own=own, groups=groups),...]
    pallas_call x1, Pallas kernels: 2.47 us -> 0.69 us  [body(): pl.pallas_call(functools.partial(averages_kernel, own=own, parts=fars), o...]
    convert_element_type x1 -> x3, other arithmetic: 1.49 us -> 0.23 us  [body(): (keep.astype(jnp.float32) + got.astype(jnp.float32)).astype(jnp.bfloat16)]
    another operation x1, other arithmetic: 0.99 us -> 0.02 us  [body(): averages = jnp.stack([real[:own], imag[:own]], axis=1)]
  transfers between devices with their start and end apart: 10 -> 13, of which waited for: 6 -> 9; matrix products, arithmetic and copies ran while one was open for 10% -> 2% of each run, Pallas kernels for 0% -> 19%
where the time goes in v2:
time: 52 us; the launch traced here: 51.8 us
  Pallas kernels  21 us (40%)
  waiting for transfers between devices  16.6 us (32%)
  starting transfers between devices  11.9 us (23%)
  local copies, waits for them, and re-layouts  0.97 us (2%)
  between operations  0.85 us (2%)
    pallas_call x8, Pallas kernels, transform(): pl.pallas_call(functools.partial(transform_kernel, near=near, other=other...  11.1 us
    ppermute x10, waiting for transfers between devices, swap(): return lax.ppermute(array, axis, [(i, i ^ flip) for i in range(size)])  11 us
    ppermute x10, starting transfers between devices, swap(): return lax.ppermute(array, axis, [(i, i ^ flip) for i in range(size)])  7.34 us
    pallas_call x1, Pallas kernels, body(): pl.pallas_call(sums_kernel, out_shape=pltpu.VMEM((CLASSES * SLAB, PIX), j...  7.27 us
    ppermute x3, waiting for transfers between devices, hop(): lax.ppermute(array, ('dp', 'grp'), [(i, i ^ ((near & 1) * groups | (near...  5.65 us
    ppermute x3, starting transfers between devices, hop(): lax.ppermute(array, ('dp', 'grp'), [(i, i ^ ((near & 1) * groups | (near...  4.59 us
    pallas_call x1, Pallas kernels, body(): pl.pallas_call(functools.partial(scores_kernel, own=own, groups=groups),...  2.01 us
  transfers between devices with their start and end apart: 13, of which 9 were waited for; matrix products, arithmetic and copies ran while one was open for 2% of the time, Pallas kernels for 19%

profile of v2, /device:TPU:0, one launch (start us, length us, event | category | flops | bytes accessed | tf_op | source)
XLA Modules:
  0.0 51.8 jit_solution(9201374110932526930)
XLA Ops:
  0.7 7.3 %shard_map.104.acc = f32[40960,128]{1,0:T(8,128)S(1)} custom-call(s32[512]{0:T(512)} %class_ids.1, s32[2,512]{1,0:T(2,128)} %bitcast.39, bf16[512,128,128]{2,1,0:T(8,128)(2,1)} %images.1), custom_call_target="tpu_custom_call" | custom-call | tf_op jit(solution)/shard_map/pallas_call | solution.py:325
  8.0 1.4 %shard_map.105 = (bf16[4,272,128]{2,1,0:T(8,128)(2,1)S(1)}, bf16[4,256,2,128]{3,2,1,0:T(2,128)(2,1)S(1)}) custom-call(s32[4,128]{1,0:T(4,128)S(1)} %bitcast.30, f32[40960,128]{1,0:T(8,128)S(1)} %shard_map.104.acc, s32[4,128]{1,0:T(4,128)S(1)} %bitcast.31, bf16[256,128]{1,0:T(8,128)(2,1)S(1)} %copy-done.3, bf16[80,128]{1,0:T(8,128)(2,1)S(1)} %copy-done.5, ...), custom_call_target="tpu_custom_call" | custom-call | flops 10000000000 | bytes 1048576 | tf_op jit(solution)/shard_map/pallas_call | solution.py:347
  9.9 1.4 %shard_map.106 = (bf16[4,272,128]{2,1,0:T(8,128)(2,1)S(1)}, bf16[4,256,2,128]{3,2,1,0:T(2,128)(2,1)S(1)}) custom-call(bf16[4,272,128]{2,1,0:T(8,128)(2,1)S(1)} %get-tuple-element.21._, f32[40960,128]{1,0:T(8,128)S(1)} %shard_map.104.acc, s32[4,128]{1,0:T(4,128)S(1)} %bitcast.32, bf16[256,128]{1,0:T(8,128)(2,1)S(1)} %copy-done.3, ...), custom_call_target="tpu_custom_call" | custom-call | flops 10000000000 | bytes 1048576 | tf_op jit(solution)/shard_map/pallas_call | solution.py:347
  11.4 3.7 %collective-permute-start.6 = (bf16[4,272,128]{2,1,0:T(8,128)(2,1)S(1)}, bf16[4,272,128]{2,1,0:T(8,128)(2,1)S(1)}, u32[]{:S(2)}, u32[]{:S(2)}) collective-permute-start(bf16[4,272,128]{2,1,0:T(8,128)(2,1)S(1)} %add_convert_fusion.4._), channel_id=1, source_target_pairs={{0,6},{1,7},{2,4},{3,5},{4,2},{5,3},{6,0},{7,1},{8,14},{9,15},{10,... | collective-permute-start | bytes 835592 | tf_op jit(solution)/shard_map/ppermute | solution.py:301
  15.1 1.4 %shard_map.107 = (bf16[4,272,128]{2,1,0:T(8,128)(2,1)S(1)}, bf16[4,256,2,128]{3,2,1,0:T(2,128)(2,1)S(1)}) custom-call(bf16[4,272,128]{2,1,0:T(8,128)(2,1)S(1)} %add_convert_fusion.4._, f32[40960,128]{1,0:T(8,128)S(1)} %shard_map.104.acc, s32[4,128]{1,0:T(4,128)S(1)} %bitcast.33, bf16[256,128]{1,0:T(8,128)(2,1)S(1)} %copy-done.3, ...), custom_call_target="tpu_custom_call" | custom-call | flops 10000000000 | bytes 1048576 | tf_op jit(solution)/shard_map/pallas_call | solution.py:347
  16.6 1.4 %shard_map.108 = (bf16[4,272,128]{2,1,0:T(8,128)(2,1)S(1)}, bf16[4,256,2,128]{3,2,1,0:T(2,128)(2,1)S(1)}) custom-call(bf16[4,272,128]{2,1,0:T(8,128)(2,1)S(1)} %get-tuple-element.23._, f32[40960,128]{1,0:T(8,128)S(1)} %shard_map.104.acc, s32[4,128]{1,0:T(4,128)S(1)} %bitcast.34, bf16[256,128]{1,0:T(8,128)(2,1)S(1)} %copy-done.3, ...), custom_call_target="tpu_custom_call" | custom-call | flops 10000000000 | bytes 1048576 | tf_op jit(solution)/shard_map/pallas_call | solution.py:347
  18.2 0.6 %collective-permute-start.5 = (bf16[4,272,128]{2,1,0:T(8,128)(2,1)S(1)}, bf16[4,272,128]{2,1,0:T(8,128)(2,1)S(1)}, u32[]{:S(2)}, u32[]{:S(2)}) collective-permute-start(bf16[4,272,128]{2,1,0:T(8,128)(2,1)S(1)} %add_convert_fusion.3._), channel_id=1, source_target_pairs={{0,2},{1,3},{2,0},{3,1},{4,6},{5,7},{6,4},{7,5},{8,10},{9,11},{10,... | collective-permute-start | bytes 835592 | tf_op jit(solution)/shard_map/ppermute | solution.py:301
  18.7 1.4 %shard_map.109 = (bf16[4,272,128]{2,1,0:T(8,128)(2,1)S(1)}, bf16[4,256,2,128]{3,2,1,0:T(2,128)(2,1)S(1)}) custom-call(bf16[4,272,128]{2,1,0:T(8,128)(2,1)S(1)} %add_convert_fusion.3._, f32[40960,128]{1,0:T(8,128)S(1)} %shard_map.104.acc, s32[4,128]{1,0:T(4,128)S(1)} %bitcast.35, bf16[256,128]{1,0:T(8,128)(2,1)S(1)} %copy-done.3, ...), custom_call_target="tpu_custom_call" | custom-call | flops 10000000000 | bytes 1048576 | tf_op jit(solution)/shard_map/pallas_call | solution.py:347
  20.3 1.4 %shard_map.110 = (bf16[4,272,128]{2,1,0:T(8,128)(2,1)S(1)}, bf16[4,256,2,128]{3,2,1,0:T(2,128)(2,1)S(1)}) custom-call(bf16[4,272,128]{2,1,0:T(8,128)(2,1)S(1)} %get-tuple-element.25._, f32[40960,128]{1,0:T(8,128)S(1)} %shard_map.104.acc, s32[4,128]{1,0:T(4,128)S(1)} %bitcast.36, bf16[256,128]{1,0:T(8,128)(2,1)S(1)} %copy-done.3, ...), custom_call_target="tpu_custom_call" | custom-call | flops 10000000000 | bytes 1048576 | tf_op jit(solution)/shard_map/pallas_call | solution.py:347
  22.2 1.4 %shard_map.111 = (bf16[4,272,128]{2,1,0:T(8,128)(2,1)S(1)}, bf16[4,256,2,128]{3,2,1,0:T(2,128)(2,1)S(1)}) custom-call(bf16[4,272,128]{2,1,0:T(8,128)(2,1)S(1)} %add_convert_fusion.2._, f32[40960,128]{1,0:T(8,128)S(1)} %shard_map.104.acc, s32[4,128]{1,0:T(4,128)S(1)} %bitcast.37, bf16[256,128]{1,0:T(8,128)(2,1)S(1)} %copy-done.3, ...), custom_call_target="tpu_custom_call" | custom-call | flops 10000000000 | bytes 1048576 | tf_op jit(solution)/shard_map/pallas_call | solution.py:347
  23.8 1.4 %shard_map.112 = (bf16[4,272,128]{2,1,0:T(8,128)(2,1)S(1)}, bf16[4,256,2,128]{3,2,1,0:T(2,128)(2,1)S(1)}) custom-call(bf16[4,272,128]{2,1,0:T(8,128)(2,1)S(1)} %get-tuple-element.27._, f32[40960,128]{1,0:T(8,128)S(1)} %shard_map.104.acc, s32[4,128]{1,0:T(4,128)S(1)} %bitcast.38, bf16[256,128]{1,0:T(8,128)(2,1)S(1)} %copy-done.3, ...), custom_call_target="tpu_custom_call" | custom-call | flops 10000000000 | bytes 1048576 | tf_op jit(solution)/shard_map/pallas_call | solution.py:347
  25.2 3.0 %collective-permute-done.5 = bf16[4,272,128]{2,1,0:T(8,128)(2,1)S(1)} collective-permute-done((bf16[4,272,128]{2,1,0:T(8,128)(2,1)S(1)}, bf16[4,272,128]{2,1,0:T(8,128)(2,1)S(1)}, u32[]{:S(2)}, u32[]{:S(2)}) %collective-permute-start.5) | collective-permute-done | bytes 278560 | tf_op jit(solution)/shard_map/ppermute | solution.py:301
  28.2 2.6 %collective-permute-done.4 = bf16[4,272,128]{2,1,0:T(8,128)(2,1)S(1)} collective-permute-done((bf16[4,272,128]{2,1,0:T(8,128)(2,1)S(1)}, bf16[4,272,128]{2,1,0:T(8,128)(2,1)S(1)}, u32[]{:S(2)}, u32[]{:S(2)}) %collective-permute-start.4) | collective-permute-done | bytes 278560 | tf_op jit(solution)/shard_map/ppermute | solution.py:301
  31.0 3.7 %collective-permute-start.9 = (bf16[272,128]{1,0:T(8,128)(2,1)S(1)}, bf16[272,128]{1,0:T(8,128)(2,1)S(1)}, u32[]{:S(2)}, u32[]{:S(2)}) collective-permute-start(bf16[272,128]{1,0:T(8,128)(2,1)S(1)} %get-tuple-element.42), channel_id=1, source_target_pairs={{0,24},{4,28},{8,16},{12,20},{16,8},{20,12},{24,0},{28,4},{1,25},{... | collective-permute-start | bytes 208904 | tf_op jit(solution)/shard_map/ppermute | solution.py:296
  34.7 0.8 %collective-permute-start.7 = (bf16[272,128]{1,0:T(8,128)(2,1)S(1)}, bf16[272,128]{1,0:T(8,128)(2,1)S(1)}, u32[]{:S(2)}, u32[]{:S(2)}) collective-permute-start(bf16[272,128]{1,0:T(8,128)(2,1)S(1)} %get-tuple-element.44), channel_id=1, source_target_pairs={{0,8},{4,12},{8,0},{12,4},{16,24},{20,28},{24,16},{28,20},{1,9},{5... | collective-permute-start | bytes 208904 | tf_op jit(solution)/shard_map/ppermute | solution.py:296
  35.5 2.6 %collective-permute-done.9.refs_3_ = bf16[272,128]{1,0:T(8,128)(2,1)S(1)} collective-permute-done((bf16[272,128]{1,0:T(8,128)(2,1)S(1)}, bf16[272,128]{1,0:T(8,128)(2,1)S(1)}, u32[]{:S(2)}, u32[]{:S(2)}) %collective-permute-start.9) | collective-permute-done | bytes 69664 | tf_op jit(solution)/shard_map/ppermute | solution.py:296
  38.0 2.3 %collective-permute-done.8.refs_2_ = bf16[272,128]{1,0:T(8,128)(2,1)S(1)} collective-permute-done((bf16[272,128]{1,0:T(8,128)(2,1)S(1)}, bf16[272,128]{1,0:T(8,128)(2,1)S(1)}, u32[]{:S(2)}, u32[]{:S(2)}) %collective-permute-start.8) | collective-permute-done | bytes 69664 | tf_op jit(solution)/shard_map/ppermute | solution.py:296
  40.4 0.7 %shard_map.113 = (f32[8,4096]{1,0:T(8,128)S(1)}, f32[8,4096]{1,0:T(8,128)S(1)}, bf16[8,8192]{1,0:T(8,128)(2,1)S(1)}) custom-call(bf16[272,128]{1,0:T(8,128)(2,1)S(1)} %get-tuple-element.45.refs_0_, bf16[272,128]{1,0:T(8,128)(2,1)S(1)} %collective-permute-done.7.refs_1_, bf16[272,128]{1,0:T(8,128)(2,1)S(1)} %collective-permute-done.8.refs_2_, ...), custom_call_target="tpu_custom_call" | custom-call | tf_op jit(solution)/shard_map/pallas_call | solution.py:372
  41.1 0.8 %collective-permute-start.12 = (bf16[8,8192]{1,0:T(8,128)(2,1)S(1)}, bf16[8,8192]{1,0:T(8,128)(2,1)S(1)}, u32[]{:S(2)}, u32[]{:S(2)}) collective-permute-start(bf16[8,8192]{1,0:T(8,128)(2,1)S(1)} %get-tuple-element.31.refs_0_), channel_id=1, source_target_pairs={{0,3},{1,2},{2,1},{3,0},{4,7},{5,6},{6,5},{7,4},{8,11},{9,10},{10,... | collective-permute-start | bytes 393224 | tf_op jit(solution)/shard_map/ppermute | solution.py:296
  41.9 0.9 %collective-permute-start.11 = (bf16[8,8192]{1,0:T(8,128)(2,1)S(1)}, bf16[8,8192]{1,0:T(8,128)(2,1)S(1)}, u32[]{:S(2)}, u32[]{:S(2)}) collective-permute-start(bf16[8,8192]{1,0:T(8,128)(2,1)S(1)} %get-tuple-element.31.refs_0_), channel_id=1, source_target_pairs={{0,2},{1,3},{2,0},{3,1},{4,6},{5,7},{6,4},{7,5},{8,10},{9,11},{10,... | collective-permute-start | bytes 393224 | tf_op jit(solution)/shard_map/ppermute | solution.py:296
  43.1 0.9 %copy.11 = f32[8,2,4096]{2,1,0:T(2,128)} copy(f32[8,2,4096]{2,0,1:T(8,128)S(1)} %pad_maximum_fusion) | data formatting | bytes 524288
  44.0 2.9 %collective-permute-done.12.refs_3_ = bf16[8,8192]{1,0:T(8,128)(2,1)S(1)} collective-permute-done((bf16[8,8192]{1,0:T(8,128)(2,1)S(1)}, bf16[8,8192]{1,0:T(8,128)(2,1)S(1)}, u32[]{:S(2)}, u32[]{:S(2)}) %collective-permute-start.12) | collective-permute-done | bytes 131104 | tf_op jit(solution)/shard_map/ppermute | solution.py:296
  46.9 2.9 %collective-permute-done.11.refs_2_ = bf16[8,8192]{1,0:T(8,128)(2,1)S(1)} collective-permute-done((bf16[8,8192]{1,0:T(8,128)(2,1)S(1)}, bf16[8,8192]{1,0:T(8,128)(2,1)S(1)}, u32[]{:S(2)}, u32[]{:S(2)}) %collective-permute-start.11) | collective-permute-done | bytes 131104 | tf_op jit(solution)/shard_map/ppermute | solution.py:296
  49.8 2.0 %shard_map.114 = f32[32,256]{1,0:T(8,128)} custom-call(bf16[8,8192]{1,0:T(8,128)(2,1)S(1)} %get-tuple-element.31.refs_0_, bf16[8,8192]{1,0:T(8,128)(2,1)S(1)} %collective-permute-done.10.refs_1_, bf16[8,8192]{1,0:T(8,128)(2,1)S(1)} %collective-permute-done.11.refs_2_, bf16[8,8192]{1,0:T(8,128)(2,1)S(1)} %collective-permute-done.12.refs_3_, ...), custom_call_target="tpu_custom_call" | custom-call | tf_op jit(solution)/shard_map/pallas_call | solution.py:390
  (32 shorter events, 2.3 us)
Async XLA Ops:
  0.6 7.3 %copy-start.2 = (s32[512]{0:T(512)S(1)}, s32[512]{0:T(512)}, u32[]{:S(2)}) copy-start(s32[512]{0:T(512)} %class_ids.1) | copy-start | bytes 6148
  0.6 7.3 %copy-start.3 = (bf16[256,128]{1,0:T(8,128)(2,1)S(1)}, bf16[256,128]{1,0:T(8,128)(2,1)}, u32[]{:S(2)}) copy-start(bf16[256,128]{1,0:T(8,128)(2,1)} %constant.10.clone.col) | copy-start | bytes 196612
  0.7 7.3 %copy-start.4 = (bf16[4,16,256]{2,1,0:T(8,128)(2,1)S(1)}, bf16[4,16,256]{2,1,0:T(8,128)(2,1)}, u32[]{:S(2)}) copy-start(bf16[4,16,256]{2,1,0:T(8,128)(2,1)} %constant.12.clone.last) | copy-start | bytes 98308
  0.7 7.3 %copy-start.5 = (bf16[80,128]{1,0:T(8,128)(2,1)S(1)}, bf16[80,128]{1,0:T(8,128)(2,1)}, u32[]{:S(2)}) copy-start(bf16[80,128]{1,0:T(8,128)(2,1)} %constant.11.clone.row) | copy-start | bytes 61444
  9.4 1.9 %collective-permute-start = (bf16[4,272,128]{2,1,0:T(8,128)(2,1)S(1)}, bf16[4,272,128]{2,1,0:T(8,128)(2,1)S(1)}, u32[]{:S(2)}, u32[]{:S(2)}) collective-permute-start(bf16[4,272,128]{2,1,0:T(8,128)(2,1)S(1)} %get-tuple-element.21._), channel_id=1, source_target_pairs={{0,1},{1,0},{2,3},{3,2},{4,5},{5,4},{6,7},{7,6},{8,9},{9,8},{10,11... | collective-permute-start | bytes 835592 | tf_op jit(solution)/shard_map/ppermute | solution.py:296
  11.4 13.8 %collective-permute-start.6 = (bf16[4,272,128]{2,1,0:T(8,128)(2,1)S(1)}, bf16[4,272,128]{2,1,0:T(8,128)(2,1)S(1)}, u32[]{:S(2)}, u32[]{:S(2)}) collective-permute-start(bf16[4,272,128]{2,1,0:T(8,128)(2,1)S(1)} %add_convert_fusion.4._), channel_id=1, source_target_pairs={{0,6},{1,7},{2,4},{3,5},{4,2},{5,3},{6,0},{7,1},{8,14},{9,15},{10,... | collective-permute-start | bytes 835592 | tf_op jit(solution)/shard_map/ppermute | solution.py:301
  16.5 1.6 %collective-permute-start.1 = (bf16[4,272,128]{2,1,0:T(8,128)(2,1)S(1)}, bf16[4,272,128]{2,1,0:T(8,128)(2,1)S(1)}, u32[]{:S(2)}, u32[]{:S(2)}) collective-permute-start(bf16[4,272,128]{2,1,0:T(8,128)(2,1)S(1)} %get-tuple-element.23._), channel_id=1, source_target_pairs={{0,1},{1,0},{2,3},{3,2},{4,5},{5,4},{6,7},{7,6},{8,9},{9,8},{10,11... | collective-permute-start | bytes 835592 | tf_op jit(solution)/shard_map/ppermute | solution.py:296
  18.2 10.0 %collective-permute-start.5 = (bf16[4,272,128]{2,1,0:T(8,128)(2,1)S(1)}, bf16[4,272,128]{2,1,0:T(8,128)(2,1)S(1)}, u32[]{:S(2)}, u32[]{:S(2)}) collective-permute-start(bf16[4,272,128]{2,1,0:T(8,128)(2,1)S(1)} %add_convert_fusion.3._), channel_id=1, source_target_pairs={{0,2},{1,3},{2,0},{3,1},{4,6},{5,7},{6,4},{7,5},{8,10},{9,11},{10,... | collective-permute-start | bytes 835592 | tf_op jit(solution)/shard_map/ppermute | solution.py:301
  20.1 1.6 %collective-permute-start.2 = (bf16[4,272,128]{2,1,0:T(8,128)(2,1)S(1)}, bf16[4,272,128]{2,1,0:T(8,128)(2,1)S(1)}, u32[]{:S(2)}, u32[]{:S(2)}) collective-permute-start(bf16[4,272,128]{2,1,0:T(8,128)(2,1)S(1)} %get-tuple-element.25._), channel_id=1, source_target_pairs={{0,1},{1,0},{2,3},{3,2},{4,5},{5,4},{6,7},{7,6},{8,9},{9,8},{10,11... | collective-permute-start | bytes 835592 | tf_op jit(solution)/shard_map/ppermute | solution.py:296
  21.8 9.0 %collective-permute-start.4 = (bf16[4,272,128]{2,1,0:T(8,128)(2,1)S(1)}, bf16[4,272,128]{2,1,0:T(8,128)(2,1)S(1)}, u32[]{:S(2)}, u32[]{:S(2)}) collective-permute-start(bf16[4,272,128]{2,1,0:T(8,128)(2,1)S(1)} %add_convert_fusion.2._), channel_id=1, source_target_pairs={{0,4},{1,5},{2,6},{3,7},{4,0},{5,1},{6,2},{7,3},{8,12},{9,13},{10,... | collective-permute-start | bytes 835592 | tf_op jit(solution)/shard_map/ppermute | solution.py:301
  23.6 16.9 %copy-start = (f32[128,256]{1,0:T(8,128)S(1)}, f32[128,256]{1,0:T(8,128)}, u32[]{:S(2)}) copy-start(f32[128,256]{1,0:T(8,128)} %constant.13.clone.refs_4_) | copy-start | bytes 393220
  23.6 16.9 %copy-start.1 = (f32[32,128]{1,0:T(8,128)S(1)}, f32[32,128]{1,0:T(8,128)}, u32[]{:S(2)}) copy-start(f32[32,128]{1,0:T(8,128)} %constant.14.clone.refs_5_) | copy-start | bytes 49156
  23.6 7.2 %collective-permute-start.3 = (bf16[4,272,128]{2,1,0:T(8,128)(2,1)S(1)}, bf16[4,272,128]{2,1,0:T(8,128)(2,1)S(1)}, u32[]{:S(2)}, u32[]{:S(2)}) collective-permute-start(bf16[4,272,128]{2,1,0:T(8,128)(2,1)S(1)} %get-tuple-element.27._), channel_id=1, source_target_pairs={{0,1},{1,0},{2,3},{3,2},{4,5},{5,4},{6,7},{7,6},{8,9},{9,8},{10,11... | collective-permute-start | bytes 835592 | tf_op jit(solution)/shard_map/ppermute | solution.py:296
  31.0 7.0 %collective-permute-start.9 = (bf16[272,128]{1,0:T(8,128)(2,1)S(1)}, bf16[272,128]{1,0:T(8,128)(2,1)S(1)}, u32[]{:S(2)}, u32[]{:S(2)}) collective-permute-start(bf16[272,128]{1,0:T(8,128)(2,1)S(1)} %get-tuple-element.42), channel_id=1, source_target_pairs={{0,24},{4,28},{8,16},{12,20},{16,8},{20,12},{24,0},{28,4},{1,25},{... | collective-permute-start | bytes 208904 | tf_op jit(solution)/shard_map/ppermute | solution.py:296
  34.7 5.7 %collective-permute-start.8 = (bf16[272,128]{1,0:T(8,128)(2,1)S(1)}, bf16[272,128]{1,0:T(8,128)(2,1)S(1)}, u32[]{:S(2)}, u32[]{:S(2)}) collective-permute-start(bf16[272,128]{1,0:T(8,128)(2,1)S(1)} %get-tuple-element.43), channel_id=1, source_target_pairs={{0,16},{4,20},{8,24},{12,28},{16,0},{20,4},{24,8},{28,12},{1,17},{... | collective-permute-start | bytes 208904 | tf_op jit(solution)/shard_map/ppermute | solution.py:296
  34.7 5.7 %collective-permute-start.7 = (bf16[272,128]{1,0:T(8,128)(2,1)S(1)}, bf16[272,128]{1,0:T(8,128)(2,1)S(1)}, u32[]{:S(2)}, u32[]{:S(2)}) collective-permute-start(bf16[272,128]{1,0:T(8,128)(2,1)S(1)} %get-tuple-element.44), channel_id=1, source_target_pairs={{0,8},{4,12},{8,0},{12,4},{16,24},{20,28},{24,16},{28,20},{1,9},{5... | collective-permute-start | bytes 208904 | tf_op jit(solution)/shard_map/ppermute | solution.py:296
  41.1 5.8 %collective-permute-start.12 = (bf16[8,8192]{1,0:T(8,128)(2,1)S(1)}, bf16[8,8192]{1,0:T(8,128)(2,1)S(1)}, u32[]{:S(2)}, u32[]{:S(2)}) collective-permute-start(bf16[8,8192]{1,0:T(8,128)(2,1)S(1)} %get-tuple-element.31.refs_0_), channel_id=1, source_target_pairs={{0,3},{1,2},{2,1},{3,0},{4,7},{5,6},{6,5},{7,4},{8,11},{9,10},{10,... | collective-permute-start | bytes 393224 | tf_op jit(solution)/shard_map/ppermute | solution.py:296
  41.9 7.9 %collective-permute-start.11 = (bf16[8,8192]{1,0:T(8,128)(2,1)S(1)}, bf16[8,8192]{1,0:T(8,128)(2,1)S(1)}, u32[]{:S(2)}, u32[]{:S(2)}) collective-permute-start(bf16[8,8192]{1,0:T(8,128)(2,1)S(1)} %get-tuple-element.31.refs_0_), channel_id=1, source_target_pairs={{0,2},{1,3},{2,0},{3,1},{4,6},{5,7},{6,4},{7,5},{8,10},{9,11},{10,... | collective-permute-start | bytes 393224 | tf_op jit(solution)/shard_map/ppermute | solution.py:296
  42.8 7.0 %collective-permute-start.10 = (bf16[8,8192]{1,0:T(8,128)(2,1)S(1)}, bf16[8,8192]{1,0:T(8,128)(2,1)S(1)}, u32[]{:S(2)}, u32[]{:S(2)}) collective-permute-start(bf16[8,8192]{1,0:T(8,128)(2,1)S(1)} %get-tuple-element.31.refs_0_), channel_id=1, source_target_pairs={{0,1},{1,0},{2,3},{3,2},{4,5},{5,4},{6,7},{7,6},{8,9},{9,8},{10,11... | collective-permute-start | bytes 393224 | tf_op jit(solution)/shard_map/ppermute | solution.py:296

commit v3 on v2

--- a/solution.py
+++ b/solution.py
@@ -46,11 +46,11 @@
 
 def last_table(pairs):
     table = basis()
-    out = np.zeros((pairs, PACK, 2 * PIX), ml_dtypes.bfloat16)
+    out = np.zeros((PACK, pairs, 2 * PIX), ml_dtypes.bfloat16)
     for j in range(pairs):
         for side in range(2):
-            out[j, j + side * pairs, side * PIX : (side + 1) * PIX] = table[:, BAND]
-    return out
+            out[j + side * pairs, j, side * PIX : (side + 1) * PIX] = table[:, BAND]
+    return out.reshape(PACK, -1)
 
 
 def row_table():
@@ -133,18 +133,19 @@
 
 
 def transform_kernel(
-    _, acc, ids_rows, col, row, last, block, out, fresh, edges, sems, *, near, other, groups, own
+    _, acc, ids_rows, col, row, last, block, out, fresh, edges, sems, *, jobs, step, other, groups, own
 ):
     pairs = own // 2
-    fars = out.shape[0]
-    together = 2 if fars % 2 == 0 else 1
+    count = out.shape[0]
+    half = count // len(jobs)
+    together = 2 if count % 2 == 0 else 1
     lane = lax.broadcasted_iota(jnp.int32, (TILE, ROWS), 1)
     sub = lax.broadcasted_iota(jnp.int32, (TILE, PIX), 0)
     edges[...] = jnp.zeros_like(edges)
     spans = fresh.shape[0]
 
     def regroup(f):
-        at = ((2 * near + other) * spans + f) * PIX
+        at = (step * spans + f) * PIX
         return pltpu.make_async_copy(block.at[:, :, pl.ds(at, PIX)], fresh.at[f], sems.at[f])
 
     for f in range(spans):
@@ -158,20 +159,25 @@
         return jnp.concatenate([head, mid, tail], axis=0).astype(jnp.bfloat16)
 
     def transform(far, edge):
-        owner = owner_of(near, far, other, groups)
-        section = []
-        ends = jnp.zeros((PACK, ROWS), jnp.float32)
-        for j in range(pairs):
-            both = jnp.concatenate(
-                [folded(owner * own + j), folded(owner * own + j + pairs)], axis=1
-            )
-            part = jnp.dot(row[...], both, preferred_element_type=jnp.float32).astype(jnp.bfloat16)
-            ends += lax.dot_general(
-                last[j], part, (((1,), (1,)), ((), ())), preferred_element_type=jnp.float32
-            )
-            section.append(part)
+        near, first = jobs[-1]
+        which = lax.div(far, half)
+        for k, job in enumerate(jobs[:-1]):
+            near = jnp.where(which == k, job[0], near)
+            first = jnp.where(which == k, job[1], first)
+        owner = owner_of(near, first + lax.rem(far, half), other, groups)
+        wide = jnp.concatenate(
+            [folded(owner * own + j + side * pairs) for j in range(pairs) for side in range(2)], axis=1
+        )
+        part = jnp.dot(row[...], wide, preferred_element_type=jnp.float32).astype(jnp.bfloat16)
+        ends = lax.dot_general(
+            last[...], part, (((1,), (1,)), ((), ())), preferred_element_type=jnp.float32
+        )
         full = jnp.dot(
-            jnp.concatenate(section, axis=0), col[...], preferred_element_type=jnp.float32
+            jnp.concatenate(
+                [part[:, 2 * PIX * j : 2 * PIX * (j + 1)] for j in range(pairs)], axis=0
+            ),
+            col[...],
+            preferred_element_type=jnp.float32,
         )
         for j in range(pairs):
             at = j * ROWS
@@ -194,9 +200,17 @@
             transform(n * together + k, edges.at[k])
         return 0
 
-    lax.fori_loop(0, fars // together, some, 0)
+    lax.fori_loop(0, count // together, some, 0)
     for f in range(spans):
         regroup(f).wait()
+
+
+def totals_kernel(_, *refs, parts):
+    for r, out in enumerate(refs[parts:]):
+        total = refs[0][r].astype(jnp.float32)
+        for ref in refs[1:parts]:
+            total += ref[r].astype(jnp.float32)
+        out[...] = total.astype(jnp.bfloat16)
 
 
 def averages_kernel(*refs, own, parts):
@@ -336,16 +350,21 @@
         ],
         compiler_params=pltpu.CompilerParams(vmem_limit_bytes=10 * MIB),
     )(*put(pltpu.HBM, class_ids, shifts.T, images))
-    piece = jax.ShapeDtypeStruct((fars, block_rows, PIX), jnp.bfloat16)
+    half = fars // 2
+    piece = jax.ShapeDtypeStruct((2 * half, block_rows, PIX), jnp.bfloat16)
     ids_rows = class_ids.reshape(count // PIX, PIX)
     tables = [jnp.asarray(t) for t in (column_table(), row_table(), last_table(pairs))]
 
     (block,) = put(pltpu.HBM, next_block)
     (held_acc,) = put(pltpu.VMEM, acc)
 
-    def transform(after, near, other):
-        return pl.pallas_call(
-            functools.partial(transform_kernel, near=near, other=other, groups=groups, own=own),
+    fresh = []
+
+    def transform(after, jobs, other):
+        out, block_part = pl.pallas_call(
+            functools.partial(
+                transform_kernel, jobs=jobs, step=len(fresh), other=other, groups=groups, own=own
+            ),
             out_shape=(piece, pltpu.VMEM((spans, fresh_count, 2, PIX), jnp.bfloat16)),
             in_specs=[anywhere] + [vmem] * 5 + [hbm],
             out_specs=(vmem, vmem),
@@ -356,19 +375,36 @@
             compiler_params=pltpu.CompilerParams(vmem_limit_bytes=8 * MIB),
             cost_estimate=pl.CostEstimate(flops=10**10, bytes_accessed=MIB, transcendentals=0),
         )(after, held_acc, ids_rows, *tables, block)
-
-    met = [None] * nears
+        fresh.append(block_part)
+        return out
+
+    met = {half: [], 0: []}
     done = ids_rows
-    fresh = [None] * (2 * nears)
-    for near in reversed(range(nears)):
-        send, fresh[2 * near + 1] = transform(done, near, 1)
-        got = swap(send, "grp", 1)
-        keep, fresh[2 * near] = transform(send, near, 0)
-        part = (keep.astype(jnp.float32) + got.astype(jnp.float32)).astype(jnp.bfloat16)
-        met[near] = hop(part, near, groups) if near else part
-        done = part
-    chip_sum = sum(m.astype(jnp.float32) for m in met).astype(jnp.bfloat16)
-    pieces = [chip_sum[0]] + [swap(chip_sum[r], "dp", r << 1) for r in range(1, fars)]
+    for first in (half, 0):
+        for nears_here in ((3, 2), (1, 0)):
+            jobs = tuple((near, first) for near in nears_here)
+            send = transform(done, jobs, 1)
+            got = swap(send, "grp", 1)
+            keep = transform(send, jobs, 0)
+            for k, near in enumerate(nears_here):
+                span = slice(k * half, (k + 1) * half)
+                part = keep[span].astype(jnp.float32) + got[span].astype(jnp.float32)
+                part = part.astype(jnp.bfloat16)
+                met[first].append(hop(part, near, groups) if near else part)
+            done = part
+    pieces = [None] * fars
+    for first in (half, 0):
+        totals = pl.pallas_call(
+            functools.partial(totals_kernel, parts=nears),
+            out_shape=[jax.ShapeDtypeStruct((block_rows, PIX), jnp.bfloat16)] * half,
+            in_specs=[anywhere] + [vmem] * nears,
+            out_specs=[vmem] * half,
+            compiler_params=pltpu.CompilerParams(vmem_limit_bytes=8 * MIB),
+        )(done, *met[first])
+        for r, total in enumerate(totals):
+            far = first + r
+            pieces[far] = swap(total, "dp", far << 1) if far else total
+        done = totals[0]
     real, imag, rounded = pl.pallas_call(
         functools.partial(averages_kernel, own=own, parts=fars),
         out_shape=(
@@ -385,7 +421,10 @@
         compiler_params=pltpu.CompilerParams(vmem_limit_bytes=8 * MIB),
     )(*put(pltpu.VMEM, *pieces), jnp.asarray(expand_table()), jnp.asarray(filter_table()))
     averages = jnp.stack([real[:own], imag[:own]], axis=1)
-    held = [rounded] + [swap(rounded, "grp", k) for k in range(1, groups)]
+    held = [rounded, swap(rounded, "grp", 1)]
+    for k in range(2, groups, 2):
+        across = swap(rounded, "grp", k)
+        held += [across, swap(across, "grp", 1)]
     fresh = [f.reshape(spans, 2 * fresh_count, PIX) for f in fresh]
     scores = pl.pallas_call(
         functools.partial(scores_kernel, own=own, groups=groups),

time: 52 us -> 48.3 us (0.929)
  waiting for transfers between devices: 16.6 us -> 9.46 us
  starting transfers between devices: 11.9 us -> 16.7 us
  Pallas kernels: 21 us -> 19.8 us
    ppermute x10, waiting for transfers between devices: 11 us -> 6.77 us  [swap(): return lax.ppermute(array, axis, [(i, i ^ flip) for i in range(size)])]
    ppermute x3 -> x6, starting transfers between devices: 4.59 us -> 8.46 us  [hop(): lax.ppermute(array, ('dp', 'grp'), [(i, i ^ ((near & 1) * groups | (near...]
    ppermute x3 -> x6, waiting for transfers between devices: 5.65 us -> 2.69 us  [hop(): lax.ppermute(array, ('dp', 'grp'), [(i, i ^ ((near & 1) * groups | (near...]
    pallas_call x8 -> x10, Pallas kernels: 11.1 us -> 9.82 us  [the longest x8 9.67 us: transform(): pl.pallas_call(functools.partial(transform_kernel, jobs=jobs, step=len(fr...]
    ppermute x10, starting transfers between devices: 7.34 us -> 8.24 us  [swap(): return lax.ppermute(array, axis, [(i, i ^ flip) for i in range(size)])]
  transfers between devices with their start and end apart: 13 -> 16, of which waited for: 9 -> 7; matrix products, arithmetic and copies ran while one was open for 2% -> 2% of each run, Pallas kernels for 19% -> 18%
where the time goes in v3:
time: 48.3 us; the launch traced here: 48.1 us
  Pallas kernels  19.8 us (41%)
  starting transfers between devices  16.7 us (35%)
  waiting for transfers between devices  9.46 us (20%)
  local copies, waits for them, and re-layouts  0.94 us (2%)
  between operations  0.86 us (2%)
    pallas_call x8, Pallas kernels, transform(): pl.pallas_call(functools.partial(transform_kernel, jobs=jobs, step=len(fr...  9.67 us
    ppermute x6, starting transfers between devices, hop(): lax.ppermute(array, ('dp', 'grp'), [(i, i ^ ((near & 1) * groups | (near...  8.46 us
    ppermute x10, starting transfers between devices, swap(): return lax.ppermute(array, axis, [(i, i ^ flip) for i in range(size)])  8.24 us
    pallas_call x1, Pallas kernels, body(): pl.pallas_call(sums_kernel, out_shape=pltpu.VMEM((CLASSES * SLAB, PIX), j...  7.26 us
    ppermute x10, waiting for transfers between devices, swap(): return lax.ppermute(array, axis, [(i, i ^ flip) for i in range(size)])  6.77 us
    ppermute x6, waiting for transfers between devices, hop(): lax.ppermute(array, ('dp', 'grp'), [(i, i ^ ((near & 1) * groups | (near...  2.69 us
    pallas_call x1, Pallas kernels, body(): pl.pallas_call(functools.partial(scores_kernel, own=own, groups=groups),...  2 us
  transfers between devices with their start and end apart: 16, of which 7 were waited for; matrix products, arithmetic and copies ran while one was open for 2% of the time, Pallas kernels for 18%

profile of v3, /device:TPU:0, one launch (start us, length us, event | category | flops | bytes accessed | tf_op | source)
XLA Modules:
  0.0 48.1 jit_solution(17546197271329943667)
XLA Ops:
  0.7 7.3 %shard_map.104.acc = f32[40960,128]{1,0:T(8,128)S(1)} custom-call(s32[512]{0:T(512)} %class_ids.1, s32[2,512]{1,0:T(2,128)} %bitcast.31, bf16[512,128,128]{2,1,0:T(8,128)(2,1)} %images.1), custom_call_target="tpu_custom_call" | custom-call | tf_op jit(solution)/shard_map/pallas_call | solution.py:339
  8.0 1.2 %shard_map.105 = (bf16[4,272,128]{2,1,0:T(8,128)(2,1)S(1)}, bf16[4,256,2,128]{3,2,1,0:T(2,128)(2,1)S(1)}) custom-call(s32[4,128]{1,0:T(4,128)S(1)} %bitcast.22, f32[40960,128]{1,0:T(8,128)S(1)} %shard_map.104.acc, s32[4,128]{1,0:T(4,128)S(1)} %bitcast.23, bf16[256,128]{1,0:T(8,128)(2,1)S(1)} %copy-done.3, bf16[80,128]{1,0:T(8,128)(2,1)S(1)} %copy-done.5, ...), custom_call_target="tpu_custom_call" | custom-call | flops 10000000000 | bytes 1048576 | tf_op jit(solution)/shard_map/pallas_call | solution.py:364
  9.7 1.2 %shard_map.106 = (bf16[4,272,128]{2,1,0:T(8,128)(2,1)S(1)}, bf16[4,256,2,128]{3,2,1,0:T(2,128)(2,1)S(1)}) custom-call(bf16[4,272,128]{2,1,0:T(8,128)(2,1)S(1)} %get-tuple-element.25._, f32[40960,128]{1,0:T(8,128)S(1)} %shard_map.104.acc, s32[4,128]{1,0:T(4,128)S(1)} %bitcast.24, bf16[256,128]{1,0:T(8,128)(2,1)S(1)} %copy-done.3, ...), custom_call_target="tpu_custom_call" | custom-call | flops 10000000000 | bytes 1048576 | tf_op jit(solution)/shard_map/pallas_call | solution.py:364
  11.0 2.9 %collective-permute-start.5 = (bf16[2,272,128]{2,1,0:T(8,128)(2,1)S(1)}, bf16[2,272,128]{2,1,0:T(8,128)(2,1)S(1)}, u32[]{:S(2)}, u32[]{:S(2)}) collective-permute-start(bf16[2,272,128]{2,1,0:T(8,128)(2,1)S(1)} %get-tuple-element.57._), channel_id=1, source_target_pairs={{0,2},{1,3},{2,0},{3,1},{4,6},{5,7},{6,4},{7,5},{8,10},{9,11},{10,... | collective-permute-start | bytes 417800 | tf_op jit(solution)/shard_map/ppermute | solution.py:315
  14.0 1.2 %shard_map.107 = (bf16[4,272,128]{2,1,0:T(8,128)(2,1)S(1)}, bf16[4,256,2,128]{3,2,1,0:T(2,128)(2,1)S(1)}) custom-call(bf16[2,272,128]{2,1,0:T(8,128)(2,1)S(1)} %get-tuple-element.57._, f32[40960,128]{1,0:T(8,128)S(1)} %shard_map.104.acc, s32[4,128]{1,0:T(4,128)S(1)} %bitcast.25, bf16[256,128]{1,0:T(8,128)(2,1)S(1)} %copy-done.3, ...), custom_call_target="tpu_custom_call" | custom-call | flops 10000000000 | bytes 1048576 | tf_op jit(solution)/shard_map/pallas_call | solution.py:364
  15.2 1.2 %shard_map.108 = (bf16[4,272,128]{2,1,0:T(8,128)(2,1)S(1)}, bf16[4,256,2,128]{3,2,1,0:T(2,128)(2,1)S(1)}) custom-call(bf16[4,272,128]{2,1,0:T(8,128)(2,1)S(1)} %get-tuple-element.27._, f32[40960,128]{1,0:T(8,128)S(1)} %shard_map.104.acc, s32[4,128]{1,0:T(4,128)S(1)} %bitcast.26, bf16[256,128]{1,0:T(8,128)(2,1)S(1)} %copy-done.3, ...), custom_call_target="tpu_custom_call" | custom-call | flops 10000000000 | bytes 1048576 | tf_op jit(solution)/shard_map/pallas_call | solution.py:364
  16.5 1.5 %collective-permute-start.4 = (bf16[2,272,128]{2,1,0:T(8,128)(2,1)S(1)}, bf16[2,272,128]{2,1,0:T(8,128)(2,1)S(1)}, u32[]{:S(2)}, u32[]{:S(2)}) collective-permute-start(bf16[2,272,128]{2,1,0:T(8,128)(2,1)S(1)} %get-tuple-element.56), channel_id=1, source_target_pairs={{0,6},{1,7},{2,4},{3,5},{4,2},{5,3},{6,0},{7,1},{8,14},{9,15},{10,... | collective-permute-start | bytes 417800 | tf_op jit(solution)/shard_map/ppermute | solution.py:315
  18.1 1.2 %shard_map.109 = (bf16[4,272,128]{2,1,0:T(8,128)(2,1)S(1)}, bf16[4,256,2,128]{3,2,1,0:T(2,128)(2,1)S(1)}) custom-call(bf16[2,272,128]{2,1,0:T(8,128)(2,1)S(1)} %get-tuple-element.55._.refs_3_, f32[40960,128]{1,0:T(8,128)S(1)} %shard_map.104.acc, s32[4,128]{1,0:T(4,128)S(1)} %bitcast.27, bf16[256,128]{1,0:T(8,128)(2,1)S(1)} %copy-done.3, ...), custom_call_target="tpu_custom_call" | custom-call | flops 10000000000 | bytes 1048576 | tf_op jit(solution)/shard_map/pallas_call | solution.py:364
  19.5 1.2 %shard_map.110 = (bf16[4,272,128]{2,1,0:T(8,128)(2,1)S(1)}, bf16[4,256,2,128]{3,2,1,0:T(2,128)(2,1)S(1)}) custom-call(bf16[4,272,128]{2,1,0:T(8,128)(2,1)S(1)} %get-tuple-element.29._, f32[40960,128]{1,0:T(8,128)S(1)} %shard_map.104.acc, s32[4,128]{1,0:T(4,128)S(1)} %bitcast.28, bf16[256,128]{1,0:T(8,128)(2,1)S(1)} %copy-done.3, ...), custom_call_target="tpu_custom_call" | custom-call | flops 10000000000 | bytes 1048576 | tf_op jit(solution)/shard_map/pallas_call | solution.py:364
  21.3 1.8 %collective-permute-start.8 = (bf16[2,272,128]{2,1,0:T(8,128)(2,1)S(1)}, bf16[2,272,128]{2,1,0:T(8,128)(2,1)S(1)}, u32[]{:S(2)}, u32[]{:S(2)}) collective-permute-start(bf16[2,272,128]{2,1,0:T(8,128)(2,1)S(1)} %get-tuple-element.53._), channel_id=1, source_target_pairs={{0,2},{1,3},{2,0},{3,1},{4,6},{5,7},{6,4},{7,5},{8,10},{9,11},{10,... | collective-permute-start | bytes 417800 | tf_op jit(solution)/shard_map/ppermute | solution.py:315
  23.0 1.2 %shard_map.111 = (bf16[4,272,128]{2,1,0:T(8,128)(2,1)S(1)}, bf16[4,256,2,128]{3,2,1,0:T(2,128)(2,1)S(1)}) custom-call(bf16[2,272,128]{2,1,0:T(8,128)(2,1)S(1)} %get-tuple-element.53._, f32[40960,128]{1,0:T(8,128)S(1)} %shard_map.104.acc, s32[4,128]{1,0:T(4,128)S(1)} %bitcast.29, bf16[256,128]{1,0:T(8,128)(2,1)S(1)} %copy-done.3, ...), custom_call_target="tpu_custom_call" | custom-call | flops 10000000000 | bytes 1048576 | tf_op jit(solution)/shard_map/pallas_call | solution.py:364
  24.3 1.2 %shard_map.112 = (bf16[4,272,128]{2,1,0:T(8,128)(2,1)S(1)}, bf16[4,256,2,128]{3,2,1,0:T(2,128)(2,1)S(1)}) custom-call(bf16[4,272,128]{2,1,0:T(8,128)(2,1)S(1)} %get-tuple-element.31._, f32[40960,128]{1,0:T(8,128)S(1)} %shard_map.104.acc, s32[4,128]{1,0:T(4,128)S(1)} %bitcast.30, bf16[256,128]{1,0:T(8,128)(2,1)S(1)} %copy-done.3, ...), custom_call_target="tpu_custom_call" | custom-call | flops 10000000000 | bytes 1048576 | tf_op jit(solution)/shard_map/pallas_call | solution.py:364
  25.9 1.4 %collective-permute-start.7 = (bf16[2,272,128]{2,1,0:T(8,128)(2,1)S(1)}, bf16[2,272,128]{2,1,0:T(8,128)(2,1)S(1)}, u32[]{:S(2)}, u32[]{:S(2)}) collective-permute-start(bf16[2,272,128]{2,1,0:T(8,128)(2,1)S(1)} %get-tuple-element.52), channel_id=1, source_target_pairs={{0,6},{1,7},{2,4},{3,5},{4,2},{5,3},{6,0},{7,1},{8,14},{9,15},{10,... | collective-permute-start | bytes 417800 | tf_op jit(solution)/shard_map/ppermute | solution.py:315
  27.9 3.8 %collective-permute-start.12 = (bf16[272,128]{1,0:T(8,128)(2,1)S(1)}, bf16[272,128]{1,0:T(8,128)(2,1)S(1)}, u32[]{:S(2)}, u32[]{:S(2)}) collective-permute-start(bf16[272,128]{1,0:T(8,128)(2,1)S(1)} %get-tuple-element.36), channel_id=1, source_target_pairs={{0,24},{4,28},{8,16},{12,20},{16,8},{20,12},{24,0},{28,4},{1,25},{... | collective-permute-start | bytes 208904 | tf_op jit(solution)/shard_map/ppermute | solution.py:310
  31.8 1.5 %collective-permute-done.7.refs_0_ = bf16[2,272,128]{2,1,0:T(8,128)(2,1)S(1)} collective-permute-done((bf16[2,272,128]{2,1,0:T(8,128)(2,1)S(1)}, bf16[2,272,128]{2,1,0:T(8,128)(2,1)S(1)}, u32[]{:S(2)}, u32[]{:S(2)}) %collective-permute-start.7) | collective-permute-done | bytes 139296 | tf_op jit(solution)/shard_map/ppermute | solution.py:315
  33.3 1.2 %collective-permute-done.9.refs_2_ = bf16[2,272,128]{2,1,0:T(8,128)(2,1)S(1)} collective-permute-done((bf16[2,272,128]{2,1,0:T(8,128)(2,1)S(1)}, bf16[2,272,128]{2,1,0:T(8,128)(2,1)S(1)}, u32[]{:S(2)}, u32[]{:S(2)}) %collective-permute-start.9) | collective-permute-done | bytes 139296 | tf_op jit(solution)/shard_map/ppermute | solution.py:315
  34.5 1.8 %collective-permute-start.10 = (bf16[272,128]{1,0:T(8,128)(2,1)S(1)}, bf16[272,128]{1,0:T(8,128)(2,1)S(1)}, u32[]{:S(2)}, u32[]{:S(2)}) collective-permute-start(bf16[272,128]{1,0:T(8,128)(2,1)S(1)} %get-tuple-element.35), channel_id=1, source_target_pairs={{0,8},{4,12},{8,0},{12,4},{16,24},{20,28},{24,16},{28,20},{1,9},{5... | collective-permute-start | bytes 208904 | tf_op jit(solution)/shard_map/ppermute | solution.py:310
  36.3 1.3 %collective-permute-done.11.refs_2_ = bf16[272,128]{1,0:T(8,128)(2,1)S(1)} collective-permute-done((bf16[272,128]{1,0:T(8,128)(2,1)S(1)}, bf16[272,128]{1,0:T(8,128)(2,1)S(1)}, u32[]{:S(2)}, u32[]{:S(2)}) %collective-permute-start.11) | collective-permute-done | bytes 69664 | tf_op jit(solution)/shard_map/ppermute | solution.py:310
  37.6 1.4 %collective-permute-done.10.refs_1_ = bf16[272,128]{1,0:T(8,128)(2,1)S(1)} collective-permute-done((bf16[272,128]{1,0:T(8,128)(2,1)S(1)}, bf16[272,128]{1,0:T(8,128)(2,1)S(1)}, u32[]{:S(2)}, u32[]{:S(2)}) %collective-permute-start.10) | collective-permute-done | bytes 69664 | tf_op jit(solution)/shard_map/ppermute | solution.py:310
  39.0 0.7 %shard_map.115 = (f32[8,4096]{1,0:T(8,128)S(1)}, f32[8,4096]{1,0:T(8,128)S(1)}, bf16[8,8192]{1,0:T(8,128)(2,1)S(1)}) custom-call(bf16[272,128]{1,0:T(8,128)(2,1)S(1)} %get-tuple-element.34.refs_0_, bf16[272,128]{1,0:T(8,128)(2,1)S(1)} %collective-permute-done.10.refs_1_, bf16[272,128]{1,0:T(8,128)(2,1)S(1)} %collective-permute-done.11.refs_2_, ...), custom_call_target="tpu_custom_call" | custom-call | tf_op jit(solution)/shard_map/pallas_call | solution.py:408
  39.7 1.7 %collective-permute-start.14 = (bf16[8,8192]{1,0:T(8,128)(2,1)S(1)}, bf16[8,8192]{1,0:T(8,128)(2,1)S(1)}, u32[]{:S(2)}, u32[]{:S(2)}) collective-permute-start(bf16[8,8192]{1,0:T(8,128)(2,1)S(1)} %get-tuple-element.39.refs_0_), channel_id=1, source_target_pairs={{0,2},{1,3},{2,0},{3,1},{4,6},{5,7},{6,4},{7,5},{8,10},{9,11},{10,... | collective-permute-start | bytes 393224 | tf_op jit(solution)/shard_map/ppermute | solution.py:310
  41.4 3.4 %collective-permute-done.14.refs_2_ = bf16[8,8192]{1,0:T(8,128)(2,1)S(1)} collective-permute-done((bf16[8,8192]{1,0:T(8,128)(2,1)S(1)}, bf16[8,8192]{1,0:T(8,128)(2,1)S(1)}, u32[]{:S(2)}, u32[]{:S(2)}) %collective-permute-start.14) | collective-permute-done | bytes 131104 | tf_op jit(solution)/shard_map/ppermute | solution.py:310
  44.8 0.9 %copy.11 = f32[8,2,4096]{2,1,0:T(2,128)} copy(f32[8,2,4096]{2,0,1:T(8,128)S(1)} %pad_maximum_fusion) | data formatting | bytes 524288
  46.1 2.0 %shard_map.116 = f32[32,256]{1,0:T(8,128)} custom-call(bf16[8,8192]{1,0:T(8,128)(2,1)S(1)} %get-tuple-element.39.refs_0_, bf16[8,8192]{1,0:T(8,128)(2,1)S(1)} %collective-permute-done.13.refs_1_, bf16[8,8192]{1,0:T(8,128)(2,1)S(1)} %collective-permute-done.14.refs_2_, bf16[8,8192]{1,0:T(8,128)(2,1)S(1)} %collective-permute-done.15.refs_3_, ...), custom_call_target="tpu_custom_call" | custom-call | tf_op jit(solution)/shard_map/pallas_call | solution.py:429
  (39 shorter events, 3.1 us)
Async XLA Ops:
  0.6 7.3 %copy-start.2 = (s32[512]{0:T(512)S(1)}, s32[512]{0:T(512)}, u32[]{:S(2)}) copy-start(s32[512]{0:T(512)} %class_ids.1) | copy-start | bytes 6148
  0.6 7.3 %copy-start.3 = (bf16[256,128]{1,0:T(8,128)(2,1)S(1)}, bf16[256,128]{1,0:T(8,128)(2,1)}, u32[]{:S(2)}) copy-start(bf16[256,128]{1,0:T(8,128)(2,1)} %constant.10.clone.col) | copy-start | bytes 196612
  0.7 7.3 %copy-start.4 = (bf16[16,1024]{1,0:T(8,128)(2,1)S(1)}, bf16[16,1024]{1,0:T(8,128)(2,1)}, u32[]{:S(2)}) copy-start(bf16[16,1024]{1,0:T(8,128)(2,1)} %constant.12.clone.last) | copy-start | bytes 98308
  0.7 7.3 %copy-start.5 = (bf16[80,128]{1,0:T(8,128)(2,1)S(1)}, bf16[80,128]{1,0:T(8,128)(2,1)}, u32[]{:S(2)}) copy-start(bf16[80,128]{1,0:T(8,128)(2,1)} %constant.11.clone.row) | copy-start | bytes 61444
  9.2 1.7 %collective-permute-start = (bf16[4,272,128]{2,1,0:T(8,128)(2,1)S(1)}, bf16[4,272,128]{2,1,0:T(8,128)(2,1)S(1)}, u32[]{:S(2)}, u32[]{:S(2)}) collective-permute-start(bf16[4,272,128]{2,1,0:T(8,128)(2,1)S(1)} %get-tuple-element.25._), channel_id=1, source_target_pairs={{0,1},{1,0},{2,3},{3,2},{4,5},{5,4},{6,7},{7,6},{8,9},{9,8},{10,11... | collective-permute-start | bytes 835592 | tf_op jit(solution)/shard_map/ppermute | solution.py:310
  11.0 16.8 %collective-permute-start.5 = (bf16[2,272,128]{2,1,0:T(8,128)(2,1)S(1)}, bf16[2,272,128]{2,1,0:T(8,128)(2,1)S(1)}, u32[]{:S(2)}, u32[]{:S(2)}) collective-permute-start(bf16[2,272,128]{2,1,0:T(8,128)(2,1)S(1)} %get-tuple-element.57._), channel_id=1, source_target_pairs={{0,2},{1,3},{2,0},{3,1},{4,6},{5,7},{6,4},{7,5},{8,10},{9,11},{10,... | collective-permute-start | bytes 417800 | tf_op jit(solution)/shard_map/ppermute | solution.py:315
  15.2 2.8 %collective-permute-start.1 = (bf16[4,272,128]{2,1,0:T(8,128)(2,1)S(1)}, bf16[4,272,128]{2,1,0:T(8,128)(2,1)S(1)}, u32[]{:S(2)}, u32[]{:S(2)}) collective-permute-start(bf16[4,272,128]{2,1,0:T(8,128)(2,1)S(1)} %get-tuple-element.27._), channel_id=1, source_target_pairs={{0,1},{1,0},{2,3},{3,2},{4,5},{5,4},{6,7},{7,6},{8,9},{9,8},{10,11... | collective-permute-start | bytes 835592 | tf_op jit(solution)/shard_map/ppermute | solution.py:310
  16.5 10.9 %collective-permute-start.4 = (bf16[2,272,128]{2,1,0:T(8,128)(2,1)S(1)}, bf16[2,272,128]{2,1,0:T(8,128)(2,1)S(1)}, u32[]{:S(2)}, u32[]{:S(2)}) collective-permute-start(bf16[2,272,128]{2,1,0:T(8,128)(2,1)S(1)} %get-tuple-element.56), channel_id=1, source_target_pairs={{0,6},{1,7},{2,4},{3,5},{4,2},{5,3},{6,0},{7,1},{8,14},{9,15},{10,... | collective-permute-start | bytes 417800 | tf_op jit(solution)/shard_map/ppermute | solution.py:315
  19.3 1.9 %collective-permute-start.2 = (bf16[4,272,128]{2,1,0:T(8,128)(2,1)S(1)}, bf16[4,272,128]{2,1,0:T(8,128)(2,1)S(1)}, u32[]{:S(2)}, u32[]{:S(2)}) collective-permute-start(bf16[4,272,128]{2,1,0:T(8,128)(2,1)S(1)} %get-tuple-element.29._), channel_id=1, source_target_pairs={{0,1},{1,0},{2,3},{3,2},{4,5},{5,4},{6,7},{7,6},{8,9},{9,8},{10,11... | collective-permute-start | bytes 835592 | tf_op jit(solution)/shard_map/ppermute | solution.py:310
  20.8 7.1 %collective-permute-start.6 = (bf16[2,272,128]{2,1,0:T(8,128)(2,1)S(1)}, bf16[2,272,128]{2,1,0:T(8,128)(2,1)S(1)}, u32[]{:S(2)}, u32[]{:S(2)}) collective-permute-start(bf16[2,272,128]{2,1,0:T(8,128)(2,1)S(1)} %get-tuple-element.54), channel_id=1, source_target_pairs={{0,4},{1,5},{2,6},{3,7},{4,0},{5,1},{6,2},{7,3},{8,12},{9,13},{10,... | collective-permute-start | bytes 417800 | tf_op jit(solution)/shard_map/ppermute | solution.py:315
  21.3 12.0 %collective-permute-start.8 = (bf16[2,272,128]{2,1,0:T(8,128)(2,1)S(1)}, bf16[2,272,128]{2,1,0:T(8,128)(2,1)S(1)}, u32[]{:S(2)}, u32[]{:S(2)}) collective-permute-start(bf16[2,272,128]{2,1,0:T(8,128)(2,1)S(1)} %get-tuple-element.53._), channel_id=1, source_target_pairs={{0,2},{1,3},{2,0},{3,1},{4,6},{5,7},{6,4},{7,5},{8,10},{9,11},{10,... | collective-permute-start | bytes 417800 | tf_op jit(solution)/shard_map/ppermute | solution.py:315
  24.2 14.8 %copy-start = (f32[128,256]{1,0:T(8,128)S(1)}, f32[128,256]{1,0:T(8,128)}, u32[]{:S(2)}) copy-start(f32[128,256]{1,0:T(8,128)} %constant.13.clone.refs_4_) | copy-start | bytes 393220
  24.2 14.8 %copy-start.1 = (f32[32,128]{1,0:T(8,128)S(1)}, f32[32,128]{1,0:T(8,128)}, u32[]{:S(2)}) copy-start(f32[32,128]{1,0:T(8,128)} %constant.14.clone.refs_5_) | copy-start | bytes 49156
  24.3 1.6 %collective-permute-start.3 = (bf16[4,272,128]{2,1,0:T(8,128)(2,1)S(1)}, bf16[4,272,128]{2,1,0:T(8,128)(2,1)S(1)}, u32[]{:S(2)}, u32[]{:S(2)}) collective-permute-start(bf16[4,272,128]{2,1,0:T(8,128)(2,1)S(1)} %get-tuple-element.31._), channel_id=1, source_target_pairs={{0,1},{1,0},{2,3},{3,2},{4,5},{5,4},{6,7},{7,6},{8,9},{9,8},{10,11... | collective-permute-start | bytes 835592 | tf_op jit(solution)/shard_map/ppermute | solution.py:310
  25.9 7.4 %collective-permute-start.7 = (bf16[2,272,128]{2,1,0:T(8,128)(2,1)S(1)}, bf16[2,272,128]{2,1,0:T(8,128)(2,1)S(1)}, u32[]{:S(2)}, u32[]{:S(2)}) collective-permute-start(bf16[2,272,128]{2,1,0:T(8,128)(2,1)S(1)} %get-tuple-element.52), channel_id=1, source_target_pairs={{0,6},{1,7},{2,4},{3,5},{4,2},{5,3},{6,0},{7,1},{8,14},{9,15},{10,... | collective-permute-start | bytes 417800 | tf_op jit(solution)/shard_map/ppermute | solution.py:315
  27.4 7.0 %collective-permute-start.9 = (bf16[2,272,128]{2,1,0:T(8,128)(2,1)S(1)}, bf16[2,272,128]{2,1,0:T(8,128)(2,1)S(1)}, u32[]{:S(2)}, u32[]{:S(2)}) collective-permute-start(bf16[2,272,128]{2,1,0:T(8,128)(2,1)S(1)} %get-tuple-element.50), channel_id=1, source_target_pairs={{0,4},{1,5},{2,6},{3,7},{4,0},{5,1},{6,2},{7,3},{8,12},{9,13},{10,... | collective-permute-start | bytes 417800 | tf_op jit(solution)/shard_map/ppermute | solution.py:315
  27.9 8.4 %collective-permute-start.12 = (bf16[272,128]{1,0:T(8,128)(2,1)S(1)}, bf16[272,128]{1,0:T(8,128)(2,1)S(1)}, u32[]{:S(2)}, u32[]{:S(2)}) collective-permute-start(bf16[272,128]{1,0:T(8,128)(2,1)S(1)} %get-tuple-element.36), channel_id=1, source_target_pairs={{0,24},{4,28},{8,16},{12,20},{16,8},{20,12},{24,0},{28,4},{1,25},{... | collective-permute-start | bytes 208904 | tf_op jit(solution)/shard_map/ppermute | solution.py:310
  31.8 5.8 %collective-permute-start.11 = (bf16[272,128]{1,0:T(8,128)(2,1)S(1)}, bf16[272,128]{1,0:T(8,128)(2,1)S(1)}, u32[]{:S(2)}, u32[]{:S(2)}) collective-permute-start(bf16[272,128]{1,0:T(8,128)(2,1)S(1)} %get-tuple-element.33._), channel_id=1, source_target_pairs={{0,16},{4,20},{8,24},{12,28},{16,0},{20,4},{24,8},{28,12},{1,17},{... | collective-permute-start | bytes 208904 | tf_op jit(solution)/shard_map/ppermute | solution.py:310
  34.5 4.5 %collective-permute-start.10 = (bf16[272,128]{1,0:T(8,128)(2,1)S(1)}, bf16[272,128]{1,0:T(8,128)(2,1)S(1)}, u32[]{:S(2)}, u32[]{:S(2)}) collective-permute-start(bf16[272,128]{1,0:T(8,128)(2,1)S(1)} %get-tuple-element.35), channel_id=1, source_target_pairs={{0,8},{4,12},{8,0},{12,4},{16,24},{20,28},{24,16},{28,20},{1,9},{5... | collective-permute-start | bytes 208904 | tf_op jit(solution)/shard_map/ppermute | solution.py:310
  39.7 5.0 %collective-permute-start.14 = (bf16[8,8192]{1,0:T(8,128)(2,1)S(1)}, bf16[8,8192]{1,0:T(8,128)(2,1)S(1)}, u32[]{:S(2)}, u32[]{:S(2)}) collective-permute-start(bf16[8,8192]{1,0:T(8,128)(2,1)S(1)} %get-tuple-element.39.refs_0_), channel_id=1, source_target_pairs={{0,2},{1,3},{2,0},{3,1},{4,6},{5,7},{6,4},{7,5},{8,10},{9,11},{10,... | collective-permute-start | bytes 393224 | tf_op jit(solution)/shard_map/ppermute | solution.py:310
  41.4 4.3 %collective-permute-start.13 = (bf16[8,8192]{1,0:T(8,128)(2,1)S(1)}, bf16[8,8192]{1,0:T(8,128)(2,1)S(1)}, u32[]{:S(2)}, u32[]{:S(2)}) collective-permute-start(bf16[8,8192]{1,0:T(8,128)(2,1)S(1)} %get-tuple-element.39.refs_0_), channel_id=1, source_target_pairs={{0,1},{1,0},{2,3},{3,2},{4,5},{5,4},{6,7},{7,6},{8,9},{9,8},{10,11... | collective-permute-start | bytes 393224 | tf_op jit(solution)/shard_map/ppermute | solution.py:310
  44.7 1.3 %collective-permute-start.15 = (bf16[8,8192]{1,0:T(8,128)(2,1)S(1)}, bf16[8,8192]{1,0:T(8,128)(2,1)S(1)}, u32[]{:S(2)}, u32[]{:S(2)}) collective-permute-start(bf16[8,8192]{1,0:T(8,128)(2,1)S(1)} %collective-permute-done.14.refs_2_), channel_id=1, source_target_pairs={{0,1},{1,0},{2,3},{3,2},{4,5},{5,4},{6,7},{7,6},{8,9},{9,8},{10,11... | collective-permute-start | bytes 393224 | tf_op jit(solution)/shard_map/ppermute | solution.py:310

commit v4 on v3

--- a/solution.py
+++ b/solution.py
@@ -60,7 +60,7 @@
 
 
 def expand_table():
-    out = np.zeros((PIX, 2 * PIX), np.float32)
+    out = np.zeros((PIX, 2 * PIX), ml_dtypes.bfloat16)
     for at in range(BAND):
         k = at - HALF
         for copy in range(2):
@@ -133,23 +133,15 @@
 
 
 def transform_kernel(
-    _, acc, ids_rows, col, row, last, block, out, fresh, edges, sems, *, jobs, step, other, groups, own
+    _, acc, ids_rows, col, row, last, out, edges, *, jobs, other, groups, own
 ):
     pairs = own // 2
     count = out.shape[0]
     half = count // len(jobs)
-    together = 2 if count % 2 == 0 else 1
+    together = 4 if count % 4 == 0 else 1
     lane = lax.broadcasted_iota(jnp.int32, (TILE, ROWS), 1)
     sub = lax.broadcasted_iota(jnp.int32, (TILE, PIX), 0)
     edges[...] = jnp.zeros_like(edges)
-    spans = fresh.shape[0]
-
-    def regroup(f):
-        at = (step * spans + f) * PIX
-        return pltpu.make_async_copy(block.at[:, :, pl.ds(at, PIX)], fresh.at[f], sems.at[f])
-
-    for f in range(spans):
-        regroup(f).start()
 
     def folded(c):
         at = pl.multiple_of(c * SLAB, TILE)
@@ -201,8 +193,17 @@
         return 0
 
     lax.fori_loop(0, count // together, some, 0)
-    for f in range(spans):
-        regroup(f).wait()
+
+
+def regroup_kernel(_, block, fresh, sems):
+    copies = [
+        pltpu.make_async_copy(block.at[:, :, pl.ds(f * PIX, PIX)], fresh.at[f], sems.at[f])
+        for f in range(fresh.shape[0])
+    ]
+    for copy in copies:
+        copy.start()
+    for copy in copies:
+        copy.wait()
 
 
 def totals_kernel(_, *refs, parts):
@@ -213,12 +214,40 @@
         out[...] = total.astype(jnp.bfloat16)
 
 
-def averages_kernel(*refs, own, parts):
-    pieces, (expand, taper, real, imag, rounded, wide, rows) = refs[:parts], refs[parts:]
-    pairs = own // 2
+def added(pieces):
     total = pieces[0][...].astype(jnp.float32)
     for piece in pieces[1:]:
         total += piece[...].astype(jnp.float32)
+    return total
+
+
+def added_kernel(*refs):
+    refs[-1][...] = added(refs[:-1]).astype(jnp.bfloat16)
+
+
+def averages_kernel(*refs, own, parts):
+    pieces, (expand, taper, out, rounded, wide, rows) = refs[:parts], refs[parts:]
+
+    def emit(u, part, value):
+        out[:, part, u * PIX : (u + 1) * PIX] = value[:own]
+        at = part * BAND * BAND + u * PIX
+        rounded[:, at : at + PIX] = value.astype(jnp.bfloat16)
+
+    spread_out(added(pieces), 3, expand, taper, wide, rows, own, emit)
+
+
+def references_kernel(*refs, own):
+    _, piece, expand, taper, rounded, wide, rows = refs
+
+    def emit(u, part, value):
+        at = part * BAND * BAND + u * PIX
+        rounded[:, at : at + PIX] = value.astype(jnp.bfloat16)
+
+    spread_out(piece[...].astype(jnp.float32), 1, expand, taper, wide, rows, own, emit)
+
+
+def spread_out(total, pieces, expand, taper, wide, rows, own, emit):
+    pairs = own // 2
     main, ends = total[: pairs * BAND], total[pairs * BAND :]
     if own < TILE:
         wide[...] = jnp.zeros_like(wide)
@@ -238,9 +267,13 @@
             lane < BAND, line, jnp.where(lane == BAND, extra[:, t : t + 1], 0.0)
         )
         rows[t * TILE : (t + 1) * TILE, :] = line
-    spread = jnp.dot(
-        rows[...], expand[...], preferred_element_type=jnp.float32, precision=lax.Precision.HIGHEST
-    )
+    spread = None
+    rest = rows[...]
+    for k in range(pieces):
+        here = rest.astype(jnp.bfloat16)
+        rest = rest - here.astype(jnp.float32) if k + 1 < pieces else None
+        term = jnp.dot(here, expand[...], preferred_element_type=jnp.float32)
+        spread = term if spread is None else spread + term
 
     def cos_part(t):
         return spread[t * TILE : (t + 1) * TILE, :PIX]
@@ -264,12 +297,9 @@
 
     for u in range(BAND // 2):
         even, odd = at_frequency(2 * u - HALF), at_frequency(2 * u + 1 - HALF)
-        span = slice(u * PIX, (u + 1) * PIX)
-        for part, out in ((0, real), (1, imag)):
+        for part in range(2):
             value = jnp.where(lane < BAND, even[part], odd[part]) * taper[u : u + 1, :] / weight
-            out[:, span] = value
-            at = part * BAND * BAND + u * PIX
-            rounded[:, at : at + PIX] = value.astype(jnp.bfloat16)
+            emit(u, part, value)
 
 
 def scores_kernel(*refs, own, groups):
@@ -330,7 +360,7 @@
     hbm = pl.BlockSpec(memory_space=pltpu.HBM)
     anywhere = pl.BlockSpec(memory_space=pl.ANY)
     flat = BAND * BAND
-    spans = flat // PIX // (2 * nears)
+    spans = flat // PIX
     fresh_count = next_block.shape[0]
 
     def put(space, *arrays):
@@ -358,25 +388,16 @@
     (block,) = put(pltpu.HBM, next_block)
     (held_acc,) = put(pltpu.VMEM, acc)
 
-    fresh = []
-
     def transform(after, jobs, other):
-        out, block_part = pl.pallas_call(
-            functools.partial(
-                transform_kernel, jobs=jobs, step=len(fresh), other=other, groups=groups, own=own
-            ),
-            out_shape=(piece, pltpu.VMEM((spans, fresh_count, 2, PIX), jnp.bfloat16)),
-            in_specs=[anywhere] + [vmem] * 5 + [hbm],
-            out_specs=(vmem, vmem),
-            scratch_shapes=[
-                pltpu.VMEM((2, PACK, PIX), jnp.float32),
-                pltpu.SemaphoreType.DMA((spans,)),
-            ],
+        return pl.pallas_call(
+            functools.partial(transform_kernel, jobs=jobs, other=other, groups=groups, own=own),
+            out_shape=piece,
+            in_specs=[anywhere] + [vmem] * 5,
+            out_specs=vmem,
+            scratch_shapes=[pltpu.VMEM((4, PACK, PIX), jnp.float32)],
             compiler_params=pltpu.CompilerParams(vmem_limit_bytes=8 * MIB),
             cost_estimate=pl.CostEstimate(flops=10**10, bytes_accessed=MIB, transcendentals=0),
-        )(after, held_acc, ids_rows, *tables, block)
-        fresh.append(block_part)
-        return out
+        )(after, held_acc, ids_rows, *tables)
 
     met = {half: [], 0: []}
     done = ids_rows
@@ -404,28 +425,58 @@
         for r, total in enumerate(totals):
             far = first + r
             pieces[far] = swap(total, "dp", far << 1) if far else total
-        done = totals[0]
-    real, imag, rounded = pl.pallas_call(
+        if first:
+            fresh = pl.pallas_call(
+                regroup_kernel,
+                out_shape=pltpu.VMEM((spans, fresh_count, 2, PIX), jnp.bfloat16),
+                in_specs=[anywhere, hbm],
+                out_specs=vmem,
+                scratch_shapes=[pltpu.SemaphoreType.DMA((spans,))],
+                compiler_params=pltpu.CompilerParams(vmem_limit_bytes=8 * MIB),
+                cost_estimate=pl.CostEstimate(flops=10**8, bytes_accessed=MIB, transcendentals=0),
+            )(totals[0], block)
+            done = fresh
+    summed = pl.pallas_call(
+        added_kernel,
+        out_shape=jax.ShapeDtypeStruct((block_rows, PIX), jnp.bfloat16),
+        in_specs=[vmem] * fars,
+        out_specs=vmem,
+        compiler_params=pltpu.CompilerParams(vmem_limit_bytes=8 * MIB),
+    )(*put(pltpu.VMEM, *pieces))
+    final_tables = jnp.asarray(expand_table()), jnp.asarray(filter_table())
+    spread_scratch = [
+        pltpu.VMEM((TILE * BAND, PIX), jnp.float32),
+        pltpu.VMEM(((BAND + 1) * TILE, PIX), jnp.float32),
+    ]
+    averages, rounded = pl.pallas_call(
         functools.partial(averages_kernel, own=own, parts=fars),
         out_shape=(
-            jax.ShapeDtypeStruct((TILE, flat), jnp.float32),
-            jax.ShapeDtypeStruct((TILE, flat), jnp.float32),
+            jax.ShapeDtypeStruct((own, 2, flat), jnp.float32),
             jax.ShapeDtypeStruct((TILE, 2 * flat), jnp.bfloat16),
         ),
         in_specs=[vmem] * (fars + 2),
-        out_specs=(vmem, vmem, vmem),
-        scratch_shapes=[
-            pltpu.VMEM((TILE * BAND, PIX), jnp.float32),
-            pltpu.VMEM(((BAND + 1) * TILE, PIX), jnp.float32),
-        ],
+        out_specs=(vmem, vmem),
+        scratch_shapes=spread_scratch,
         compiler_params=pltpu.CompilerParams(vmem_limit_bytes=8 * MIB),
-    )(*put(pltpu.VMEM, *pieces), jnp.asarray(expand_table()), jnp.asarray(filter_table()))
-    averages = jnp.stack([real[:own], imag[:own]], axis=1)
-    held = [rounded, swap(rounded, "grp", 1)]
+    )(*put(pltpu.VMEM, *pieces), *final_tables)
+
+    def references(after, piece):
+        return pl.pallas_call(
+            functools.partial(references_kernel, own=own),
+            out_shape=jax.ShapeDtypeStruct((TILE, 2 * flat), jnp.bfloat16),
+            in_specs=[anywhere] + [vmem] * 3,
+            out_specs=vmem,
+            scratch_shapes=spread_scratch,
+            compiler_params=pltpu.CompilerParams(vmem_limit_bytes=8 * MIB),
+            cost_estimate=pl.CostEstimate(flops=10**10, bytes_accessed=MIB, transcendentals=0),
+        )(after, *put(pltpu.VMEM, piece), *final_tables)
+
+    held = [rounded, references(rounded, swap(summed, "grp", 1))]
     for k in range(2, groups, 2):
-        across = swap(rounded, "grp", k)
-        held += [across, swap(across, "grp", 1)]
-    fresh = [f.reshape(spans, 2 * fresh_count, PIX) for f in fresh]
+        across = swap(summed, "grp", k)
+        held.append(references(held[-1], across))
+        held.append(references(held[-1], swap(across, "grp", 1)))
+    fresh = [fresh.reshape(spans, 2 * fresh_count, PIX)]
     scores = pl.pallas_call(
         functools.partial(scores_kernel, own=own, groups=groups),
         out_shape=jax.ShapeDtypeStruct((own * groups, fresh_count), jnp.float32),

time: 48.3 us -> 46.3 us (0.959)
  waiting for transfers between devices: 9.46 us -> 5.75 us
  Pallas kernels: 19.8 us -> 23 us
  local copies, waits for them, and re-layouts: 0.94 us -> 0.04 us
  starting transfers between devices: 16.7 us -> 16.2 us
    ppermute x6, waiting for transfers between devices: 2.69 us -> 0.02 us  [hop(): lax.ppermute(array, ('dp', 'grp'), [(i, i ^ ((near & 1) * groups | (near...]
    pallas_call x8 -> x13, Pallas kernels: 9.67 us -> 12.2 us  [the longest x8 8.09 us: transform(): pl.pallas_call(functools.partial(transform_kernel, jobs=jobs, other=other...]
    ppermute x10, waiting for transfers between devices: 6.77 us -> 5.73 us  [swap(): return lax.ppermute(array, axis, [(i, i ^ flip) for i in range(size)])]
    unnamed x13 -> x12, local copies, waits for them, and re-layouts: 0.94 us -> 0.04 us
    ppermute x10, starting transfers between devices: 8.24 us -> 7.59 us  [swap(): return lax.ppermute(array, axis, [(i, i ^ flip) for i in range(size)])]
    pallas_call x1, Pallas kernels: 0.69 us -> 1.33 us  [body(): pl.pallas_call(functools.partial(averages_kernel, own=own, parts=fars), o...]
  transfers between devices with their start and end apart: 16 -> 16, of which waited for: 7 -> 6; matrix products, arithmetic and copies ran while one was open for 2% -> 1% of each run, Pallas kernels for 18% -> 27%
where the time goes in v4:
time: 46.3 us; the launch traced here: 46.1 us
  Pallas kernels  23 us (50%)
  starting transfers between devices  16.2 us (35%)
  waiting for transfers between devices  5.75 us (12%)
  between operations  0.86 us (2%)
    ppermute x6, starting transfers between devices, hop(): lax.ppermute(array, ('dp', 'grp'), [(i, i ^ ((near & 1) * groups | (near...  8.6 us
    pallas_call x8, Pallas kernels, transform(): pl.pallas_call(functools.partial(transform_kernel, jobs=jobs, other=other...  8.09 us
    ppermute x10, starting transfers between devices, swap(): return lax.ppermute(array, axis, [(i, i ^ flip) for i in range(size)])  7.59 us
    pallas_call x1, Pallas kernels, body(): pl.pallas_call(sums_kernel, out_shape=pltpu.VMEM((CLASSES * SLAB, PIX), j...  7.26 us
    ppermute x10, waiting for transfers between devices, swap(): return lax.ppermute(array, axis, [(i, i ^ flip) for i in range(size)])  5.73 us
    pallas_call x1, Pallas kernels, body(): pl.pallas_call(regroup_kernel, out_shape=pltpu.VMEM((spans, fresh_count,...  3.02 us
    pallas_call x1, Pallas kernels, body(): pl.pallas_call(functools.partial(scores_kernel, own=own, groups=groups),...  2 us
    pallas_call x1, Pallas kernels, body(): pl.pallas_call(functools.partial(averages_kernel, own=own, parts=fars), o...  1.33 us
  transfers between devices with their start and end apart: 16, of which 6 were waited for; matrix products, arithmetic and copies ran while one was open for 1% of the time, Pallas kernels for 27%

profile of v4, /device:TPU:0, one launch (start us, length us, event | category | flops | bytes accessed | tf_op | source)
XLA Modules:
  0.0 46.1 jit_solution(6255416512445512964)
XLA Ops:
  0.7 7.3 %shard_map.104.acc = f32[40960,128]{1,0:T(8,128)S(1)} custom-call(s32[512]{0:T(512)} %class_ids.1, s32[2,512]{1,0:T(2,128)} %bitcast.13, bf16[512,128,128]{2,1,0:T(8,128)(2,1)} %images.1), custom_call_target="tpu_custom_call" | custom-call | tf_op jit(solution)/shard_map/pallas_call | solution.py:369
  8.0 1.0 %shard_map.105._ = bf16[4,272,128]{2,1,0:T(8,128)(2,1)S(1)} custom-call(s32[4,128]{1,0:T(4,128)S(1)} %bitcast.4, f32[40960,128]{1,0:T(8,128)S(1)} %shard_map.104.acc, s32[4,128]{1,0:T(4,128)S(1)} %bitcast.5, bf16[256,128]{1,0:T(8,128)(2,1)S(1)} %copy-done.3, bf16[80,128]{1,0:T(8,128)(2,1)S(1)} %copy-done.5, bf16[16,1024]{1,0:T(8,128)(2,1)S(1)} %copy-done.4), custom_call_target="tpu_custom_call" | custom-call | flops 10000000000 | bytes 1048576 | tf_op jit(solution)/shard_map/pallas_call | solution.py:392
  9.5 1.0 %shard_map.106 = bf16[4,272,128]{2,1,0:T(8,128)(2,1)S(1)} custom-call(bf16[4,272,128]{2,1,0:T(8,128)(2,1)S(1)} %shard_map.105._, f32[40960,128]{1,0:T(8,128)S(1)} %shard_map.104.acc, s32[4,128]{1,0:T(4,128)S(1)} %bitcast.6, bf16[256,128]{1,0:T(8,128)(2,1)S(1)} %copy-done.3, bf16[80,128]{1,0:T(8,128)(2,1)S(1)} %copy-done.5, bf16[16,1024]{1,0:T(8,128)(2,1)S(1)} %copy-done.4), custom_call_target="tpu_custom_call" | custom-call | flops 10000000000 | bytes 1048576 | tf_op jit(solution)/shard_map/pallas_call | solution.py:392
  10.8 3.0 %collective-permute-start.5 = (bf16[2,272,128]{2,1,0:T(8,128)(2,1)S(1)}, bf16[2,272,128]{2,1,0:T(8,128)(2,1)S(1)}, u32[]{:S(2)}, u32[]{:S(2)}) collective-permute-start(bf16[2,272,128]{2,1,0:T(8,128)(2,1)S(1)} %get-tuple-element.21._), channel_id=1, source_target_pairs={{0,2},{1,3},{2,0},{3,1},{4,6},{5,7},{6,4},{7,5},{8,10},{9,11},{10,... | collective-permute-start | bytes 417800 | tf_op jit(solution)/shard_map/ppermute | solution.py:345
  13.7 1.0 %shard_map.107._ = bf16[4,272,128]{2,1,0:T(8,128)(2,1)S(1)} custom-call(bf16[2,272,128]{2,1,0:T(8,128)(2,1)S(1)} %get-tuple-element.21._, f32[40960,128]{1,0:T(8,128)S(1)} %shard_map.104.acc, s32[4,128]{1,0:T(4,128)S(1)} %bitcast.7, bf16[256,128]{1,0:T(8,128)(2,1)S(1)} %copy-done.3, bf16[80,128]{1,0:T(8,128)(2,1)S(1)} %copy-done.5, ...), custom_call_target="tpu_custom_call" | custom-call | flops 10000000000 | bytes 1048576 | tf_op jit(solution)/shard_map/pallas_call | solution.py:392
  14.8 1.0 %shard_map.108 = bf16[4,272,128]{2,1,0:T(8,128)(2,1)S(1)} custom-call(bf16[4,272,128]{2,1,0:T(8,128)(2,1)S(1)} %shard_map.107._, f32[40960,128]{1,0:T(8,128)S(1)} %shard_map.104.acc, s32[4,128]{1,0:T(4,128)S(1)} %bitcast.8, bf16[256,128]{1,0:T(8,128)(2,1)S(1)} %copy-done.3, bf16[80,128]{1,0:T(8,128)(2,1)S(1)} %copy-done.5, bf16[16,1024]{1,0:T(8,128)(2,1)S(1)} %copy-done.4), custom_call_target="tpu_custom_call" | custom-call | flops 10000000000 | bytes 1048576 | tf_op jit(solution)/shard_map/pallas_call | solution.py:392
  15.9 1.5 %collective-permute-start.4 = (bf16[2,272,128]{2,1,0:T(8,128)(2,1)S(1)}, bf16[2,272,128]{2,1,0:T(8,128)(2,1)S(1)}, u32[]{:S(2)}, u32[]{:S(2)}) collective-permute-start(bf16[2,272,128]{2,1,0:T(8,128)(2,1)S(1)} %get-tuple-element.20), channel_id=1, source_target_pairs={{0,6},{1,7},{2,4},{3,5},{4,2},{5,3},{6,0},{7,1},{8,14},{9,15},{10,... | collective-permute-start | bytes 417800 | tf_op jit(solution)/shard_map/ppermute | solution.py:345
  17.4 1.0 %shard_map.109._ = bf16[4,272,128]{2,1,0:T(8,128)(2,1)S(1)} custom-call(bf16[2,272,128]{2,1,0:T(8,128)(2,1)S(1)} %get-tuple-element.19._.refs_3_, f32[40960,128]{1,0:T(8,128)S(1)} %shard_map.104.acc, s32[4,128]{1,0:T(4,128)S(1)} %bitcast.9, bf16[256,128]{1,0:T(8,128)(2,1)S(1)} %copy-done.3, bf16[80,128]{1,0:T(8,128)(2,1)S(1)} %copy-done.5, ...), custom_call_target="tpu_custom_call" | custom-call | flops 10000000000 | bytes 1048576 | tf_op jit(solution)/shard_map/pallas_call | solution.py:392
  18.7 1.0 %shard_map.110 = bf16[4,272,128]{2,1,0:T(8,128)(2,1)S(1)} custom-call(bf16[4,272,128]{2,1,0:T(8,128)(2,1)S(1)} %shard_map.109._, f32[40960,128]{1,0:T(8,128)S(1)} %shard_map.104.acc, s32[4,128]{1,0:T(4,128)S(1)} %bitcast.10, bf16[256,128]{1,0:T(8,128)(2,1)S(1)} %copy-done.3, bf16[80,128]{1,0:T(8,128)(2,1)S(1)} %copy-done.5, bf16[16,1024]{1,0:T(8,128)(2,1)S(1)} %copy-done.4), custom_call_target="tpu_custom_call" | custom-call | flops 10000000000 | bytes 1048576 | tf_op jit(solution)/shard_map/pallas_call | solution.py:392
  19.7 0.5 %collective-permute-start.6 = (bf16[2,272,128]{2,1,0:T(8,128)(2,1)S(1)}, bf16[2,272,128]{2,1,0:T(8,128)(2,1)S(1)}, u32[]{:S(2)}, u32[]{:S(2)}) collective-permute-start(bf16[2,272,128]{2,1,0:T(8,128)(2,1)S(1)} %get-tuple-element.18), channel_id=1, source_target_pairs={{0,4},{1,5},{2,6},{3,7},{4,0},{5,1},{6,2},{7,3},{8,12},{9,13},{10,... | collective-permute-start | bytes 417800 | tf_op jit(solution)/shard_map/ppermute | solution.py:345
  20.3 1.7 %collective-permute-start.8 = (bf16[2,272,128]{2,1,0:T(8,128)(2,1)S(1)}, bf16[2,272,128]{2,1,0:T(8,128)(2,1)S(1)}, u32[]{:S(2)}, u32[]{:S(2)}) collective-permute-start(bf16[2,272,128]{2,1,0:T(8,128)(2,1)S(1)} %get-tuple-element.17._), channel_id=1, source_target_pairs={{0,2},{1,3},{2,0},{3,1},{4,6},{5,7},{6,4},{7,5},{8,10},{9,11},{10,... | collective-permute-start | bytes 417800 | tf_op jit(solution)/shard_map/ppermute | solution.py:345
  22.0 1.0 %shard_map.111._ = bf16[4,272,128]{2,1,0:T(8,128)(2,1)S(1)} custom-call(bf16[2,272,128]{2,1,0:T(8,128)(2,1)S(1)} %get-tuple-element.17._, f32[40960,128]{1,0:T(8,128)S(1)} %shard_map.104.acc, s32[4,128]{1,0:T(4,128)S(1)} %bitcast.11, bf16[256,128]{1,0:T(8,128)(2,1)S(1)} %copy-done.3, bf16[80,128]{1,0:T(8,128)(2,1)S(1)} %copy-done.5, ...), custom_call_target="tpu_custom_call" | custom-call | flops 10000000000 | bytes 1048576 | tf_op jit(solution)/shard_map/pallas_call | solution.py:392
  23.1 1.0 %shard_map.112 = bf16[4,272,128]{2,1,0:T(8,128)(2,1)S(1)} custom-call(bf16[4,272,128]{2,1,0:T(8,128)(2,1)S(1)} %shard_map.111._, f32[40960,128]{1,0:T(8,128)S(1)} %shard_map.104.acc, s32[4,128]{1,0:T(4,128)S(1)} %bitcast.12, bf16[256,128]{1,0:T(8,128)(2,1)S(1)} %copy-done.3, bf16[80,128]{1,0:T(8,128)(2,1)S(1)} %copy-done.5, bf16[16,1024]{1,0:T(8,128)(2,1)S(1)} %copy-done.4), custom_call_target="tpu_custom_call" | custom-call | flops 10000000000 | bytes 1048576 | tf_op jit(solution)/shard_map/pallas_call | solution.py:392
  24.1 0.5 %collective-permute-done.3 = bf16[4,272,128]{2,1,0:T(8,128)(2,1)S(1)} collective-permute-done((bf16[4,272,128]{2,1,0:T(8,128)(2,1)S(1)}, bf16[4,272,128]{2,1,0:T(8,128)(2,1)S(1)}, u32[]{:S(2)}, u32[]{:S(2)}) %collective-permute-start.3) | collective-permute-done | bytes 278560 | tf_op jit(solution)/shard_map/ppermute | solution.py:340
  24.7 1.4 %collective-permute-start.7 = (bf16[2,272,128]{2,1,0:T(8,128)(2,1)S(1)}, bf16[2,272,128]{2,1,0:T(8,128)(2,1)S(1)}, u32[]{:S(2)}, u32[]{:S(2)}) collective-permute-start(bf16[2,272,128]{2,1,0:T(8,128)(2,1)S(1)} %get-tuple-element.16), channel_id=1, source_target_pairs={{0,6},{1,7},{2,4},{3,5},{4,2},{5,3},{6,0},{7,1},{8,14},{9,15},{10,... | collective-permute-start | bytes 417800 | tf_op jit(solution)/shard_map/ppermute | solution.py:345
  26.8 3.7 %collective-permute-start.12 = (bf16[272,128]{1,0:T(8,128)(2,1)S(1)}, bf16[272,128]{1,0:T(8,128)(2,1)S(1)}, u32[]{:S(2)}, u32[]{:S(2)}) collective-permute-start(bf16[272,128]{1,0:T(8,128)(2,1)S(1)} %get-tuple-element.11), channel_id=1, source_target_pairs={{0,24},{4,28},{8,16},{12,20},{16,8},{20,12},{24,0},{28,4},{1,25},{... | collective-permute-start | bytes 208904 | tf_op jit(solution)/shard_map/ppermute | solution.py:340
  30.6 3.0 %shard_map.114._ = bf16[32,256,2,128]{3,2,1,0:T(2,128)(2,1)S(1)} custom-call(bf16[272,128]{1,0:T(8,128)(2,1)S(1)} %get-tuple-element.8._, bf16[256,2,4096]{2,1,0:T(2,128)(2,1)} %block.1), custom_call_target="tpu_custom_call" | custom-call | flops 100000000 | bytes 1048576 | tf_op jit(solution)/shard_map/pallas_call | solution.py:429
  33.7 1.3 %collective-permute-start.10 = (bf16[272,128]{1,0:T(8,128)(2,1)S(1)}, bf16[272,128]{1,0:T(8,128)(2,1)S(1)}, u32[]{:S(2)}, u32[]{:S(2)}) collective-permute-start(bf16[272,128]{1,0:T(8,128)(2,1)S(1)} %get-tuple-element.10), channel_id=1, source_target_pairs={{0,8},{4,12},{8,0},{12,4},{16,24},{20,28},{24,16},{28,20},{1,9},{5... | collective-permute-start | bytes 208904 | tf_op jit(solution)/shard_map/ppermute | solution.py:340
  35.0 1.2 %collective-permute-done.11.refs_2_ = bf16[272,128]{1,0:T(8,128)(2,1)S(1)} collective-permute-done((bf16[272,128]{1,0:T(8,128)(2,1)S(1)}, bf16[272,128]{1,0:T(8,128)(2,1)S(1)}, u32[]{:S(2)}, u32[]{:S(2)}) %collective-permute-start.11) | collective-permute-done | bytes 69664 | tf_op jit(solution)/shard_map/ppermute | solution.py:340
  36.3 1.8 %collective-permute-done.10.refs_1_ = bf16[272,128]{1,0:T(8,128)(2,1)S(1)} collective-permute-done((bf16[272,128]{1,0:T(8,128)(2,1)S(1)}, bf16[272,128]{1,0:T(8,128)(2,1)S(1)}, u32[]{:S(2)}, u32[]{:S(2)}) %collective-permute-start.10) | collective-permute-done | bytes 69664 | tf_op jit(solution)/shard_map/ppermute | solution.py:340
  38.1 1.6 %collective-permute-start.14 = (bf16[272,128]{1,0:T(8,128)(2,1)S(1)}, bf16[272,128]{1,0:T(8,128)(2,1)S(1)}, u32[]{:S(2)}, u32[]{:S(2)}) collective-permute-start(bf16[272,128]{1,0:T(8,128)(2,1)S(1)} %shard_map.117), channel_id=1, source_target_pairs={{0,2},{1,3},{2,0},{3,1},{4,6},{5,7},{6,4},{7,5},{8,10},{9,11},{10,... | collective-permute-start | bytes 208904 | tf_op jit(solution)/shard_map/ppermute | solution.py:340
  39.7 1.3 %shard_map.116 = (f32[8,2,4096]{2,1,0:T(2,128)}, bf16[8,8192]{1,0:T(8,128)(2,1)S(1)}) custom-call(bf16[272,128]{1,0:T(8,128)(2,1)S(1)} %get-tuple-element.9.refs_0_, bf16[272,128]{1,0:T(8,128)(2,1)S(1)} %collective-permute-done.10.refs_1_, bf16[272,128]{1,0:T(8,128)(2,1)S(1)} %collective-permute-done.11.refs_2_, ...), custom_call_target="tpu_custom_call" | custom-call | tf_op jit(solution)/shard_map/pallas_call | solution.py:451
  41.0 1.5 %collective-permute-done.14.refs_1_ = bf16[272,128]{1,0:T(8,128)(2,1)S(1)} collective-permute-done((bf16[272,128]{1,0:T(8,128)(2,1)S(1)}, bf16[272,128]{1,0:T(8,128)(2,1)S(1)}, u32[]{:S(2)}, u32[]{:S(2)}) %collective-permute-start.14) | collective-permute-done | bytes 69664 | tf_op jit(solution)/shard_map/ppermute | solution.py:340
  44.1 2.0 %shard_map.121 = f32[32,256]{1,0:T(8,128)} custom-call(bf16[8,8192]{1,0:T(8,128)(2,1)S(1)} %get-tuple-element.13.refs_0_, bf16[8,8192]{1,0:T(8,128)(2,1)S(1)} %shard_map.118.refs_0_.refs_1_, bf16[8,8192]{1,0:T(8,128)(2,1)S(1)} %shard_map.119.refs_0_.refs_2_, bf16[8,8192]{1,0:T(8,128)(2,1)S(1)} %shard_map.120.refs_3_, bf16[32,512,128]{2,1,0:T(8,128)(2,1)S(1)} %bitcast.3), custom_call_target="tpu_custom_call" | custom-call | tf_op jit(solution)/shard_map/pallas_call | solution.py:480
  (42 shorter events, 3.8 us)
Async XLA Ops:
  0.6 7.3 %copy-start.2 = (s32[512]{0:T(512)S(1)}, s32[512]{0:T(512)}, u32[]{:S(2)}) copy-start(s32[512]{0:T(512)} %class_ids.1) | copy-start | bytes 6148
  0.6 7.3 %copy-start.3 = (bf16[256,128]{1,0:T(8,128)(2,1)S(1)}, bf16[256,128]{1,0:T(8,128)(2,1)}, u32[]{:S(2)}) copy-start(bf16[256,128]{1,0:T(8,128)(2,1)} %constant.10.clone.col) | copy-start | bytes 196612
  0.7 7.3 %copy-start.4 = (bf16[16,1024]{1,0:T(8,128)(2,1)S(1)}, bf16[16,1024]{1,0:T(8,128)(2,1)}, u32[]{:S(2)}) copy-start(bf16[16,1024]{1,0:T(8,128)(2,1)} %constant.12.clone.last) | copy-start | bytes 98308
  0.7 7.3 %copy-start.5 = (bf16[80,128]{1,0:T(8,128)(2,1)S(1)}, bf16[80,128]{1,0:T(8,128)(2,1)}, u32[]{:S(2)}) copy-start(bf16[80,128]{1,0:T(8,128)(2,1)} %constant.11.clone.row) | copy-start | bytes 61444
  9.0 1.7 %collective-permute-start = (bf16[4,272,128]{2,1,0:T(8,128)(2,1)S(1)}, bf16[4,272,128]{2,1,0:T(8,128)(2,1)S(1)}, u32[]{:S(2)}, u32[]{:S(2)}) collective-permute-start(bf16[4,272,128]{2,1,0:T(8,128)(2,1)S(1)} %shard_map.105._), channel_id=1, source_target_pairs={{0,1},{1,0},{2,3},{3,2},{4,5},{5,4},{6,7},{7,6},{8,9},{9,8},{10,11... | collective-permute-start | bytes 835592 | tf_op jit(solution)/shard_map/ppermute | solution.py:340
  10.8 15.9 %collective-permute-start.5 = (bf16[2,272,128]{2,1,0:T(8,128)(2,1)S(1)}, bf16[2,272,128]{2,1,0:T(8,128)(2,1)S(1)}, u32[]{:S(2)}, u32[]{:S(2)}) collective-permute-start(bf16[2,272,128]{2,1,0:T(8,128)(2,1)S(1)} %get-tuple-element.21._), channel_id=1, source_target_pairs={{0,2},{1,3},{2,0},{3,1},{4,6},{5,7},{6,4},{7,5},{8,10},{9,11},{10,... | collective-permute-start | bytes 417800 | tf_op jit(solution)/shard_map/ppermute | solution.py:345
  14.8 2.6 %collective-permute-start.1 = (bf16[4,272,128]{2,1,0:T(8,128)(2,1)S(1)}, bf16[4,272,128]{2,1,0:T(8,128)(2,1)S(1)}, u32[]{:S(2)}, u32[]{:S(2)}) collective-permute-start(bf16[4,272,128]{2,1,0:T(8,128)(2,1)S(1)} %shard_map.107._), channel_id=1, source_target_pairs={{0,1},{1,0},{2,3},{3,2},{4,5},{5,4},{6,7},{7,6},{8,9},{9,8},{10,11... | collective-permute-start | bytes 835592 | tf_op jit(solution)/shard_map/ppermute | solution.py:340
  15.9 10.3 %collective-permute-start.4 = (bf16[2,272,128]{2,1,0:T(8,128)(2,1)S(1)}, bf16[2,272,128]{2,1,0:T(8,128)(2,1)S(1)}, u32[]{:S(2)}, u32[]{:S(2)}) collective-permute-start(bf16[2,272,128]{2,1,0:T(8,128)(2,1)S(1)} %get-tuple-element.20), channel_id=1, source_target_pairs={{0,6},{1,7},{2,4},{3,5},{4,2},{5,3},{6,0},{7,1},{8,14},{9,15},{10,... | collective-permute-start | bytes 417800 | tf_op jit(solution)/shard_map/ppermute | solution.py:345
  18.5 1.8 %collective-permute-start.2 = (bf16[4,272,128]{2,1,0:T(8,128)(2,1)S(1)}, bf16[4,272,128]{2,1,0:T(8,128)(2,1)S(1)}, u32[]{:S(2)}, u32[]{:S(2)}) collective-permute-start(bf16[4,272,128]{2,1,0:T(8,128)(2,1)S(1)} %shard_map.109._), channel_id=1, source_target_pairs={{0,1},{1,0},{2,3},{3,2},{4,5},{5,4},{6,7},{7,6},{8,9},{9,8},{10,11... | collective-permute-start | bytes 835592 | tf_op jit(solution)/shard_map/ppermute | solution.py:340
  19.7 7.0 %collective-permute-start.6 = (bf16[2,272,128]{2,1,0:T(8,128)(2,1)S(1)}, bf16[2,272,128]{2,1,0:T(8,128)(2,1)S(1)}, u32[]{:S(2)}, u32[]{:S(2)}) collective-permute-start(bf16[2,272,128]{2,1,0:T(8,128)(2,1)S(1)} %get-tuple-element.18), channel_id=1, source_target_pairs={{0,4},{1,5},{2,6},{3,7},{4,0},{5,1},{6,2},{7,3},{8,12},{9,13},{10,... | collective-permute-start | bytes 417800 | tf_op jit(solution)/shard_map/ppermute | solution.py:345
  20.3 13.2 %collective-permute-start.8 = (bf16[2,272,128]{2,1,0:T(8,128)(2,1)S(1)}, bf16[2,272,128]{2,1,0:T(8,128)(2,1)S(1)}, u32[]{:S(2)}, u32[]{:S(2)}) collective-permute-start(bf16[2,272,128]{2,1,0:T(8,128)(2,1)S(1)} %get-tuple-element.17._), channel_id=1, source_target_pairs={{0,2},{1,3},{2,0},{3,1},{4,6},{5,7},{6,4},{7,5},{8,10},{9,11},{10,... | collective-permute-start | bytes 417800 | tf_op jit(solution)/shard_map/ppermute | solution.py:345
  23.0 16.7 %copy-start = (bf16[128,256]{1,0:T(8,128)(2,1)S(1)}, bf16[128,256]{1,0:T(8,128)(2,1)}, u32[]{:S(2)}) copy-start(bf16[128,256]{1,0:T(8,128)(2,1)} %constant.13.clone.refs_4_.refs_2_) | copy-start | bytes 196612
  23.0 16.7 %copy-start.1 = (f32[32,128]{1,0:T(8,128)S(1)}, f32[32,128]{1,0:T(8,128)}, u32[]{:S(2)}) copy-start(f32[32,128]{1,0:T(8,128)} %constant.14.clone.refs_5_.refs_3_) | copy-start | bytes 49156
  23.0 1.6 %collective-permute-start.3 = (bf16[4,272,128]{2,1,0:T(8,128)(2,1)S(1)}, bf16[4,272,128]{2,1,0:T(8,128)(2,1)S(1)}, u32[]{:S(2)}, u32[]{:S(2)}) collective-permute-start(bf16[4,272,128]{2,1,0:T(8,128)(2,1)S(1)} %shard_map.111._), channel_id=1, source_target_pairs={{0,1},{1,0},{2,3},{3,2},{4,5},{5,4},{6,7},{7,6},{8,9},{9,8},{10,11... | collective-permute-start | bytes 835592 | tf_op jit(solution)/shard_map/ppermute | solution.py:340
  24.7 8.9 %collective-permute-start.7 = (bf16[2,272,128]{2,1,0:T(8,128)(2,1)S(1)}, bf16[2,272,128]{2,1,0:T(8,128)(2,1)S(1)}, u32[]{:S(2)}, u32[]{:S(2)}) collective-permute-start(bf16[2,272,128]{2,1,0:T(8,128)(2,1)S(1)} %get-tuple-element.16), channel_id=1, source_target_pairs={{0,6},{1,7},{2,4},{3,5},{4,2},{5,3},{6,0},{7,1},{8,14},{9,15},{10,... | collective-permute-start | bytes 417800 | tf_op jit(solution)/shard_map/ppermute | solution.py:345
  26.2 7.4 %collective-permute-start.9 = (bf16[2,272,128]{2,1,0:T(8,128)(2,1)S(1)}, bf16[2,272,128]{2,1,0:T(8,128)(2,1)S(1)}, u32[]{:S(2)}, u32[]{:S(2)}) collective-permute-start(bf16[2,272,128]{2,1,0:T(8,128)(2,1)S(1)} %get-tuple-element.14), channel_id=1, source_target_pairs={{0,4},{1,5},{2,6},{3,7},{4,0},{5,1},{6,2},{7,3},{8,12},{9,13},{10,... | collective-permute-start | bytes 417800 | tf_op jit(solution)/shard_map/ppermute | solution.py:345
  26.8 8.2 %collective-permute-start.12 = (bf16[272,128]{1,0:T(8,128)(2,1)S(1)}, bf16[272,128]{1,0:T(8,128)(2,1)S(1)}, u32[]{:S(2)}, u32[]{:S(2)}) collective-permute-start(bf16[272,128]{1,0:T(8,128)(2,1)S(1)} %get-tuple-element.11), channel_id=1, source_target_pairs={{0,24},{4,28},{8,16},{12,20},{16,8},{20,12},{24,0},{28,4},{1,25},{... | collective-permute-start | bytes 208904 | tf_op jit(solution)/shard_map/ppermute | solution.py:340
  30.6 5.7 %collective-permute-start.11 = (bf16[272,128]{1,0:T(8,128)(2,1)S(1)}, bf16[272,128]{1,0:T(8,128)(2,1)S(1)}, u32[]{:S(2)}, u32[]{:S(2)}) collective-permute-start(bf16[272,128]{1,0:T(8,128)(2,1)S(1)} %get-tuple-element.8._), channel_id=1, source_target_pairs={{0,16},{4,20},{8,24},{12,28},{16,0},{20,4},{24,8},{28,12},{1,17},{... | collective-permute-start | bytes 208904 | tf_op jit(solution)/shard_map/ppermute | solution.py:340
  33.7 4.4 %collective-permute-start.10 = (bf16[272,128]{1,0:T(8,128)(2,1)S(1)}, bf16[272,128]{1,0:T(8,128)(2,1)S(1)}, u32[]{:S(2)}, u32[]{:S(2)}) collective-permute-start(bf16[272,128]{1,0:T(8,128)(2,1)S(1)} %get-tuple-element.10), channel_id=1, source_target_pairs={{0,8},{4,12},{8,0},{12,4},{16,24},{20,28},{24,16},{28,20},{1,9},{5... | collective-permute-start | bytes 208904 | tf_op jit(solution)/shard_map/ppermute | solution.py:340
  38.1 4.4 %collective-permute-start.14 = (bf16[272,128]{1,0:T(8,128)(2,1)S(1)}, bf16[272,128]{1,0:T(8,128)(2,1)S(1)}, u32[]{:S(2)}, u32[]{:S(2)}) collective-permute-start(bf16[272,128]{1,0:T(8,128)(2,1)S(1)} %shard_map.117), channel_id=1, source_target_pairs={{0,2},{1,3},{2,0},{3,1},{4,6},{5,7},{6,4},{7,5},{8,10},{9,11},{10,... | collective-permute-start | bytes 208904 | tf_op jit(solution)/shard_map/ppermute | solution.py:340
  39.7 2.8 %collective-permute-start.13 = (bf16[272,128]{1,0:T(8,128)(2,1)S(1)}, bf16[272,128]{1,0:T(8,128)(2,1)S(1)}, u32[]{:S(2)}, u32[]{:S(2)}) collective-permute-start(bf16[272,128]{1,0:T(8,128)(2,1)S(1)} %shard_map.117), channel_id=1, source_target_pairs={{0,1},{1,0},{2,3},{3,2},{4,5},{5,4},{6,7},{7,6},{8,9},{9,8},{10,11... | collective-permute-start | bytes 208904 | tf_op jit(solution)/shard_map/ppermute | solution.py:340
  42.5 1.3 %collective-permute-start.15 = (bf16[272,128]{1,0:T(8,128)(2,1)S(1)}, bf16[272,128]{1,0:T(8,128)(2,1)S(1)}, u32[]{:S(2)}, u32[]{:S(2)}) collective-permute-start(bf16[272,128]{1,0:T(8,128)(2,1)S(1)} %collective-permute-done.14.refs_1_), channel_id=1, source_target_pairs={{0,1},{1,0},{2,3},{3,2},{4,5},{5,4},{6,7},{7,6},{8,9},{9,8},{10,11... | collective-permute-start | bytes 208904 | tf_op jit(solution)/shard_map/ppermute | solution.py:340

commit v5 on v4

--- a/solution.py
+++ b/solution.py
@@ -195,9 +195,11 @@
     lax.fori_loop(0, count // together, some, 0)
 
 
-def regroup_kernel(_, block, fresh, sems):
+def regroup_kernel(_, block, fresh, sems, *, first):
     copies = [
-        pltpu.make_async_copy(block.at[:, :, pl.ds(f * PIX, PIX)], fresh.at[f], sems.at[f])
+        pltpu.make_async_copy(
+            block.at[:, :, pl.ds((first + f) * PIX, PIX)], fresh.at[f], sems.at[f]
+        )
         for f in range(fresh.shape[0])
     ]
     for copy in copies:
@@ -221,7 +223,7 @@
     return total
 
 
-def added_kernel(*refs):
+def added_kernel(_, *refs):
     refs[-1][...] = added(refs[:-1]).astype(jnp.bfloat16)
 
 
@@ -360,7 +362,7 @@
     hbm = pl.BlockSpec(memory_space=pltpu.HBM)
     anywhere = pl.BlockSpec(memory_space=pl.ANY)
     flat = BAND * BAND
-    spans = flat // PIX
+    spans = flat // PIX // 2
     fresh_count = next_block.shape[0]
 
     def put(space, *arrays):
@@ -413,6 +415,18 @@
                 part = part.astype(jnp.bfloat16)
                 met[first].append(hop(part, near, groups) if near else part)
             done = part
+    def regroup(after, first):
+        return pl.pallas_call(
+            functools.partial(regroup_kernel, first=first),
+            out_shape=pltpu.VMEM((spans, fresh_count, 2, PIX), jnp.bfloat16),
+            in_specs=[anywhere, hbm],
+            out_specs=vmem,
+            scratch_shapes=[pltpu.SemaphoreType.DMA((spans,))],
+            compiler_params=pltpu.CompilerParams(vmem_limit_bytes=8 * MIB),
+            cost_estimate=pl.CostEstimate(flops=10**8, bytes_accessed=MIB, transcendentals=0),
+        )(after, block)
+
+    fresh = []
     pieces = [None] * fars
     for first in (half, 0):
         totals = pl.pallas_call(
@@ -425,24 +439,15 @@
         for r, total in enumerate(totals):
             far = first + r
             pieces[far] = swap(total, "dp", far << 1) if far else total
-        if first:
-            fresh = pl.pallas_call(
-                regroup_kernel,
-                out_shape=pltpu.VMEM((spans, fresh_count, 2, PIX), jnp.bfloat16),
-                in_specs=[anywhere, hbm],
-                out_specs=vmem,
-                scratch_shapes=[pltpu.SemaphoreType.DMA((spans,))],
-                compiler_params=pltpu.CompilerParams(vmem_limit_bytes=8 * MIB),
-                cost_estimate=pl.CostEstimate(flops=10**8, bytes_accessed=MIB, transcendentals=0),
-            )(totals[0], block)
-            done = fresh
+        done = regroup(totals[0], len(fresh) * spans)
+        fresh.append(done)
     summed = pl.pallas_call(
         added_kernel,
         out_shape=jax.ShapeDtypeStruct((block_rows, PIX), jnp.bfloat16),
-        in_specs=[vmem] * fars,
+        in_specs=[anywhere] + [vmem] * fars,
         out_specs=vmem,
         compiler_params=pltpu.CompilerParams(vmem_limit_bytes=8 * MIB),
-    )(*put(pltpu.VMEM, *pieces))
+    )(done, *put(pltpu.VMEM, *pieces))
     final_tables = jnp.asarray(expand_table()), jnp.asarray(filter_table())
     spread_scratch = [
         pltpu.VMEM((TILE * BAND, PIX), jnp.float32),
@@ -476,7 +481,7 @@
         across = swap(summed, "grp", k)
         held.append(references(held[-1], across))
         held.append(references(held[-1], swap(across, "grp", 1)))
-    fresh = [fresh.reshape(spans, 2 * fresh_count, PIX)]
+    fresh = [f.reshape(spans, 2 * fresh_count, PIX) for f in fresh]
     scores = pl.pallas_call(
         functools.partial(scores_kernel, own=own, groups=groups),
         out_shape=jax.ShapeDtypeStruct((own * groups, fresh_count), jnp.float32),

time: 46.3 us -> 45.9 us (level)
  waiting for transfers between devices: 5.75 us -> 3.92 us
  Pallas kernels: 23 us -> 23.9 us
  starting transfers between devices: 16.2 us -> 16.7 us
    ppermute x10, waiting for transfers between devices: 5.73 us -> 3.24 us  [swap(): return lax.ppermute(array, axis, [(i, i ^ flip) for i in range(size)])]
    pallas_call x1 -> x2, Pallas kernels: 3.02 us -> 3.99 us  [regroup(): pl.pallas_call(functools.partial(regroup_kernel, first=first), out_shape=...]
    ppermute x6, waiting for transfers between devices: 0.02 us -> 0.69 us  [hop(): lax.ppermute(array, ('dp', 'grp'), [(i, i ^ ((near & 1) * groups | (near...]
    ppermute x10, starting transfers between devices: 7.59 us -> 8.06 us  [swap(): return lax.ppermute(array, axis, [(i, i ^ flip) for i in range(size)])]
  transfers between devices with their start and end apart: 16 -> 16, of which waited for: 6 -> 6; matrix products, arithmetic and copies ran while one was open for 1% -> 1% of each run, Pallas kernels for 27% -> 29%
where the time goes in v5:
time: 45.9 us; the launch traced here: 45.7 us
  Pallas kernels  23.9 us (52%)
  starting transfers between devices  16.7 us (36%)
  waiting for transfers between devices  3.92 us (9%)
  between operations  0.86 us (2%)
    ppermute x6, starting transfers between devices, hop(): lax.ppermute(array, ('dp', 'grp'), [(i, i ^ ((near & 1) * groups | (near...  8.6 us
    pallas_call x8, Pallas kernels, transform(): pl.pallas_call(functools.partial(transform_kernel, jobs=jobs, other=other...  8.09 us
    ppermute x10, starting transfers between devices, swap(): return lax.ppermute(array, axis, [(i, i ^ flip) for i in range(size)])  8.06 us
    pallas_call x1, Pallas kernels, body(): pl.pallas_call(sums_kernel, out_shape=pltpu.VMEM((CLASSES * SLAB, PIX), j...  7.26 us
    pallas_call x2, Pallas kernels, regroup(): pl.pallas_call(functools.partial(regroup_kernel, first=first), out_shape=...  3.99 us
    ppermute x10, waiting for transfers between devices, swap(): return lax.ppermute(array, axis, [(i, i ^ flip) for i in range(size)])  3.24 us
    pallas_call x1, Pallas kernels, body(): pl.pallas_call(functools.partial(scores_kernel, own=own, groups=groups),...  2 us
    pallas_call x1, Pallas kernels, body(): pl.pallas_call(functools.partial(averages_kernel, own=own, parts=fars), o...  1.33 us
  transfers between devices with their start and end apart: 16, of which 6 were waited for; matrix products, arithmetic and copies ran while one was open for 1% of the time, Pallas kernels for 29%

profile of v5, /device:TPU:0, one launch (start us, length us, event | category | flops | bytes accessed | tf_op | source)
XLA Modules:
  0.0 45.7 jit_solution(12230054899912125078)
XLA Ops:
  0.7 7.3 %shard_map.104.acc = f32[40960,128]{1,0:T(8,128)S(1)} custom-call(s32[512]{0:T(512)} %class_ids.1, s32[2,512]{1,0:T(2,128)} %bitcast.15, bf16[512,128,128]{2,1,0:T(8,128)(2,1)} %images.1), custom_call_target="tpu_custom_call" | custom-call | tf_op jit(solution)/shard_map/pallas_call | solution.py:371
  8.0 1.0 %shard_map.105._ = bf16[4,272,128]{2,1,0:T(8,128)(2,1)S(1)} custom-call(s32[4,128]{1,0:T(4,128)S(1)} %bitcast.6, f32[40960,128]{1,0:T(8,128)S(1)} %shard_map.104.acc, s32[4,128]{1,0:T(4,128)S(1)} %bitcast.7, bf16[256,128]{1,0:T(8,128)(2,1)S(1)} %copy-done.3, bf16[80,128]{1,0:T(8,128)(2,1)S(1)} %copy-done.5, bf16[16,1024]{1,0:T(8,128)(2,1)S(1)} %copy-done.4), custom_call_target="tpu_custom_call" | custom-call | flops 10000000000 | bytes 1048576 | tf_op jit(solution)/shard_map/pallas_call | solution.py:394
  9.5 1.0 %shard_map.106 = bf16[4,272,128]{2,1,0:T(8,128)(2,1)S(1)} custom-call(bf16[4,272,128]{2,1,0:T(8,128)(2,1)S(1)} %shard_map.105._, f32[40960,128]{1,0:T(8,128)S(1)} %shard_map.104.acc, s32[4,128]{1,0:T(4,128)S(1)} %bitcast.8, bf16[256,128]{1,0:T(8,128)(2,1)S(1)} %copy-done.3, bf16[80,128]{1,0:T(8,128)(2,1)S(1)} %copy-done.5, bf16[16,1024]{1,0:T(8,128)(2,1)S(1)} %copy-done.4), custom_call_target="tpu_custom_call" | custom-call | flops 10000000000 | bytes 1048576 | tf_op jit(solution)/shard_map/pallas_call | solution.py:394
  10.8 3.0 %collective-permute-start.5 = (bf16[2,272,128]{2,1,0:T(8,128)(2,1)S(1)}, bf16[2,272,128]{2,1,0:T(8,128)(2,1)S(1)}, u32[]{:S(2)}, u32[]{:S(2)}) collective-permute-start(bf16[2,272,128]{2,1,0:T(8,128)(2,1)S(1)} %get-tuple-element.21._), channel_id=1, source_target_pairs={{0,2},{1,3},{2,0},{3,1},{4,6},{5,7},{6,4},{7,5},{8,10},{9,11},{10,... | collective-permute-start | bytes 417800 | tf_op jit(solution)/shard_map/ppermute | solution.py:347
  13.8 1.0 %shard_map.107._ = bf16[4,272,128]{2,1,0:T(8,128)(2,1)S(1)} custom-call(bf16[2,272,128]{2,1,0:T(8,128)(2,1)S(1)} %get-tuple-element.21._, f32[40960,128]{1,0:T(8,128)S(1)} %shard_map.104.acc, s32[4,128]{1,0:T(4,128)S(1)} %bitcast.9, bf16[256,128]{1,0:T(8,128)(2,1)S(1)} %copy-done.3, bf16[80,128]{1,0:T(8,128)(2,1)S(1)} %copy-done.5, ...), custom_call_target="tpu_custom_call" | custom-call | flops 10000000000 | bytes 1048576 | tf_op jit(solution)/shard_map/pallas_call | solution.py:394
  14.8 1.0 %shard_map.108 = bf16[4,272,128]{2,1,0:T(8,128)(2,1)S(1)} custom-call(bf16[4,272,128]{2,1,0:T(8,128)(2,1)S(1)} %shard_map.107._, f32[40960,128]{1,0:T(8,128)S(1)} %shard_map.104.acc, s32[4,128]{1,0:T(4,128)S(1)} %bitcast.10, bf16[256,128]{1,0:T(8,128)(2,1)S(1)} %copy-done.3, bf16[80,128]{1,0:T(8,128)(2,1)S(1)} %copy-done.5, bf16[16,1024]{1,0:T(8,128)(2,1)S(1)} %copy-done.4), custom_call_target="tpu_custom_call" | custom-call | flops 10000000000 | bytes 1048576 | tf_op jit(solution)/shard_map/pallas_call | solution.py:394
  15.9 1.5 %collective-permute-start.4 = (bf16[2,272,128]{2,1,0:T(8,128)(2,1)S(1)}, bf16[2,272,128]{2,1,0:T(8,128)(2,1)S(1)}, u32[]{:S(2)}, u32[]{:S(2)}) collective-permute-start(bf16[2,272,128]{2,1,0:T(8,128)(2,1)S(1)} %get-tuple-element.20), channel_id=1, source_target_pairs={{0,6},{1,7},{2,4},{3,5},{4,2},{5,3},{6,0},{7,1},{8,14},{9,15},{10,... | collective-permute-start | bytes 417800 | tf_op jit(solution)/shard_map/ppermute | solution.py:347
  17.4 1.0 %shard_map.109._ = bf16[4,272,128]{2,1,0:T(8,128)(2,1)S(1)} custom-call(bf16[2,272,128]{2,1,0:T(8,128)(2,1)S(1)} %get-tuple-element.19._.refs_3_, f32[40960,128]{1,0:T(8,128)S(1)} %shard_map.104.acc, s32[4,128]{1,0:T(4,128)S(1)} %bitcast.11, bf16[256,128]{1,0:T(8,128)(2,1)S(1)} %copy-done.3, bf16[80,128]{1,0:T(8,128)(2,1)S(1)} %copy-done.5, ...), custom_call_target="tpu_custom_call" | custom-call | flops 10000000000 | bytes 1048576 | tf_op jit(solution)/shard_map/pallas_call | solution.py:394
  18.7 1.0 %shard_map.110 = bf16[4,272,128]{2,1,0:T(8,128)(2,1)S(1)} custom-call(bf16[4,272,128]{2,1,0:T(8,128)(2,1)S(1)} %shard_map.109._, f32[40960,128]{1,0:T(8,128)S(1)} %shard_map.104.acc, s32[4,128]{1,0:T(4,128)S(1)} %bitcast.12, bf16[256,128]{1,0:T(8,128)(2,1)S(1)} %copy-done.3, bf16[80,128]{1,0:T(8,128)(2,1)S(1)} %copy-done.5, bf16[16,1024]{1,0:T(8,128)(2,1)S(1)} %copy-done.4), custom_call_target="tpu_custom_call" | custom-call | flops 10000000000 | bytes 1048576 | tf_op jit(solution)/shard_map/pallas_call | solution.py:394
  20.4 1.7 %collective-permute-start.8 = (bf16[2,272,128]{2,1,0:T(8,128)(2,1)S(1)}, bf16[2,272,128]{2,1,0:T(8,128)(2,1)S(1)}, u32[]{:S(2)}, u32[]{:S(2)}) collective-permute-start(bf16[2,272,128]{2,1,0:T(8,128)(2,1)S(1)} %get-tuple-element.17._), channel_id=1, source_target_pairs={{0,2},{1,3},{2,0},{3,1},{4,6},{5,7},{6,4},{7,5},{8,10},{9,11},{10,... | collective-permute-start | bytes 417800 | tf_op jit(solution)/shard_map/ppermute | solution.py:347
  22.0 1.0 %shard_map.111._ = bf16[4,272,128]{2,1,0:T(8,128)(2,1)S(1)} custom-call(bf16[2,272,128]{2,1,0:T(8,128)(2,1)S(1)} %get-tuple-element.17._, f32[40960,128]{1,0:T(8,128)S(1)} %shard_map.104.acc, s32[4,128]{1,0:T(4,128)S(1)} %bitcast.13, bf16[256,128]{1,0:T(8,128)(2,1)S(1)} %copy-done.3, bf16[80,128]{1,0:T(8,128)(2,1)S(1)} %copy-done.5, ...), custom_call_target="tpu_custom_call" | custom-call | flops 10000000000 | bytes 1048576 | tf_op jit(solution)/shard_map/pallas_call | solution.py:394
  23.1 1.0 %shard_map.112 = bf16[4,272,128]{2,1,0:T(8,128)(2,1)S(1)} custom-call(bf16[4,272,128]{2,1,0:T(8,128)(2,1)S(1)} %shard_map.111._, f32[40960,128]{1,0:T(8,128)S(1)} %shard_map.104.acc, s32[4,128]{1,0:T(4,128)S(1)} %bitcast.14, bf16[256,128]{1,0:T(8,128)(2,1)S(1)} %copy-done.3, bf16[80,128]{1,0:T(8,128)(2,1)S(1)} %copy-done.5, bf16[16,1024]{1,0:T(8,128)(2,1)S(1)} %copy-done.4), custom_call_target="tpu_custom_call" | custom-call | flops 10000000000 | bytes 1048576 | tf_op jit(solution)/shard_map/pallas_call | solution.py:394
  24.6 1.4 %collective-permute-start.7 = (bf16[2,272,128]{2,1,0:T(8,128)(2,1)S(1)}, bf16[2,272,128]{2,1,0:T(8,128)(2,1)S(1)}, u32[]{:S(2)}, u32[]{:S(2)}) collective-permute-start(bf16[2,272,128]{2,1,0:T(8,128)(2,1)S(1)} %get-tuple-element.16), channel_id=1, source_target_pairs={{0,6},{1,7},{2,4},{3,5},{4,2},{5,3},{6,0},{7,1},{8,14},{9,15},{10,... | collective-permute-start | bytes 417800 | tf_op jit(solution)/shard_map/ppermute | solution.py:347
  26.2 0.5 %collective-permute-start.9 = (bf16[2,272,128]{2,1,0:T(8,128)(2,1)S(1)}, bf16[2,272,128]{2,1,0:T(8,128)(2,1)S(1)}, u32[]{:S(2)}, u32[]{:S(2)}) collective-permute-start(bf16[2,272,128]{2,1,0:T(8,128)(2,1)S(1)} %get-tuple-element.14), channel_id=1, source_target_pairs={{0,4},{1,5},{2,6},{3,7},{4,0},{5,1},{6,2},{7,3},{8,12},{9,13},{10,... | collective-permute-start | bytes 417800 | tf_op jit(solution)/shard_map/ppermute | solution.py:347
  26.8 3.7 %collective-permute-start.12 = (bf16[272,128]{1,0:T(8,128)(2,1)S(1)}, bf16[272,128]{1,0:T(8,128)(2,1)S(1)}, u32[]{:S(2)}, u32[]{:S(2)}) collective-permute-start(bf16[272,128]{1,0:T(8,128)(2,1)S(1)} %get-tuple-element.11), channel_id=1, source_target_pairs={{0,24},{4,28},{8,16},{12,20},{16,8},{20,12},{24,0},{28,4},{1,25},{... | collective-permute-start | bytes 208904 | tf_op jit(solution)/shard_map/ppermute | solution.py:342
  30.5 2.0 %shard_map.114._ = bf16[16,256,2,128]{3,2,1,0:T(2,128)(2,1)S(1)} custom-call(bf16[272,128]{1,0:T(8,128)(2,1)S(1)} %get-tuple-element.8._, bf16[256,2,4096]{2,1,0:T(2,128)(2,1)} %block.3), custom_call_target="tpu_custom_call" | custom-call | flops 100000000 | bytes 1048576 | tf_op jit(solution)/shard_map/pallas_call | solution.py:419
  32.5 0.7 %collective-permute-done.9.refs_2_ = bf16[2,272,128]{2,1,0:T(8,128)(2,1)S(1)} collective-permute-done((bf16[2,272,128]{2,1,0:T(8,128)(2,1)S(1)}, bf16[2,272,128]{2,1,0:T(8,128)(2,1)S(1)}, u32[]{:S(2)}, u32[]{:S(2)}) %collective-permute-start.9) | collective-permute-done | bytes 139296 | tf_op jit(solution)/shard_map/ppermute | solution.py:347
  33.3 1.7 %collective-permute-start.10 = (bf16[272,128]{1,0:T(8,128)(2,1)S(1)}, bf16[272,128]{1,0:T(8,128)(2,1)S(1)}, u32[]{:S(2)}, u32[]{:S(2)}) collective-permute-start(bf16[272,128]{1,0:T(8,128)(2,1)S(1)} %get-tuple-element.10), channel_id=1, source_target_pairs={{0,8},{4,12},{8,0},{12,4},{16,24},{20,28},{24,16},{28,20},{1,9},{5... | collective-permute-start | bytes 208904 | tf_op jit(solution)/shard_map/ppermute | solution.py:342
  35.0 2.0 %shard_map.117._ = bf16[16,256,2,128]{3,2,1,0:T(2,128)(2,1)S(1)} custom-call(bf16[272,128]{1,0:T(8,128)(2,1)S(1)} %get-tuple-element.9.refs_0_._, bf16[256,2,4096]{2,1,0:T(2,128)(2,1)} %block.3), custom_call_target="tpu_custom_call" | custom-call | flops 100000000 | bytes 1048576 | tf_op jit(solution)/shard_map/pallas_call | solution.py:419
  37.1 0.6 %collective-permute-done.10.refs_1_ = bf16[272,128]{1,0:T(8,128)(2,1)S(1)} collective-permute-done((bf16[272,128]{1,0:T(8,128)(2,1)S(1)}, bf16[272,128]{1,0:T(8,128)(2,1)S(1)}, u32[]{:S(2)}, u32[]{:S(2)}) %collective-permute-start.10) | collective-permute-done | bytes 69664 | tf_op jit(solution)/shard_map/ppermute | solution.py:342
  37.7 1.7 %collective-permute-start.14 = (bf16[272,128]{1,0:T(8,128)(2,1)S(1)}, bf16[272,128]{1,0:T(8,128)(2,1)S(1)}, u32[]{:S(2)}, u32[]{:S(2)}) collective-permute-start(bf16[272,128]{1,0:T(8,128)(2,1)S(1)} %shard_map.118), channel_id=1, source_target_pairs={{0,2},{1,3},{2,0},{3,1},{4,6},{5,7},{6,4},{7,5},{8,10},{9,11},{10,... | collective-permute-start | bytes 208904 | tf_op jit(solution)/shard_map/ppermute | solution.py:342
  39.4 1.3 %shard_map.116 = (f32[8,2,4096]{2,1,0:T(2,128)}, bf16[8,8192]{1,0:T(8,128)(2,1)S(1)}) custom-call(bf16[272,128]{1,0:T(8,128)(2,1)S(1)} %get-tuple-element.9.refs_0_._, bf16[272,128]{1,0:T(8,128)(2,1)S(1)} %collective-permute-done.10.refs_1_, bf16[272,128]{1,0:T(8,128)(2,1)S(1)} %collective-permute-done.11.refs_2_, ...), custom_call_target="tpu_custom_call" | custom-call | tf_op jit(solution)/shard_map/pallas_call | solution.py:456
  40.7 1.4 %collective-permute-done.14.refs_1_ = bf16[272,128]{1,0:T(8,128)(2,1)S(1)} collective-permute-done((bf16[272,128]{1,0:T(8,128)(2,1)S(1)}, bf16[272,128]{1,0:T(8,128)(2,1)S(1)}, u32[]{:S(2)}, u32[]{:S(2)}) %collective-permute-start.14) | collective-permute-done | bytes 69664 | tf_op jit(solution)/shard_map/ppermute | solution.py:342
  43.7 2.0 %shard_map.122 = f32[32,256]{1,0:T(8,128)} custom-call(bf16[8,8192]{1,0:T(8,128)(2,1)S(1)} %get-tuple-element.13.refs_0_, bf16[8,8192]{1,0:T(8,128)(2,1)S(1)} %shard_map.119.refs_0_.refs_1_, bf16[8,8192]{1,0:T(8,128)(2,1)S(1)} %shard_map.120.refs_0_.refs_2_, bf16[8,8192]{1,0:T(8,128)(2,1)S(1)} %shard_map.121.refs_3_, bf16[16,512,128]{2,1,0:T(8,128)(2,1)S(1)} %bitcast.4, ...), custom_call_target="tpu_custom_call" | custom-call | tf_op jit(solution)/shard_map/pallas_call | solution.py:485
  (43 shorter events, 4.3 us)
Async XLA Ops:
  0.6 7.3 %copy-start.2 = (s32[512]{0:T(512)S(1)}, s32[512]{0:T(512)}, u32[]{:S(2)}) copy-start(s32[512]{0:T(512)} %class_ids.1) | copy-start | bytes 6148
  0.6 7.3 %copy-start.3 = (bf16[256,128]{1,0:T(8,128)(2,1)S(1)}, bf16[256,128]{1,0:T(8,128)(2,1)}, u32[]{:S(2)}) copy-start(bf16[256,128]{1,0:T(8,128)(2,1)} %constant.10.clone.col) | copy-start | bytes 196612
  0.7 7.3 %copy-start.4 = (bf16[16,1024]{1,0:T(8,128)(2,1)S(1)}, bf16[16,1024]{1,0:T(8,128)(2,1)}, u32[]{:S(2)}) copy-start(bf16[16,1024]{1,0:T(8,128)(2,1)} %constant.12.clone.last) | copy-start | bytes 98308
  0.7 7.3 %copy-start.5 = (bf16[80,128]{1,0:T(8,128)(2,1)S(1)}, bf16[80,128]{1,0:T(8,128)(2,1)}, u32[]{:S(2)}) copy-start(bf16[80,128]{1,0:T(8,128)(2,1)} %constant.11.clone.row) | copy-start | bytes 61444
  9.0 1.7 %collective-permute-start = (bf16[4,272,128]{2,1,0:T(8,128)(2,1)S(1)}, bf16[4,272,128]{2,1,0:T(8,128)(2,1)S(1)}, u32[]{:S(2)}, u32[]{:S(2)}) collective-permute-start(bf16[4,272,128]{2,1,0:T(8,128)(2,1)S(1)} %shard_map.105._), channel_id=1, source_target_pairs={{0,1},{1,0},{2,3},{3,2},{4,5},{5,4},{6,7},{7,6},{8,9},{9,8},{10,11... | collective-permute-start | bytes 835592 | tf_op jit(solution)/shard_map/ppermute | solution.py:342
  10.8 15.9 %collective-permute-start.5 = (bf16[2,272,128]{2,1,0:T(8,128)(2,1)S(1)}, bf16[2,272,128]{2,1,0:T(8,128)(2,1)S(1)}, u32[]{:S(2)}, u32[]{:S(2)}) collective-permute-start(bf16[2,272,128]{2,1,0:T(8,128)(2,1)S(1)} %get-tuple-element.21._), channel_id=1, source_target_pairs={{0,2},{1,3},{2,0},{3,1},{4,6},{5,7},{6,4},{7,5},{8,10},{9,11},{10,... | collective-permute-start | bytes 417800 | tf_op jit(solution)/shard_map/ppermute | solution.py:347
  14.8 2.6 %collective-permute-start.1 = (bf16[4,272,128]{2,1,0:T(8,128)(2,1)S(1)}, bf16[4,272,128]{2,1,0:T(8,128)(2,1)S(1)}, u32[]{:S(2)}, u32[]{:S(2)}) collective-permute-start(bf16[4,272,128]{2,1,0:T(8,128)(2,1)S(1)} %shard_map.107._), channel_id=1, source_target_pairs={{0,1},{1,0},{2,3},{3,2},{4,5},{5,4},{6,7},{7,6},{8,9},{9,8},{10,11... | collective-permute-start | bytes 835592 | tf_op jit(solution)/shard_map/ppermute | solution.py:342
  15.9 10.3 %collective-permute-start.4 = (bf16[2,272,128]{2,1,0:T(8,128)(2,1)S(1)}, bf16[2,272,128]{2,1,0:T(8,128)(2,1)S(1)}, u32[]{:S(2)}, u32[]{:S(2)}) collective-permute-start(bf16[2,272,128]{2,1,0:T(8,128)(2,1)S(1)} %get-tuple-element.20), channel_id=1, source_target_pairs={{0,6},{1,7},{2,4},{3,5},{4,2},{5,3},{6,0},{7,1},{8,14},{9,15},{10,... | collective-permute-start | bytes 417800 | tf_op jit(solution)/shard_map/ppermute | solution.py:347
  18.5 1.8 %collective-permute-start.2 = (bf16[4,272,128]{2,1,0:T(8,128)(2,1)S(1)}, bf16[4,272,128]{2,1,0:T(8,128)(2,1)S(1)}, u32[]{:S(2)}, u32[]{:S(2)}) collective-permute-start(bf16[4,272,128]{2,1,0:T(8,128)(2,1)S(1)} %shard_map.109._), channel_id=1, source_target_pairs={{0,1},{1,0},{2,3},{3,2},{4,5},{5,4},{6,7},{7,6},{8,9},{9,8},{10,11... | collective-permute-start | bytes 835592 | tf_op jit(solution)/shard_map/ppermute | solution.py:342
  19.7 7.0 %collective-permute-start.6 = (bf16[2,272,128]{2,1,0:T(8,128)(2,1)S(1)}, bf16[2,272,128]{2,1,0:T(8,128)(2,1)S(1)}, u32[]{:S(2)}, u32[]{:S(2)}) collective-permute-start(bf16[2,272,128]{2,1,0:T(8,128)(2,1)S(1)} %get-tuple-element.18), channel_id=1, source_target_pairs={{0,4},{1,5},{2,6},{3,7},{4,0},{5,1},{6,2},{7,3},{8,12},{9,13},{10,... | collective-permute-start | bytes 417800 | tf_op jit(solution)/shard_map/ppermute | solution.py:347
  20.4 12.2 %collective-permute-start.8 = (bf16[2,272,128]{2,1,0:T(8,128)(2,1)S(1)}, bf16[2,272,128]{2,1,0:T(8,128)(2,1)S(1)}, u32[]{:S(2)}, u32[]{:S(2)}) collective-permute-start(bf16[2,272,128]{2,1,0:T(8,128)(2,1)S(1)} %get-tuple-element.17._), channel_id=1, source_target_pairs={{0,2},{1,3},{2,0},{3,1},{4,6},{5,7},{6,4},{7,5},{8,10},{9,11},{10,... | collective-permute-start | bytes 417800 | tf_op jit(solution)/shard_map/ppermute | solution.py:347
  23.0 1.6 %collective-permute-start.3 = (bf16[4,272,128]{2,1,0:T(8,128)(2,1)S(1)}, bf16[4,272,128]{2,1,0:T(8,128)(2,1)S(1)}, u32[]{:S(2)}, u32[]{:S(2)}) collective-permute-start(bf16[4,272,128]{2,1,0:T(8,128)(2,1)S(1)} %shard_map.111._), channel_id=1, source_target_pairs={{0,1},{1,0},{2,3},{3,2},{4,5},{5,4},{6,7},{7,6},{8,9},{9,8},{10,11... | collective-permute-start | bytes 835592 | tf_op jit(solution)/shard_map/ppermute | solution.py:342
  24.6 7.9 %collective-permute-start.7 = (bf16[2,272,128]{2,1,0:T(8,128)(2,1)S(1)}, bf16[2,272,128]{2,1,0:T(8,128)(2,1)S(1)}, u32[]{:S(2)}, u32[]{:S(2)}) collective-permute-start(bf16[2,272,128]{2,1,0:T(8,128)(2,1)S(1)} %get-tuple-element.16), channel_id=1, source_target_pairs={{0,6},{1,7},{2,4},{3,5},{4,2},{5,3},{6,0},{7,1},{8,14},{9,15},{10,... | collective-permute-start | bytes 417800 | tf_op jit(solution)/shard_map/ppermute | solution.py:347
  26.2 7.0 %collective-permute-start.9 = (bf16[2,272,128]{2,1,0:T(8,128)(2,1)S(1)}, bf16[2,272,128]{2,1,0:T(8,128)(2,1)S(1)}, u32[]{:S(2)}, u32[]{:S(2)}) collective-permute-start(bf16[2,272,128]{2,1,0:T(8,128)(2,1)S(1)} %get-tuple-element.14), channel_id=1, source_target_pairs={{0,4},{1,5},{2,6},{3,7},{4,0},{5,1},{6,2},{7,3},{8,12},{9,13},{10,... | collective-permute-start | bytes 417800 | tf_op jit(solution)/shard_map/ppermute | solution.py:347
  26.8 10.3 %collective-permute-start.12 = (bf16[272,128]{1,0:T(8,128)(2,1)S(1)}, bf16[272,128]{1,0:T(8,128)(2,1)S(1)}, u32[]{:S(2)}, u32[]{:S(2)}) collective-permute-start(bf16[272,128]{1,0:T(8,128)(2,1)S(1)} %get-tuple-element.11), channel_id=1, source_target_pairs={{0,24},{4,28},{8,16},{12,20},{16,8},{20,12},{24,0},{28,4},{1,25},{... | collective-permute-start | bytes 208904 | tf_op jit(solution)/shard_map/ppermute | solution.py:342
  30.5 6.5 %collective-permute-start.11 = (bf16[272,128]{1,0:T(8,128)(2,1)S(1)}, bf16[272,128]{1,0:T(8,128)(2,1)S(1)}, u32[]{:S(2)}, u32[]{:S(2)}) collective-permute-start(bf16[272,128]{1,0:T(8,128)(2,1)S(1)} %get-tuple-element.8._), channel_id=1, source_target_pairs={{0,16},{4,20},{8,24},{12,28},{16,0},{20,4},{24,8},{28,12},{1,17},{... | collective-permute-start | bytes 208904 | tf_op jit(solution)/shard_map/ppermute | solution.py:342
  33.3 4.4 %collective-permute-start.10 = (bf16[272,128]{1,0:T(8,128)(2,1)S(1)}, bf16[272,128]{1,0:T(8,128)(2,1)S(1)}, u32[]{:S(2)}, u32[]{:S(2)}) collective-permute-start(bf16[272,128]{1,0:T(8,128)(2,1)S(1)} %get-tuple-element.10), channel_id=1, source_target_pairs={{0,8},{4,12},{8,0},{12,4},{16,24},{20,28},{24,16},{28,20},{1,9},{5... | collective-permute-start | bytes 208904 | tf_op jit(solution)/shard_map/ppermute | solution.py:342
  35.0 4.4 %copy-start = (bf16[128,256]{1,0:T(8,128)(2,1)S(1)}, bf16[128,256]{1,0:T(8,128)(2,1)}, u32[]{:S(2)}) copy-start(bf16[128,256]{1,0:T(8,128)(2,1)} %constant.13.clone.refs_4_.refs_2_) | copy-start | bytes 196612
  35.0 4.4 %copy-start.1 = (f32[32,128]{1,0:T(8,128)S(1)}, f32[32,128]{1,0:T(8,128)}, u32[]{:S(2)}) copy-start(f32[32,128]{1,0:T(8,128)} %constant.14.clone.refs_5_.refs_3_) | copy-start | bytes 49156
  37.7 4.4 %collective-permute-start.14 = (bf16[272,128]{1,0:T(8,128)(2,1)S(1)}, bf16[272,128]{1,0:T(8,128)(2,1)S(1)}, u32[]{:S(2)}, u32[]{:S(2)}) collective-permute-start(bf16[272,128]{1,0:T(8,128)(2,1)S(1)} %shard_map.118), channel_id=1, source_target_pairs={{0,2},{1,3},{2,0},{3,1},{4,6},{5,7},{6,4},{7,5},{8,10},{9,11},{10,... | collective-permute-start | bytes 208904 | tf_op jit(solution)/shard_map/ppermute | solution.py:342
  39.4 2.7 %collective-permute-start.13 = (bf16[272,128]{1,0:T(8,128)(2,1)S(1)}, bf16[272,128]{1,0:T(8,128)(2,1)S(1)}, u32[]{:S(2)}, u32[]{:S(2)}) collective-permute-start(bf16[272,128]{1,0:T(8,128)(2,1)S(1)} %shard_map.118), channel_id=1, source_target_pairs={{0,1},{1,0},{2,3},{3,2},{4,5},{5,4},{6,7},{7,6},{8,9},{9,8},{10,11... | collective-permute-start | bytes 208904 | tf_op jit(solution)/shard_map/ppermute | solution.py:342
  42.1 1.3 %collective-permute-start.15 = (bf16[272,128]{1,0:T(8,128)(2,1)S(1)}, bf16[272,128]{1,0:T(8,128)(2,1)S(1)}, u32[]{:S(2)}, u32[]{:S(2)}) collective-permute-start(bf16[272,128]{1,0:T(8,128)(2,1)S(1)} %collective-permute-done.14.refs_1_), channel_id=1, source_target_pairs={{0,1},{1,0},{2,3},{3,2},{4,5},{5,4},{6,7},{7,6},{8,9},{9,8},{10,11... | collective-permute-start | bytes 208904 | tf_op jit(solution)/shard_map/ppermute | solution.py:342

commit v6 on v5

--- a/solution.py
+++ b/solution.py
@@ -321,7 +321,7 @@
             preferred_element_type=jnp.float32,
         )
         total = term if total is None else total + term
-    sums[:, : 2 * classes] = total
+    sums[: total.shape[0], : 2 * classes] = total
     count = out.shape[1]
     inner = sums[pl.ds(0, count, stride=2), :] + pltpu.roll(
         sums[pl.ds(1, count, stride=2), :], PIX - classes, 1
@@ -450,7 +450,7 @@
     )(done, *put(pltpu.VMEM, *pieces))
     final_tables = jnp.asarray(expand_table()), jnp.asarray(filter_table())
     spread_scratch = [
-        pltpu.VMEM((TILE * BAND, PIX), jnp.float32),
+        pltpu.VMEM((TILE * BAND + BAND, PIX), jnp.float32),
         pltpu.VMEM(((BAND + 1) * TILE, PIX), jnp.float32),
     ]
     averages, rounded = pl.pallas_call(
@@ -487,7 +487,7 @@
         out_shape=jax.ShapeDtypeStruct((own * groups, fresh_count), jnp.float32),
         in_specs=[vmem] * (groups + len(fresh)),
         out_specs=vmem,
-        scratch_shapes=[pltpu.VMEM((2 * fresh_count, PIX), jnp.float32)],
+        scratch_shapes=[pltpu.VMEM((2 * fresh_count + TILE, PIX), jnp.float32)],
         compiler_params=pltpu.CompilerParams(vmem_limit_bytes=16 * MIB),
     )(*put(pltpu.VMEM, *held, *fresh))
     return averages, scores

time: 45.9 us -> 45.9 us (level)
  no operation moved by 1% of the time
where the time goes in v6:
time: 45.9 us; the launch traced here: 45.7 us
  Pallas kernels  23.9 us (52%)
  starting transfers between devices  16.7 us (36%)
  waiting for transfers between devices  3.93 us (9%)
  between operations  0.86 us (2%)
    ppermute x6, starting transfers between devices, hop(): lax.ppermute(array, ('dp', 'grp'), [(i, i ^ ((near & 1) * groups | (near...  8.59 us
    pallas_call x8, Pallas kernels, transform(): pl.pallas_call(functools.partial(transform_kernel, jobs=jobs, other=other...  8.1 us
    ppermute x10, starting transfers between devices, swap(): return lax.ppermute(array, axis, [(i, i ^ flip) for i in range(size)])  8.06 us
    pallas_call x1, Pallas kernels, body(): pl.pallas_call(sums_kernel, out_shape=pltpu.VMEM((CLASSES * SLAB, PIX), j...  7.26 us
    pallas_call x2, Pallas kernels, regroup(): pl.pallas_call(functools.partial(regroup_kernel, first=first), out_shape=...  3.99 us
    ppermute x10, waiting for transfers between devices, swap(): return lax.ppermute(array, axis, [(i, i ^ flip) for i in range(size)])  3.25 us
    pallas_call x1, Pallas kernels, body(): pl.pallas_call(functools.partial(scores_kernel, own=own, groups=groups),...  2.01 us
    pallas_call x1, Pallas kernels, body(): pl.pallas_call(functools.partial(averages_kernel, own=own, parts=fars), o...  1.33 us
  transfers between devices with their start and end apart: 16, of which 6 were waited for; matrix products, arithmetic and copies ran while one was open for 1% of the time, Pallas kernels for 29%

profile of v6, /device:TPU:0, one launch (start us, length us, event | category | flops | bytes accessed | tf_op | source)
XLA Modules:
  0.0 45.7 jit_solution(2502823154465526842)
XLA Ops:
  0.7 7.3 %shard_map.104.acc = f32[40960,128]{1,0:T(8,128)S(1)} custom-call(s32[512]{0:T(512)} %class_ids.1, s32[2,512]{1,0:T(2,128)} %bitcast.15, bf16[512,128,128]{2,1,0:T(8,128)(2,1)} %images.1), custom_call_target="tpu_custom_call" | custom-call | tf_op jit(solution)/shard_map/pallas_call | solution.py:371
  8.0 1.0 %shard_map.105._ = bf16[4,272,128]{2,1,0:T(8,128)(2,1)S(1)} custom-call(s32[4,128]{1,0:T(4,128)S(1)} %bitcast.6, f32[40960,128]{1,0:T(8,128)S(1)} %shard_map.104.acc, s32[4,128]{1,0:T(4,128)S(1)} %bitcast.7, bf16[256,128]{1,0:T(8,128)(2,1)S(1)} %copy-done.3, bf16[80,128]{1,0:T(8,128)(2,1)S(1)} %copy-done.5, bf16[16,1024]{1,0:T(8,128)(2,1)S(1)} %copy-done.4), custom_call_target="tpu_custom_call" | custom-call | flops 10000000000 | bytes 1048576 | tf_op jit(solution)/shard_map/pallas_call | solution.py:394
  9.5 1.0 %shard_map.106 = bf16[4,272,128]{2,1,0:T(8,128)(2,1)S(1)} custom-call(bf16[4,272,128]{2,1,0:T(8,128)(2,1)S(1)} %shard_map.105._, f32[40960,128]{1,0:T(8,128)S(1)} %shard_map.104.acc, s32[4,128]{1,0:T(4,128)S(1)} %bitcast.8, bf16[256,128]{1,0:T(8,128)(2,1)S(1)} %copy-done.3, bf16[80,128]{1,0:T(8,128)(2,1)S(1)} %copy-done.5, bf16[16,1024]{1,0:T(8,128)(2,1)S(1)} %copy-done.4), custom_call_target="tpu_custom_call" | custom-call | flops 10000000000 | bytes 1048576 | tf_op jit(solution)/shard_map/pallas_call | solution.py:394
  10.8 3.0 %collective-permute-start.5 = (bf16[2,272,128]{2,1,0:T(8,128)(2,1)S(1)}, bf16[2,272,128]{2,1,0:T(8,128)(2,1)S(1)}, u32[]{:S(2)}, u32[]{:S(2)}) collective-permute-start(bf16[2,272,128]{2,1,0:T(8,128)(2,1)S(1)} %get-tuple-element.21._), channel_id=1, source_target_pairs={{0,2},{1,3},{2,0},{3,1},{4,6},{5,7},{6,4},{7,5},{8,10},{9,11},{10,... | collective-permute-start | bytes 417800 | tf_op jit(solution)/shard_map/ppermute | solution.py:347
  13.8 1.0 %shard_map.107._ = bf16[4,272,128]{2,1,0:T(8,128)(2,1)S(1)} custom-call(bf16[2,272,128]{2,1,0:T(8,128)(2,1)S(1)} %get-tuple-element.21._, f32[40960,128]{1,0:T(8,128)S(1)} %shard_map.104.acc, s32[4,128]{1,0:T(4,128)S(1)} %bitcast.9, bf16[256,128]{1,0:T(8,128)(2,1)S(1)} %copy-done.3, bf16[80,128]{1,0:T(8,128)(2,1)S(1)} %copy-done.5, ...), custom_call_target="tpu_custom_call" | custom-call | flops 10000000000 | bytes 1048576 | tf_op jit(solution)/shard_map/pallas_call | solution.py:394
  14.8 1.0 %shard_map.108 = bf16[4,272,128]{2,1,0:T(8,128)(2,1)S(1)} custom-call(bf16[4,272,128]{2,1,0:T(8,128)(2,1)S(1)} %shard_map.107._, f32[40960,128]{1,0:T(8,128)S(1)} %shard_map.104.acc, s32[4,128]{1,0:T(4,128)S(1)} %bitcast.10, bf16[256,128]{1,0:T(8,128)(2,1)S(1)} %copy-done.3, bf16[80,128]{1,0:T(8,128)(2,1)S(1)} %copy-done.5, bf16[16,1024]{1,0:T(8,128)(2,1)S(1)} %copy-done.4), custom_call_target="tpu_custom_call" | custom-call | flops 10000000000 | bytes 1048576 | tf_op jit(solution)/shard_map/pallas_call | solution.py:394
  15.9 1.5 %collective-permute-start.4 = (bf16[2,272,128]{2,1,0:T(8,128)(2,1)S(1)}, bf16[2,272,128]{2,1,0:T(8,128)(2,1)S(1)}, u32[]{:S(2)}, u32[]{:S(2)}) collective-permute-start(bf16[2,272,128]{2,1,0:T(8,128)(2,1)S(1)} %get-tuple-element.20), channel_id=1, source_target_pairs={{0,6},{1,7},{2,4},{3,5},{4,2},{5,3},{6,0},{7,1},{8,14},{9,15},{10,... | collective-permute-start | bytes 417800 | tf_op jit(solution)/shard_map/ppermute | solution.py:347
  17.4 1.0 %shard_map.109._ = bf16[4,272,128]{2,1,0:T(8,128)(2,1)S(1)} custom-call(bf16[2,272,128]{2,1,0:T(8,128)(2,1)S(1)} %get-tuple-element.19._.refs_3_, f32[40960,128]{1,0:T(8,128)S(1)} %shard_map.104.acc, s32[4,128]{1,0:T(4,128)S(1)} %bitcast.11, bf16[256,128]{1,0:T(8,128)(2,1)S(1)} %copy-done.3, bf16[80,128]{1,0:T(8,128)(2,1)S(1)} %copy-done.5, ...), custom_call_target="tpu_custom_call" | custom-call | flops 10000000000 | bytes 1048576 | tf_op jit(solution)/shard_map/pallas_call | solution.py:394
  18.7 1.0 %shard_map.110 = bf16[4,272,128]{2,1,0:T(8,128)(2,1)S(1)} custom-call(bf16[4,272,128]{2,1,0:T(8,128)(2,1)S(1)} %shard_map.109._, f32[40960,128]{1,0:T(8,128)S(1)} %shard_map.104.acc, s32[4,128]{1,0:T(4,128)S(1)} %bitcast.12, bf16[256,128]{1,0:T(8,128)(2,1)S(1)} %copy-done.3, bf16[80,128]{1,0:T(8,128)(2,1)S(1)} %copy-done.5, bf16[16,1024]{1,0:T(8,128)(2,1)S(1)} %copy-done.4), custom_call_target="tpu_custom_call" | custom-call | flops 10000000000 | bytes 1048576 | tf_op jit(solution)/shard_map/pallas_call | solution.py:394
  20.3 1.7 %collective-permute-start.8 = (bf16[2,272,128]{2,1,0:T(8,128)(2,1)S(1)}, bf16[2,272,128]{2,1,0:T(8,128)(2,1)S(1)}, u32[]{:S(2)}, u32[]{:S(2)}) collective-permute-start(bf16[2,272,128]{2,1,0:T(8,128)(2,1)S(1)} %get-tuple-element.17._), channel_id=1, source_target_pairs={{0,2},{1,3},{2,0},{3,1},{4,6},{5,7},{6,4},{7,5},{8,10},{9,11},{10,... | collective-permute-start | bytes 417800 | tf_op jit(solution)/shard_map/ppermute | solution.py:347
  22.0 1.0 %shard_map.111._ = bf16[4,272,128]{2,1,0:T(8,128)(2,1)S(1)} custom-call(bf16[2,272,128]{2,1,0:T(8,128)(2,1)S(1)} %get-tuple-element.17._, f32[40960,128]{1,0:T(8,128)S(1)} %shard_map.104.acc, s32[4,128]{1,0:T(4,128)S(1)} %bitcast.13, bf16[256,128]{1,0:T(8,128)(2,1)S(1)} %copy-done.3, bf16[80,128]{1,0:T(8,128)(2,1)S(1)} %copy-done.5, ...), custom_call_target="tpu_custom_call" | custom-call | flops 10000000000 | bytes 1048576 | tf_op jit(solution)/shard_map/pallas_call | solution.py:394
  23.1 1.0 %shard_map.112 = bf16[4,272,128]{2,1,0:T(8,128)(2,1)S(1)} custom-call(bf16[4,272,128]{2,1,0:T(8,128)(2,1)S(1)} %shard_map.111._, f32[40960,128]{1,0:T(8,128)S(1)} %shard_map.104.acc, s32[4,128]{1,0:T(4,128)S(1)} %bitcast.14, bf16[256,128]{1,0:T(8,128)(2,1)S(1)} %copy-done.3, bf16[80,128]{1,0:T(8,128)(2,1)S(1)} %copy-done.5, bf16[16,1024]{1,0:T(8,128)(2,1)S(1)} %copy-done.4), custom_call_target="tpu_custom_call" | custom-call | flops 10000000000 | bytes 1048576 | tf_op jit(solution)/shard_map/pallas_call | solution.py:394
  24.6 1.4 %collective-permute-start.7 = (bf16[2,272,128]{2,1,0:T(8,128)(2,1)S(1)}, bf16[2,272,128]{2,1,0:T(8,128)(2,1)S(1)}, u32[]{:S(2)}, u32[]{:S(2)}) collective-permute-start(bf16[2,272,128]{2,1,0:T(8,128)(2,1)S(1)} %get-tuple-element.16), channel_id=1, source_target_pairs={{0,6},{1,7},{2,4},{3,5},{4,2},{5,3},{6,0},{7,1},{8,14},{9,15},{10,... | collective-permute-start | bytes 417800 | tf_op jit(solution)/shard_map/ppermute | solution.py:347
  26.8 3.7 %collective-permute-start.12 = (bf16[272,128]{1,0:T(8,128)(2,1)S(1)}, bf16[272,128]{1,0:T(8,128)(2,1)S(1)}, u32[]{:S(2)}, u32[]{:S(2)}) collective-permute-start(bf16[272,128]{1,0:T(8,128)(2,1)S(1)} %get-tuple-element.11), channel_id=1, source_target_pairs={{0,24},{4,28},{8,16},{12,20},{16,8},{20,12},{24,0},{28,4},{1,25},{... | collective-permute-start | bytes 208904 | tf_op jit(solution)/shard_map/ppermute | solution.py:342
  30.5 2.0 %shard_map.114._ = bf16[16,256,2,128]{3,2,1,0:T(2,128)(2,1)S(1)} custom-call(bf16[272,128]{1,0:T(8,128)(2,1)S(1)} %get-tuple-element.8._, bf16[256,2,4096]{2,1,0:T(2,128)(2,1)} %block.3), custom_call_target="tpu_custom_call" | custom-call | flops 100000000 | bytes 1048576 | tf_op jit(solution)/shard_map/pallas_call | solution.py:419
  32.5 0.7 %collective-permute-done.9.refs_2_ = bf16[2,272,128]{2,1,0:T(8,128)(2,1)S(1)} collective-permute-done((bf16[2,272,128]{2,1,0:T(8,128)(2,1)S(1)}, bf16[2,272,128]{2,1,0:T(8,128)(2,1)S(1)}, u32[]{:S(2)}, u32[]{:S(2)}) %collective-permute-start.9) | collective-permute-done | bytes 139296 | tf_op jit(solution)/shard_map/ppermute | solution.py:347
  33.3 1.7 %collective-permute-start.10 = (bf16[272,128]{1,0:T(8,128)(2,1)S(1)}, bf16[272,128]{1,0:T(8,128)(2,1)S(1)}, u32[]{:S(2)}, u32[]{:S(2)}) collective-permute-start(bf16[272,128]{1,0:T(8,128)(2,1)S(1)} %get-tuple-element.10), channel_id=1, source_target_pairs={{0,8},{4,12},{8,0},{12,4},{16,24},{20,28},{24,16},{28,20},{1,9},{5... | collective-permute-start | bytes 208904 | tf_op jit(solution)/shard_map/ppermute | solution.py:342
  35.0 2.0 %shard_map.117._ = bf16[16,256,2,128]{3,2,1,0:T(2,128)(2,1)S(1)} custom-call(bf16[272,128]{1,0:T(8,128)(2,1)S(1)} %get-tuple-element.9.refs_0_._, bf16[256,2,4096]{2,1,0:T(2,128)(2,1)} %block.3), custom_call_target="tpu_custom_call" | custom-call | flops 100000000 | bytes 1048576 | tf_op jit(solution)/shard_map/pallas_call | solution.py:419
  37.1 0.6 %collective-permute-done.10.refs_1_ = bf16[272,128]{1,0:T(8,128)(2,1)S(1)} collective-permute-done((bf16[272,128]{1,0:T(8,128)(2,1)S(1)}, bf16[272,128]{1,0:T(8,128)(2,1)S(1)}, u32[]{:S(2)}, u32[]{:S(2)}) %collective-permute-start.10) | collective-permute-done | bytes 69664 | tf_op jit(solution)/shard_map/ppermute | solution.py:342
  37.7 1.7 %collective-permute-start.14 = (bf16[272,128]{1,0:T(8,128)(2,1)S(1)}, bf16[272,128]{1,0:T(8,128)(2,1)S(1)}, u32[]{:S(2)}, u32[]{:S(2)}) collective-permute-start(bf16[272,128]{1,0:T(8,128)(2,1)S(1)} %shard_map.118), channel_id=1, source_target_pairs={{0,2},{1,3},{2,0},{3,1},{4,6},{5,7},{6,4},{7,5},{8,10},{9,11},{10,... | collective-permute-start | bytes 208904 | tf_op jit(solution)/shard_map/ppermute | solution.py:342
  39.4 1.3 %shard_map.116 = (f32[8,2,4096]{2,1,0:T(2,128)}, bf16[8,8192]{1,0:T(8,128)(2,1)S(1)}) custom-call(bf16[272,128]{1,0:T(8,128)(2,1)S(1)} %get-tuple-element.9.refs_0_._, bf16[272,128]{1,0:T(8,128)(2,1)S(1)} %collective-permute-done.10.refs_1_, bf16[272,128]{1,0:T(8,128)(2,1)S(1)} %collective-permute-done.11.refs_2_, ...), custom_call_target="tpu_custom_call" | custom-call | tf_op jit(solution)/shard_map/pallas_call | solution.py:456
  40.7 1.4 %collective-permute-done.14.refs_1_ = bf16[272,128]{1,0:T(8,128)(2,1)S(1)} collective-permute-done((bf16[272,128]{1,0:T(8,128)(2,1)S(1)}, bf16[272,128]{1,0:T(8,128)(2,1)S(1)}, u32[]{:S(2)}, u32[]{:S(2)}) %collective-permute-start.14) | collective-permute-done | bytes 69664 | tf_op jit(solution)/shard_map/ppermute | solution.py:342
  42.8 0.5 %collective-permute-done.15.refs_1_ = bf16[272,128]{1,0:T(8,128)(2,1)S(1)} collective-permute-done((bf16[272,128]{1,0:T(8,128)(2,1)S(1)}, bf16[272,128]{1,0:T(8,128)(2,1)S(1)}, u32[]{:S(2)}, u32[]{:S(2)}) %collective-permute-start.15) | collective-permute-done | bytes 69664 | tf_op jit(solution)/shard_map/ppermute | solution.py:342
  43.7 2.0 %shard_map.122 = f32[32,256]{1,0:T(8,128)} custom-call(bf16[8,8192]{1,0:T(8,128)(2,1)S(1)} %get-tuple-element.13.refs_0_, bf16[8,8192]{1,0:T(8,128)(2,1)S(1)} %shard_map.119.refs_0_.refs_1_, bf16[8,8192]{1,0:T(8,128)(2,1)S(1)} %shard_map.120.refs_0_.refs_2_, bf16[8,8192]{1,0:T(8,128)(2,1)S(1)} %shard_map.121.refs_3_, bf16[16,512,128]{2,1,0:T(8,128)(2,1)S(1)} %bitcast.4, ...), custom_call_target="tpu_custom_call" | custom-call | tf_op jit(solution)/shard_map/pallas_call | solution.py:485
  (43 shorter events, 4.3 us)
Async XLA Ops:
  0.6 7.3 %copy-start.2 = (s32[512]{0:T(512)S(1)}, s32[512]{0:T(512)}, u32[]{:S(2)}) copy-start(s32[512]{0:T(512)} %class_ids.1) | copy-start | bytes 6148
  0.6 7.3 %copy-start.3 = (bf16[256,128]{1,0:T(8,128)(2,1)S(1)}, bf16[256,128]{1,0:T(8,128)(2,1)}, u32[]{:S(2)}) copy-start(bf16[256,128]{1,0:T(8,128)(2,1)} %constant.10.clone.col) | copy-start | bytes 196612
  0.7 7.3 %copy-start.4 = (bf16[16,1024]{1,0:T(8,128)(2,1)S(1)}, bf16[16,1024]{1,0:T(8,128)(2,1)}, u32[]{:S(2)}) copy-start(bf16[16,1024]{1,0:T(8,128)(2,1)} %constant.12.clone.last) | copy-start | bytes 98308
  0.7 7.3 %copy-start.5 = (bf16[80,128]{1,0:T(8,128)(2,1)S(1)}, bf16[80,128]{1,0:T(8,128)(2,1)}, u32[]{:S(2)}) copy-start(bf16[80,128]{1,0:T(8,128)(2,1)} %constant.11.clone.row) | copy-start | bytes 61444
  9.0 1.7 %collective-permute-start = (bf16[4,272,128]{2,1,0:T(8,128)(2,1)S(1)}, bf16[4,272,128]{2,1,0:T(8,128)(2,1)S(1)}, u32[]{:S(2)}, u32[]{:S(2)}) collective-permute-start(bf16[4,272,128]{2,1,0:T(8,128)(2,1)S(1)} %shard_map.105._), channel_id=1, source_target_pairs={{0,1},{1,0},{2,3},{3,2},{4,5},{5,4},{6,7},{7,6},{8,9},{9,8},{10,11... | collective-permute-start | bytes 835592 | tf_op jit(solution)/shard_map/ppermute | solution.py:342
  10.8 15.9 %collective-permute-start.5 = (bf16[2,272,128]{2,1,0:T(8,128)(2,1)S(1)}, bf16[2,272,128]{2,1,0:T(8,128)(2,1)S(1)}, u32[]{:S(2)}, u32[]{:S(2)}) collective-permute-start(bf16[2,272,128]{2,1,0:T(8,128)(2,1)S(1)} %get-tuple-element.21._), channel_id=1, source_target_pairs={{0,2},{1,3},{2,0},{3,1},{4,6},{5,7},{6,4},{7,5},{8,10},{9,11},{10,... | collective-permute-start | bytes 417800 | tf_op jit(solution)/shard_map/ppermute | solution.py:347
  14.8 2.6 %collective-permute-start.1 = (bf16[4,272,128]{2,1,0:T(8,128)(2,1)S(1)}, bf16[4,272,128]{2,1,0:T(8,128)(2,1)S(1)}, u32[]{:S(2)}, u32[]{:S(2)}) collective-permute-start(bf16[4,272,128]{2,1,0:T(8,128)(2,1)S(1)} %shard_map.107._), channel_id=1, source_target_pairs={{0,1},{1,0},{2,3},{3,2},{4,5},{5,4},{6,7},{7,6},{8,9},{9,8},{10,11... | collective-permute-start | bytes 835592 | tf_op jit(solution)/shard_map/ppermute | solution.py:342
  15.9 10.3 %collective-permute-start.4 = (bf16[2,272,128]{2,1,0:T(8,128)(2,1)S(1)}, bf16[2,272,128]{2,1,0:T(8,128)(2,1)S(1)}, u32[]{:S(2)}, u32[]{:S(2)}) collective-permute-start(bf16[2,272,128]{2,1,0:T(8,128)(2,1)S(1)} %get-tuple-element.20), channel_id=1, source_target_pairs={{0,6},{1,7},{2,4},{3,5},{4,2},{5,3},{6,0},{7,1},{8,14},{9,15},{10,... | collective-permute-start | bytes 417800 | tf_op jit(solution)/shard_map/ppermute | solution.py:347
  18.5 1.8 %collective-permute-start.2 = (bf16[4,272,128]{2,1,0:T(8,128)(2,1)S(1)}, bf16[4,272,128]{2,1,0:T(8,128)(2,1)S(1)}, u32[]{:S(2)}, u32[]{:S(2)}) collective-permute-start(bf16[4,272,128]{2,1,0:T(8,128)(2,1)S(1)} %shard_map.109._), channel_id=1, source_target_pairs={{0,1},{1,0},{2,3},{3,2},{4,5},{5,4},{6,7},{7,6},{8,9},{9,8},{10,11... | collective-permute-start | bytes 835592 | tf_op jit(solution)/shard_map/ppermute | solution.py:342
  19.7 7.0 %collective-permute-start.6 = (bf16[2,272,128]{2,1,0:T(8,128)(2,1)S(1)}, bf16[2,272,128]{2,1,0:T(8,128)(2,1)S(1)}, u32[]{:S(2)}, u32[]{:S(2)}) collective-permute-start(bf16[2,272,128]{2,1,0:T(8,128)(2,1)S(1)} %get-tuple-element.18), channel_id=1, source_target_pairs={{0,4},{1,5},{2,6},{3,7},{4,0},{5,1},{6,2},{7,3},{8,12},{9,13},{10,... | collective-permute-start | bytes 417800 | tf_op jit(solution)/shard_map/ppermute | solution.py:347
  20.3 12.2 %collective-permute-start.8 = (bf16[2,272,128]{2,1,0:T(8,128)(2,1)S(1)}, bf16[2,272,128]{2,1,0:T(8,128)(2,1)S(1)}, u32[]{:S(2)}, u32[]{:S(2)}) collective-permute-start(bf16[2,272,128]{2,1,0:T(8,128)(2,1)S(1)} %get-tuple-element.17._), channel_id=1, source_target_pairs={{0,2},{1,3},{2,0},{3,1},{4,6},{5,7},{6,4},{7,5},{8,10},{9,11},{10,... | collective-permute-start | bytes 417800 | tf_op jit(solution)/shard_map/ppermute | solution.py:347
  23.0 1.6 %collective-permute-start.3 = (bf16[4,272,128]{2,1,0:T(8,128)(2,1)S(1)}, bf16[4,272,128]{2,1,0:T(8,128)(2,1)S(1)}, u32[]{:S(2)}, u32[]{:S(2)}) collective-permute-start(bf16[4,272,128]{2,1,0:T(8,128)(2,1)S(1)} %shard_map.111._), channel_id=1, source_target_pairs={{0,1},{1,0},{2,3},{3,2},{4,5},{5,4},{6,7},{7,6},{8,9},{9,8},{10,11... | collective-permute-start | bytes 835592 | tf_op jit(solution)/shard_map/ppermute | solution.py:342
  24.6 7.9 %collective-permute-start.7 = (bf16[2,272,128]{2,1,0:T(8,128)(2,1)S(1)}, bf16[2,272,128]{2,1,0:T(8,128)(2,1)S(1)}, u32[]{:S(2)}, u32[]{:S(2)}) collective-permute-start(bf16[2,272,128]{2,1,0:T(8,128)(2,1)S(1)} %get-tuple-element.16), channel_id=1, source_target_pairs={{0,6},{1,7},{2,4},{3,5},{4,2},{5,3},{6,0},{7,1},{8,14},{9,15},{10,... | collective-permute-start | bytes 417800 | tf_op jit(solution)/shard_map/ppermute | solution.py:347
  26.2 7.0 %collective-permute-start.9 = (bf16[2,272,128]{2,1,0:T(8,128)(2,1)S(1)}, bf16[2,272,128]{2,1,0:T(8,128)(2,1)S(1)}, u32[]{:S(2)}, u32[]{:S(2)}) collective-permute-start(bf16[2,272,128]{2,1,0:T(8,128)(2,1)S(1)} %get-tuple-element.14), channel_id=1, source_target_pairs={{0,4},{1,5},{2,6},{3,7},{4,0},{5,1},{6,2},{7,3},{8,12},{9,13},{10,... | collective-permute-start | bytes 417800 | tf_op jit(solution)/shard_map/ppermute | solution.py:347
  26.8 10.3 %collective-permute-start.12 = (bf16[272,128]{1,0:T(8,128)(2,1)S(1)}, bf16[272,128]{1,0:T(8,128)(2,1)S(1)}, u32[]{:S(2)}, u32[]{:S(2)}) collective-permute-start(bf16[272,128]{1,0:T(8,128)(2,1)S(1)} %get-tuple-element.11), channel_id=1, source_target_pairs={{0,24},{4,28},{8,16},{12,20},{16,8},{20,12},{24,0},{28,4},{1,25},{... | collective-permute-start | bytes 208904 | tf_op jit(solution)/shard_map/ppermute | solution.py:342
  30.5 6.5 %collective-permute-start.11 = (bf16[272,128]{1,0:T(8,128)(2,1)S(1)}, bf16[272,128]{1,0:T(8,128)(2,1)S(1)}, u32[]{:S(2)}, u32[]{:S(2)}) collective-permute-start(bf16[272,128]{1,0:T(8,128)(2,1)S(1)} %get-tuple-element.8._), channel_id=1, source_target_pairs={{0,16},{4,20},{8,24},{12,28},{16,0},{20,4},{24,8},{28,12},{1,17},{... | collective-permute-start | bytes 208904 | tf_op jit(solution)/shard_map/ppermute | solution.py:342
  33.3 4.4 %collective-permute-start.10 = (bf16[272,128]{1,0:T(8,128)(2,1)S(1)}, bf16[272,128]{1,0:T(8,128)(2,1)S(1)}, u32[]{:S(2)}, u32[]{:S(2)}) collective-permute-start(bf16[272,128]{1,0:T(8,128)(2,1)S(1)} %get-tuple-element.10), channel_id=1, source_target_pairs={{0,8},{4,12},{8,0},{12,4},{16,24},{20,28},{24,16},{28,20},{1,9},{5... | collective-permute-start | bytes 208904 | tf_op jit(solution)/shard_map/ppermute | solution.py:342
  35.0 4.4 %copy-start = (bf16[128,256]{1,0:T(8,128)(2,1)S(1)}, bf16[128,256]{1,0:T(8,128)(2,1)}, u32[]{:S(2)}) copy-start(bf16[128,256]{1,0:T(8,128)(2,1)} %constant.13.clone.refs_4_.refs_2_) | copy-start | bytes 196612
  35.0 4.4 %copy-start.1 = (f32[32,128]{1,0:T(8,128)S(1)}, f32[32,128]{1,0:T(8,128)}, u32[]{:S(2)}) copy-start(f32[32,128]{1,0:T(8,128)} %constant.14.clone.refs_5_.refs_3_) | copy-start | bytes 49156
  37.7 4.4 %collective-permute-start.14 = (bf16[272,128]{1,0:T(8,128)(2,1)S(1)}, bf16[272,128]{1,0:T(8,128)(2,1)S(1)}, u32[]{:S(2)}, u32[]{:S(2)}) collective-permute-start(bf16[272,128]{1,0:T(8,128)(2,1)S(1)} %shard_map.118), channel_id=1, source_target_pairs={{0,2},{1,3},{2,0},{3,1},{4,6},{5,7},{6,4},{7,5},{8,10},{9,11},{10,... | collective-permute-start | bytes 208904 | tf_op jit(solution)/shard_map/ppermute | solution.py:342
  39.4 2.7 %collective-permute-start.13 = (bf16[272,128]{1,0:T(8,128)(2,1)S(1)}, bf16[272,128]{1,0:T(8,128)(2,1)S(1)}, u32[]{:S(2)}, u32[]{:S(2)}) collective-permute-start(bf16[272,128]{1,0:T(8,128)(2,1)S(1)} %shard_map.118), channel_id=1, source_target_pairs={{0,1},{1,0},{2,3},{3,2},{4,5},{5,4},{6,7},{7,6},{8,9},{9,8},{10,11... | collective-permute-start | bytes 208904 | tf_op jit(solution)/shard_map/ppermute | solution.py:342
  42.1 1.3 %collective-permute-start.15 = (bf16[272,128]{1,0:T(8,128)(2,1)S(1)}, bf16[272,128]{1,0:T(8,128)(2,1)S(1)}, u32[]{:S(2)}, u32[]{:S(2)}) collective-permute-start(bf16[272,128]{1,0:T(8,128)(2,1)S(1)} %collective-permute-done.14.refs_1_), channel_id=1, source_target_pairs={{0,1},{1,0},{2,3},{3,2},{4,5},{5,4},{6,7},{7,6},{8,9},{9,8},{10,11... | collective-permute-start | bytes 208904 | tf_op jit(solution)/shard_map/ppermute | solution.py:342

commit v7 on v6

--- a/solution.py
+++ b/solution.py
@@ -233,7 +233,7 @@
     def emit(u, part, value):
         out[:, part, u * PIX : (u + 1) * PIX] = value[:own]
         at = part * BAND * BAND + u * PIX
-        rounded[:, at : at + PIX] = value.astype(jnp.bfloat16)
+        rounded[:, at : at + PIX] = value
 
     spread_out(added(pieces), 3, expand, taper, wide, rows, own, emit)
 
@@ -243,7 +243,7 @@
 
     def emit(u, part, value):
         at = part * BAND * BAND + u * PIX
-        rounded[:, at : at + PIX] = value.astype(jnp.bfloat16)
+        rounded[:, at : at + PIX] = value
 
     spread_out(piece[...].astype(jnp.float32), 1, expand, taper, wide, rows, own, emit)
 
@@ -309,7 +309,7 @@
     each = fresh[0].shape[0]
     spans = len(fresh) * each
     classes = own * groups
-    held = jnp.concatenate([piece[:own] for piece in pieces], axis=0)
+    held = jnp.concatenate([piece[:own] for piece in pieces], axis=0).astype(jnp.bfloat16)
     both = jnp.concatenate([held[:, : spans * PIX], held[:, spans * PIX :]], axis=0)
     total = None
     for f in range(0, spans, 2):
@@ -457,7 +457,7 @@
         functools.partial(averages_kernel, own=own, parts=fars),
         out_shape=(
             jax.ShapeDtypeStruct((own, 2, flat), jnp.float32),
-            jax.ShapeDtypeStruct((TILE, 2 * flat), jnp.bfloat16),
+            jax.ShapeDtypeStruct((TILE, 2 * flat), jnp.float32),
         ),
         in_specs=[vmem] * (fars + 2),
         out_specs=(vmem, vmem),
@@ -468,7 +468,7 @@
     def references(after, piece):
         return pl.pallas_call(
             functools.partial(references_kernel, own=own),
-            out_shape=jax.ShapeDtypeStruct((TILE, 2 * flat), jnp.bfloat16),
+            out_shape=jax.ShapeDtypeStruct((TILE, 2 * flat), jnp.float32),
             in_specs=[anywhere] + [vmem] * 3,
             out_specs=vmem,
             scratch_shapes=spread_scratch,

time: 45.9 us -> 45.9 us (level)
  no operation moved by 1% of the time
where the time goes in v7:
time: 45.9 us; the launch traced here: 45.7 us
  Pallas kernels  23.9 us (52%)
  starting transfers between devices  16.7 us (36%)
  waiting for transfers between devices  3.93 us (9%)
  between operations  0.86 us (2%)
    ppermute x6, starting transfers between devices, hop(): lax.ppermute(array, ('dp', 'grp'), [(i, i ^ ((near & 1) * groups | (near...  8.59 us
    pallas_call x8, Pallas kernels, transform(): pl.pallas_call(functools.partial(transform_kernel, jobs=jobs, other=other...  8.1 us
    ppermute x10, starting transfers between devices, swap(): return lax.ppermute(array, axis, [(i, i ^ flip) for i in range(size)])  8.06 us
    pallas_call x1, Pallas kernels, body(): pl.pallas_call(sums_kernel, out_shape=pltpu.VMEM((CLASSES * SLAB, PIX), j...  7.26 us
    pallas_call x2, Pallas kernels, regroup(): pl.pallas_call(functools.partial(regroup_kernel, first=first), out_shape=...  3.99 us
    ppermute x10, waiting for transfers between devices, swap(): return lax.ppermute(array, axis, [(i, i ^ flip) for i in range(size)])  3.24 us
    pallas_call x1, Pallas kernels, body(): pl.pallas_call(functools.partial(scores_kernel, own=own, groups=groups),...  2.01 us
    pallas_call x1, Pallas kernels, body(): pl.pallas_call(functools.partial(averages_kernel, own=own, parts=fars), o...  1.32 us
  transfers between devices with their start and end apart: 16, of which 6 were waited for; matrix products, arithmetic and copies ran while one was open for 1% of the time, Pallas kernels for 29%

profile of v7, /device:TPU:0, one launch (start us, length us, event | category | flops | bytes accessed | tf_op | source)
XLA Modules:
  0.0 45.7 jit_solution(6420874653701723759)
XLA Ops:
  0.7 7.3 %shard_map.104.acc = f32[40960,128]{1,0:T(8,128)S(1)} custom-call(s32[512]{0:T(512)} %class_ids.1, s32[2,512]{1,0:T(2,128)} %bitcast.15, bf16[512,128,128]{2,1,0:T(8,128)(2,1)} %images.1), custom_call_target="tpu_custom_call" | custom-call | tf_op jit(solution)/shard_map/pallas_call | solution.py:371
  8.0 1.0 %shard_map.105._ = bf16[4,272,128]{2,1,0:T(8,128)(2,1)S(1)} custom-call(s32[4,128]{1,0:T(4,128)S(1)} %bitcast.6, f32[40960,128]{1,0:T(8,128)S(1)} %shard_map.104.acc, s32[4,128]{1,0:T(4,128)S(1)} %bitcast.7, bf16[256,128]{1,0:T(8,128)(2,1)S(1)} %copy-done.3, bf16[80,128]{1,0:T(8,128)(2,1)S(1)} %copy-done.5, bf16[16,1024]{1,0:T(8,128)(2,1)S(1)} %copy-done.4), custom_call_target="tpu_custom_call" | custom-call | flops 10000000000 | bytes 1048576 | tf_op jit(solution)/shard_map/pallas_call | solution.py:394
  9.5 1.0 %shard_map.106 = bf16[4,272,128]{2,1,0:T(8,128)(2,1)S(1)} custom-call(bf16[4,272,128]{2,1,0:T(8,128)(2,1)S(1)} %shard_map.105._, f32[40960,128]{1,0:T(8,128)S(1)} %shard_map.104.acc, s32[4,128]{1,0:T(4,128)S(1)} %bitcast.8, bf16[256,128]{1,0:T(8,128)(2,1)S(1)} %copy-done.3, bf16[80,128]{1,0:T(8,128)(2,1)S(1)} %copy-done.5, bf16[16,1024]{1,0:T(8,128)(2,1)S(1)} %copy-done.4), custom_call_target="tpu_custom_call" | custom-call | flops 10000000000 | bytes 1048576 | tf_op jit(solution)/shard_map/pallas_call | solution.py:394
  10.8 3.0 %collective-permute-start.5 = (bf16[2,272,128]{2,1,0:T(8,128)(2,1)S(1)}, bf16[2,272,128]{2,1,0:T(8,128)(2,1)S(1)}, u32[]{:S(2)}, u32[]{:S(2)}) collective-permute-start(bf16[2,272,128]{2,1,0:T(8,128)(2,1)S(1)} %get-tuple-element.21._), channel_id=1, source_target_pairs={{0,2},{1,3},{2,0},{3,1},{4,6},{5,7},{6,4},{7,5},{8,10},{9,11},{10,... | collective-permute-start | bytes 417800 | tf_op jit(solution)/shard_map/ppermute | solution.py:347
  13.8 1.0 %shard_map.107._ = bf16[4,272,128]{2,1,0:T(8,128)(2,1)S(1)} custom-call(bf16[2,272,128]{2,1,0:T(8,128)(2,1)S(1)} %get-tuple-element.21._, f32[40960,128]{1,0:T(8,128)S(1)} %shard_map.104.acc, s32[4,128]{1,0:T(4,128)S(1)} %bitcast.9, bf16[256,128]{1,0:T(8,128)(2,1)S(1)} %copy-done.3, bf16[80,128]{1,0:T(8,128)(2,1)S(1)} %copy-done.5, ...), custom_call_target="tpu_custom_call" | custom-call | flops 10000000000 | bytes 1048576 | tf_op jit(solution)/shard_map/pallas_call | solution.py:394
  14.8 1.0 %shard_map.108 = bf16[4,272,128]{2,1,0:T(8,128)(2,1)S(1)} custom-call(bf16[4,272,128]{2,1,0:T(8,128)(2,1)S(1)} %shard_map.107._, f32[40960,128]{1,0:T(8,128)S(1)} %shard_map.104.acc, s32[4,128]{1,0:T(4,128)S(1)} %bitcast.10, bf16[256,128]{1,0:T(8,128)(2,1)S(1)} %copy-done.3, bf16[80,128]{1,0:T(8,128)(2,1)S(1)} %copy-done.5, bf16[16,1024]{1,0:T(8,128)(2,1)S(1)} %copy-done.4), custom_call_target="tpu_custom_call" | custom-call | flops 10000000000 | bytes 1048576 | tf_op jit(solution)/shard_map/pallas_call | solution.py:394
  15.9 1.5 %collective-permute-start.4 = (bf16[2,272,128]{2,1,0:T(8,128)(2,1)S(1)}, bf16[2,272,128]{2,1,0:T(8,128)(2,1)S(1)}, u32[]{:S(2)}, u32[]{:S(2)}) collective-permute-start(bf16[2,272,128]{2,1,0:T(8,128)(2,1)S(1)} %get-tuple-element.20), channel_id=1, source_target_pairs={{0,6},{1,7},{2,4},{3,5},{4,2},{5,3},{6,0},{7,1},{8,14},{9,15},{10,... | collective-permute-start | bytes 417800 | tf_op jit(solution)/shard_map/ppermute | solution.py:347
  17.4 1.0 %shard_map.109._ = bf16[4,272,128]{2,1,0:T(8,128)(2,1)S(1)} custom-call(bf16[2,272,128]{2,1,0:T(8,128)(2,1)S(1)} %get-tuple-element.19._.refs_3_, f32[40960,128]{1,0:T(8,128)S(1)} %shard_map.104.acc, s32[4,128]{1,0:T(4,128)S(1)} %bitcast.11, bf16[256,128]{1,0:T(8,128)(2,1)S(1)} %copy-done.3, bf16[80,128]{1,0:T(8,128)(2,1)S(1)} %copy-done.5, ...), custom_call_target="tpu_custom_call" | custom-call | flops 10000000000 | bytes 1048576 | tf_op jit(solution)/shard_map/pallas_call | solution.py:394
  18.7 1.0 %shard_map.110 = bf16[4,272,128]{2,1,0:T(8,128)(2,1)S(1)} custom-call(bf16[4,272,128]{2,1,0:T(8,128)(2,1)S(1)} %shard_map.109._, f32[40960,128]{1,0:T(8,128)S(1)} %shard_map.104.acc, s32[4,128]{1,0:T(4,128)S(1)} %bitcast.12, bf16[256,128]{1,0:T(8,128)(2,1)S(1)} %copy-done.3, bf16[80,128]{1,0:T(8,128)(2,1)S(1)} %copy-done.5, bf16[16,1024]{1,0:T(8,128)(2,1)S(1)} %copy-done.4), custom_call_target="tpu_custom_call" | custom-call | flops 10000000000 | bytes 1048576 | tf_op jit(solution)/shard_map/pallas_call | solution.py:394
  20.4 1.7 %collective-permute-start.8 = (bf16[2,272,128]{2,1,0:T(8,128)(2,1)S(1)}, bf16[2,272,128]{2,1,0:T(8,128)(2,1)S(1)}, u32[]{:S(2)}, u32[]{:S(2)}) collective-permute-start(bf16[2,272,128]{2,1,0:T(8,128)(2,1)S(1)} %get-tuple-element.17._), channel_id=1, source_target_pairs={{0,2},{1,3},{2,0},{3,1},{4,6},{5,7},{6,4},{7,5},{8,10},{9,11},{10,... | collective-permute-start | bytes 417800 | tf_op jit(solution)/shard_map/ppermute | solution.py:347
  22.0 1.0 %shard_map.111._ = bf16[4,272,128]{2,1,0:T(8,128)(2,1)S(1)} custom-call(bf16[2,272,128]{2,1,0:T(8,128)(2,1)S(1)} %get-tuple-element.17._, f32[40960,128]{1,0:T(8,128)S(1)} %shard_map.104.acc, s32[4,128]{1,0:T(4,128)S(1)} %bitcast.13, bf16[256,128]{1,0:T(8,128)(2,1)S(1)} %copy-done.3, bf16[80,128]{1,0:T(8,128)(2,1)S(1)} %copy-done.5, ...), custom_call_target="tpu_custom_call" | custom-call | flops 10000000000 | bytes 1048576 | tf_op jit(solution)/shard_map/pallas_call | solution.py:394
  23.1 1.0 %shard_map.112 = bf16[4,272,128]{2,1,0:T(8,128)(2,1)S(1)} custom-call(bf16[4,272,128]{2,1,0:T(8,128)(2,1)S(1)} %shard_map.111._, f32[40960,128]{1,0:T(8,128)S(1)} %shard_map.104.acc, s32[4,128]{1,0:T(4,128)S(1)} %bitcast.14, bf16[256,128]{1,0:T(8,128)(2,1)S(1)} %copy-done.3, bf16[80,128]{1,0:T(8,128)(2,1)S(1)} %copy-done.5, bf16[16,1024]{1,0:T(8,128)(2,1)S(1)} %copy-done.4), custom_call_target="tpu_custom_call" | custom-call | flops 10000000000 | bytes 1048576 | tf_op jit(solution)/shard_map/pallas_call | solution.py:394
  24.6 1.4 %collective-permute-start.7 = (bf16[2,272,128]{2,1,0:T(8,128)(2,1)S(1)}, bf16[2,272,128]{2,1,0:T(8,128)(2,1)S(1)}, u32[]{:S(2)}, u32[]{:S(2)}) collective-permute-start(bf16[2,272,128]{2,1,0:T(8,128)(2,1)S(1)} %get-tuple-element.16), channel_id=1, source_target_pairs={{0,6},{1,7},{2,4},{3,5},{4,2},{5,3},{6,0},{7,1},{8,14},{9,15},{10,... | collective-permute-start | bytes 417800 | tf_op jit(solution)/shard_map/ppermute | solution.py:347
  26.8 3.7 %collective-permute-start.12 = (bf16[272,128]{1,0:T(8,128)(2,1)S(1)}, bf16[272,128]{1,0:T(8,128)(2,1)S(1)}, u32[]{:S(2)}, u32[]{:S(2)}) collective-permute-start(bf16[272,128]{1,0:T(8,128)(2,1)S(1)} %get-tuple-element.11), channel_id=1, source_target_pairs={{0,24},{4,28},{8,16},{12,20},{16,8},{20,12},{24,0},{28,4},{1,25},{... | collective-permute-start | bytes 208904 | tf_op jit(solution)/shard_map/ppermute | solution.py:342
  30.5 2.0 %shard_map.114._ = bf16[16,256,2,128]{3,2,1,0:T(2,128)(2,1)S(1)} custom-call(bf16[272,128]{1,0:T(8,128)(2,1)S(1)} %get-tuple-element.8._, bf16[256,2,4096]{2,1,0:T(2,128)(2,1)} %block.3), custom_call_target="tpu_custom_call" | custom-call | flops 100000000 | bytes 1048576 | tf_op jit(solution)/shard_map/pallas_call | solution.py:419
  32.5 0.7 %collective-permute-done.9.refs_2_ = bf16[2,272,128]{2,1,0:T(8,128)(2,1)S(1)} collective-permute-done((bf16[2,272,128]{2,1,0:T(8,128)(2,1)S(1)}, bf16[2,272,128]{2,1,0:T(8,128)(2,1)S(1)}, u32[]{:S(2)}, u32[]{:S(2)}) %collective-permute-start.9) | collective-permute-done | bytes 139296 | tf_op jit(solution)/shard_map/ppermute | solution.py:347
  33.3 1.7 %collective-permute-start.10 = (bf16[272,128]{1,0:T(8,128)(2,1)S(1)}, bf16[272,128]{1,0:T(8,128)(2,1)S(1)}, u32[]{:S(2)}, u32[]{:S(2)}) collective-permute-start(bf16[272,128]{1,0:T(8,128)(2,1)S(1)} %get-tuple-element.10), channel_id=1, source_target_pairs={{0,8},{4,12},{8,0},{12,4},{16,24},{20,28},{24,16},{28,20},{1,9},{5... | collective-permute-start | bytes 208904 | tf_op jit(solution)/shard_map/ppermute | solution.py:342
  35.0 2.0 %shard_map.117._ = bf16[16,256,2,128]{3,2,1,0:T(2,128)(2,1)S(1)} custom-call(bf16[272,128]{1,0:T(8,128)(2,1)S(1)} %get-tuple-element.9.refs_0_._, bf16[256,2,4096]{2,1,0:T(2,128)(2,1)} %block.3), custom_call_target="tpu_custom_call" | custom-call | flops 100000000 | bytes 1048576 | tf_op jit(solution)/shard_map/pallas_call | solution.py:419
  37.1 0.6 %collective-permute-done.10.refs_1_ = bf16[272,128]{1,0:T(8,128)(2,1)S(1)} collective-permute-done((bf16[272,128]{1,0:T(8,128)(2,1)S(1)}, bf16[272,128]{1,0:T(8,128)(2,1)S(1)}, u32[]{:S(2)}, u32[]{:S(2)}) %collective-permute-start.10) | collective-permute-done | bytes 69664 | tf_op jit(solution)/shard_map/ppermute | solution.py:342
  37.7 1.7 %collective-permute-start.14 = (bf16[272,128]{1,0:T(8,128)(2,1)S(1)}, bf16[272,128]{1,0:T(8,128)(2,1)S(1)}, u32[]{:S(2)}, u32[]{:S(2)}) collective-permute-start(bf16[272,128]{1,0:T(8,128)(2,1)S(1)} %shard_map.118), channel_id=1, source_target_pairs={{0,2},{1,3},{2,0},{3,1},{4,6},{5,7},{6,4},{7,5},{8,10},{9,11},{10,... | collective-permute-start | bytes 208904 | tf_op jit(solution)/shard_map/ppermute | solution.py:342
  39.4 1.3 %shard_map.116 = (f32[8,2,4096]{2,1,0:T(2,128)}, f32[8,8192]{1,0:T(8,128)S(1)}) custom-call(bf16[272,128]{1,0:T(8,128)(2,1)S(1)} %get-tuple-element.9.refs_0_._, bf16[272,128]{1,0:T(8,128)(2,1)S(1)} %collective-permute-done.10.refs_1_, bf16[272,128]{1,0:T(8,128)(2,1)S(1)} %collective-permute-done.11.refs_2_, ...), custom_call_target="tpu_custom_call" | custom-call | tf_op jit(solution)/shard_map/pallas_call | solution.py:456
  40.7 1.4 %collective-permute-done.14.refs_1_ = bf16[272,128]{1,0:T(8,128)(2,1)S(1)} collective-permute-done((bf16[272,128]{1,0:T(8,128)(2,1)S(1)}, bf16[272,128]{1,0:T(8,128)(2,1)S(1)}, u32[]{:S(2)}, u32[]{:S(2)}) %collective-permute-start.14) | collective-permute-done | bytes 69664 | tf_op jit(solution)/shard_map/ppermute | solution.py:342
  42.8 0.5 %collective-permute-done.15.refs_1_ = bf16[272,128]{1,0:T(8,128)(2,1)S(1)} collective-permute-done((bf16[272,128]{1,0:T(8,128)(2,1)S(1)}, bf16[272,128]{1,0:T(8,128)(2,1)S(1)}, u32[]{:S(2)}, u32[]{:S(2)}) %collective-permute-start.15) | collective-permute-done | bytes 69664 | tf_op jit(solution)/shard_map/ppermute | solution.py:342
  43.7 2.0 %shard_map.122 = f32[32,256]{1,0:T(8,128)} custom-call(f32[8,8192]{1,0:T(8,128)S(1)} %get-tuple-element.13.refs_0_, f32[8,8192]{1,0:T(8,128)S(1)} %shard_map.119.refs_0_.refs_1_, f32[8,8192]{1,0:T(8,128)S(1)} %shard_map.120.refs_0_.refs_2_, f32[8,8192]{1,0:T(8,128)S(1)} %shard_map.121.refs_3_, bf16[16,512,128]{2,1,0:T(8,128)(2,1)S(1)} %bitcast.4, ...), custom_call_target="tpu_custom_call" | custom-call | tf_op jit(solution)/shard_map/pallas_call | solution.py:485
  (43 shorter events, 4.3 us)
Async XLA Ops:
  0.6 7.3 %copy-start.2 = (s32[512]{0:T(512)S(1)}, s32[512]{0:T(512)}, u32[]{:S(2)}) copy-start(s32[512]{0:T(512)} %class_ids.1) | copy-start | bytes 6148
  0.6 7.3 %copy-start.3 = (bf16[256,128]{1,0:T(8,128)(2,1)S(1)}, bf16[256,128]{1,0:T(8,128)(2,1)}, u32[]{:S(2)}) copy-start(bf16[256,128]{1,0:T(8,128)(2,1)} %constant.10.clone.col) | copy-start | bytes 196612
  0.7 7.3 %copy-start.4 = (bf16[16,1024]{1,0:T(8,128)(2,1)S(1)}, bf16[16,1024]{1,0:T(8,128)(2,1)}, u32[]{:S(2)}) copy-start(bf16[16,1024]{1,0:T(8,128)(2,1)} %constant.12.clone.last) | copy-start | bytes 98308
  0.7 7.3 %copy-start.5 = (bf16[80,128]{1,0:T(8,128)(2,1)S(1)}, bf16[80,128]{1,0:T(8,128)(2,1)}, u32[]{:S(2)}) copy-start(bf16[80,128]{1,0:T(8,128)(2,1)} %constant.11.clone.row) | copy-start | bytes 61444
  9.0 1.7 %collective-permute-start = (bf16[4,272,128]{2,1,0:T(8,128)(2,1)S(1)}, bf16[4,272,128]{2,1,0:T(8,128)(2,1)S(1)}, u32[]{:S(2)}, u32[]{:S(2)}) collective-permute-start(bf16[4,272,128]{2,1,0:T(8,128)(2,1)S(1)} %shard_map.105._), channel_id=1, source_target_pairs={{0,1},{1,0},{2,3},{3,2},{4,5},{5,4},{6,7},{7,6},{8,9},{9,8},{10,11... | collective-permute-start | bytes 835592 | tf_op jit(solution)/shard_map/ppermute | solution.py:342
  10.8 15.9 %collective-permute-start.5 = (bf16[2,272,128]{2,1,0:T(8,128)(2,1)S(1)}, bf16[2,272,128]{2,1,0:T(8,128)(2,1)S(1)}, u32[]{:S(2)}, u32[]{:S(2)}) collective-permute-start(bf16[2,272,128]{2,1,0:T(8,128)(2,1)S(1)} %get-tuple-element.21._), channel_id=1, source_target_pairs={{0,2},{1,3},{2,0},{3,1},{4,6},{5,7},{6,4},{7,5},{8,10},{9,11},{10,... | collective-permute-start | bytes 417800 | tf_op jit(solution)/shard_map/ppermute | solution.py:347
  14.8 2.6 %collective-permute-start.1 = (bf16[4,272,128]{2,1,0:T(8,128)(2,1)S(1)}, bf16[4,272,128]{2,1,0:T(8,128)(2,1)S(1)}, u32[]{:S(2)}, u32[]{:S(2)}) collective-permute-start(bf16[4,272,128]{2,1,0:T(8,128)(2,1)S(1)} %shard_map.107._), channel_id=1, source_target_pairs={{0,1},{1,0},{2,3},{3,2},{4,5},{5,4},{6,7},{7,6},{8,9},{9,8},{10,11... | collective-permute-start | bytes 835592 | tf_op jit(solution)/shard_map/ppermute | solution.py:342
  15.9 10.3 %collective-permute-start.4 = (bf16[2,272,128]{2,1,0:T(8,128)(2,1)S(1)}, bf16[2,272,128]{2,1,0:T(8,128)(2,1)S(1)}, u32[]{:S(2)}, u32[]{:S(2)}) collective-permute-start(bf16[2,272,128]{2,1,0:T(8,128)(2,1)S(1)} %get-tuple-element.20), channel_id=1, source_target_pairs={{0,6},{1,7},{2,4},{3,5},{4,2},{5,3},{6,0},{7,1},{8,14},{9,15},{10,... | collective-permute-start | bytes 417800 | tf_op jit(solution)/shard_map/ppermute | solution.py:347
  18.5 1.8 %collective-permute-start.2 = (bf16[4,272,128]{2,1,0:T(8,128)(2,1)S(1)}, bf16[4,272,128]{2,1,0:T(8,128)(2,1)S(1)}, u32[]{:S(2)}, u32[]{:S(2)}) collective-permute-start(bf16[4,272,128]{2,1,0:T(8,128)(2,1)S(1)} %shard_map.109._), channel_id=1, source_target_pairs={{0,1},{1,0},{2,3},{3,2},{4,5},{5,4},{6,7},{7,6},{8,9},{9,8},{10,11... | collective-permute-start | bytes 835592 | tf_op jit(solution)/shard_map/ppermute | solution.py:342
  19.7 7.0 %collective-permute-start.6 = (bf16[2,272,128]{2,1,0:T(8,128)(2,1)S(1)}, bf16[2,272,128]{2,1,0:T(8,128)(2,1)S(1)}, u32[]{:S(2)}, u32[]{:S(2)}) collective-permute-start(bf16[2,272,128]{2,1,0:T(8,128)(2,1)S(1)} %get-tuple-element.18), channel_id=1, source_target_pairs={{0,4},{1,5},{2,6},{3,7},{4,0},{5,1},{6,2},{7,3},{8,12},{9,13},{10,... | collective-permute-start | bytes 417800 | tf_op jit(solution)/shard_map/ppermute | solution.py:347
  20.4 12.2 %collective-permute-start.8 = (bf16[2,272,128]{2,1,0:T(8,128)(2,1)S(1)}, bf16[2,272,128]{2,1,0:T(8,128)(2,1)S(1)}, u32[]{:S(2)}, u32[]{:S(2)}) collective-permute-start(bf16[2,272,128]{2,1,0:T(8,128)(2,1)S(1)} %get-tuple-element.17._), channel_id=1, source_target_pairs={{0,2},{1,3},{2,0},{3,1},{4,6},{5,7},{6,4},{7,5},{8,10},{9,11},{10,... | collective-permute-start | bytes 417800 | tf_op jit(solution)/shard_map/ppermute | solution.py:347
  23.0 1.6 %collective-permute-start.3 = (bf16[4,272,128]{2,1,0:T(8,128)(2,1)S(1)}, bf16[4,272,128]{2,1,0:T(8,128)(2,1)S(1)}, u32[]{:S(2)}, u32[]{:S(2)}) collective-permute-start(bf16[4,272,128]{2,1,0:T(8,128)(2,1)S(1)} %shard_map.111._), channel_id=1, source_target_pairs={{0,1},{1,0},{2,3},{3,2},{4,5},{5,4},{6,7},{7,6},{8,9},{9,8},{10,11... | collective-permute-start | bytes 835592 | tf_op jit(solution)/shard_map/ppermute | solution.py:342
  24.6 7.9 %collective-permute-start.7 = (bf16[2,272,128]{2,1,0:T(8,128)(2,1)S(1)}, bf16[2,272,128]{2,1,0:T(8,128)(2,1)S(1)}, u32[]{:S(2)}, u32[]{:S(2)}) collective-permute-start(bf16[2,272,128]{2,1,0:T(8,128)(2,1)S(1)} %get-tuple-element.16), channel_id=1, source_target_pairs={{0,6},{1,7},{2,4},{3,5},{4,2},{5,3},{6,0},{7,1},{8,14},{9,15},{10,... | collective-permute-start | bytes 417800 | tf_op jit(solution)/shard_map/ppermute | solution.py:347
  26.2 7.0 %collective-permute-start.9 = (bf16[2,272,128]{2,1,0:T(8,128)(2,1)S(1)}, bf16[2,272,128]{2,1,0:T(8,128)(2,1)S(1)}, u32[]{:S(2)}, u32[]{:S(2)}) collective-permute-start(bf16[2,272,128]{2,1,0:T(8,128)(2,1)S(1)} %get-tuple-element.14), channel_id=1, source_target_pairs={{0,4},{1,5},{2,6},{3,7},{4,0},{5,1},{6,2},{7,3},{8,12},{9,13},{10,... | collective-permute-start | bytes 417800 | tf_op jit(solution)/shard_map/ppermute | solution.py:347
  26.8 10.3 %collective-permute-start.12 = (bf16[272,128]{1,0:T(8,128)(2,1)S(1)}, bf16[272,128]{1,0:T(8,128)(2,1)S(1)}, u32[]{:S(2)}, u32[]{:S(2)}) collective-permute-start(bf16[272,128]{1,0:T(8,128)(2,1)S(1)} %get-tuple-element.11), channel_id=1, source_target_pairs={{0,24},{4,28},{8,16},{12,20},{16,8},{20,12},{24,0},{28,4},{1,25},{... | collective-permute-start | bytes 208904 | tf_op jit(solution)/shard_map/ppermute | solution.py:342
  30.5 6.5 %collective-permute-start.11 = (bf16[272,128]{1,0:T(8,128)(2,1)S(1)}, bf16[272,128]{1,0:T(8,128)(2,1)S(1)}, u32[]{:S(2)}, u32[]{:S(2)}) collective-permute-start(bf16[272,128]{1,0:T(8,128)(2,1)S(1)} %get-tuple-element.8._), channel_id=1, source_target_pairs={{0,16},{4,20},{8,24},{12,28},{16,0},{20,4},{24,8},{28,12},{1,17},{... | collective-permute-start | bytes 208904 | tf_op jit(solution)/shard_map/ppermute | solution.py:342
  33.3 4.4 %collective-permute-start.10 = (bf16[272,128]{1,0:T(8,128)(2,1)S(1)}, bf16[272,128]{1,0:T(8,128)(2,1)S(1)}, u32[]{:S(2)}, u32[]{:S(2)}) collective-permute-start(bf16[272,128]{1,0:T(8,128)(2,1)S(1)} %get-tuple-element.10), channel_id=1, source_target_pairs={{0,8},{4,12},{8,0},{12,4},{16,24},{20,28},{24,16},{28,20},{1,9},{5... | collective-permute-start | bytes 208904 | tf_op jit(solution)/shard_map/ppermute | solution.py:342
  35.0 4.4 %copy-start = (bf16[128,256]{1,0:T(8,128)(2,1)S(1)}, bf16[128,256]{1,0:T(8,128)(2,1)}, u32[]{:S(2)}) copy-start(bf16[128,256]{1,0:T(8,128)(2,1)} %constant.13.clone.refs_4_.refs_2_) | copy-start | bytes 196612
  35.0 4.4 %copy-start.1 = (f32[32,128]{1,0:T(8,128)S(1)}, f32[32,128]{1,0:T(8,128)}, u32[]{:S(2)}) copy-start(f32[32,128]{1,0:T(8,128)} %constant.14.clone.refs_5_.refs_3_) | copy-start | bytes 49156
  37.7 4.4 %collective-permute-start.14 = (bf16[272,128]{1,0:T(8,128)(2,1)S(1)}, bf16[272,128]{1,0:T(8,128)(2,1)S(1)}, u32[]{:S(2)}, u32[]{:S(2)}) collective-permute-start(bf16[272,128]{1,0:T(8,128)(2,1)S(1)} %shard_map.118), channel_id=1, source_target_pairs={{0,2},{1,3},{2,0},{3,1},{4,6},{5,7},{6,4},{7,5},{8,10},{9,11},{10,... | collective-permute-start | bytes 208904 | tf_op jit(solution)/shard_map/ppermute | solution.py:342
  39.4 2.7 %collective-permute-start.13 = (bf16[272,128]{1,0:T(8,128)(2,1)S(1)}, bf16[272,128]{1,0:T(8,128)(2,1)S(1)}, u32[]{:S(2)}, u32[]{:S(2)}) collective-permute-start(bf16[272,128]{1,0:T(8,128)(2,1)S(1)} %shard_map.118), channel_id=1, source_target_pairs={{0,1},{1,0},{2,3},{3,2},{4,5},{5,4},{6,7},{7,6},{8,9},{9,8},{10,11... | collective-permute-start | bytes 208904 | tf_op jit(solution)/shard_map/ppermute | solution.py:342
  42.1 1.3 %collective-permute-start.15 = (bf16[272,128]{1,0:T(8,128)(2,1)S(1)}, bf16[272,128]{1,0:T(8,128)(2,1)S(1)}, u32[]{:S(2)}, u32[]{:S(2)}) collective-permute-start(bf16[272,128]{1,0:T(8,128)(2,1)S(1)} %collective-permute-done.14.refs_1_), channel_id=1, source_target_pairs={{0,1},{1,0},{2,3},{3,2},{4,5},{5,4},{6,7},{7,6},{8,9},{9,8},{10,11... | collective-permute-start | bytes 208904 | tf_op jit(solution)/shard_map/ppermute | solution.py:342
